TPU v7x, 512 devices: a whole 4x4x16 slice. The times are simulated.
512 devices in a mesh: dp: 8 (over z_lo), tensor: 64 (over x, y, z_hi, core).
Axes of the slice: x: 4, y: 4, z: 16 (z_hi: 2, z_lo: 8; z = z_hi * 8 + z_lo), core: 2. Of those that a mesh axis runs over, the one named last changes fastest.
Arguments:
- attn: bfloat16 [4096, 16384], P('dp', 'tensor'), may hold values from -0.25 to 0.25
- grad_out: bfloat16 [4096, 7168], P(('dp', 'tensor')), may hold values from -24 to 24
- weight: bfloat16 [16384, 7168], P('tensor'), may hold values from -0.0625 to 0.0625
Outputs:
- grad_in: bfloat16 [4096, 16384], P('dp', 'tensor')
- grad_weight: bfloat16 [16384, 7168], P('tensor', 'dp')
All inputs are finite; a program needn't handle non-finite values.
Results may differ from a plain program's by a relative error of at most 0.017.
Values may be sent and summed in bfloat16 or wider, within the bound.
No kernel may reach another device: no remote copies, remote signals or barrier semaphores. Data moves between devices by JAX's collectives and lax.ppermute only.
A program may use at most 64 MiB of HBM per device.

v0:
```python
import jax
import jax.numpy as jnp
from jax import lax
from jax.sharding import PartitionSpec as P


def contract_tokens(left, right):
    return lax.dot_general(
        left, right, (((0,), (0,)), ((), ())), preferred_element_type=jnp.float32
    )


def contract_width(left, right):
    return lax.dot_general(
        left, right, (((1,), (1,)), ((), ())), preferred_element_type=jnp.float32
    )


def body(attn, grad_out, weight):
    group_grad = lax.all_gather(grad_out, "tensor", axis=0, tiled=True)
    input_part = contract_width(group_grad, weight)
    weight_part = contract_tokens(attn, group_grad)
    grad_in = input_part.astype(jnp.bfloat16)
    summed = lax.psum_scatter(
        weight_part.astype(jnp.bfloat16), "dp", scatter_dimension=1, tiled=True
    )
    return (grad_in, summed)


def solution(mesh):
    in_specs = (P("dp", "tensor"), P(("dp", "tensor"), None), P("tensor", None))
    out_specs = (P("dp", "tensor"), P("tensor", "dp"))
    return jax.shard_map(body, mesh=mesh, in_specs=in_specs, out_specs=out_specs, check_vma=False)
```

profile of v0, /device:TPU:1, one launch (start us, length us, event | category | flops | bytes accessed | tf_op | source)
XLA Modules:
  0.0 286.7 jit_solution(15867836602572382791)
XLA Ops:
  7.2 0.0 copy-start
  7.2 0.0 all-gather.2.cloned.1.call-start
  7.2 0.7 all-gather.2.cloned.1.call-update
  7.9 0.0 reduce-scatter.4.cloned.1.call-start
  8.0 169.8 %all-gather.2.cloned.1.call-done = bf16[512,7168]{1,0:T(8,128)(2,1)} async-done(((bf16[8,7168]{1,0:T(8,128)(2,1)}), bf16[512,7168]{1,0:T(8,128)(2,1)}) %all-gather.2.cloned.1.call-update) | async-done | bytes 7340048 | tf_op jit(solution)/shard_map/all_gather | solution.py:20
  177.8 0.0 copy-done
  177.8 7.1 %convolution_convert_fusion = bf16[256,7168]{1,0:T(8,128)(2,1)} fusion(bf16[512,256]{1,0:T(8,128)(2,1)S(1)} %copy-done, bf16[512,7168]{1,0:T(8,128)(2,1)} %all-gather.2.cloned.1.call-done), kind=kOutput, calls=%fused_computation | convolution fusion | flops 1880883200 | bytes 11272192 | tf_op jit(solution)/shard_map/dot_general | solution.py:8
  184.9 5.9 %copy.5 = bf16[256,7168]{0,1:T(8,128)(2,1)} copy(bf16[256,7168]{1,0:T(8,128)(2,1)} %convolution_convert_fusion) | data formatting | bytes 7340032
  190.8 0.0 reduce-scatter.4.cloned.1.call-update
  190.8 6.9 %convolution_convert_fusion.1 = bf16[512,256]{1,0:T(8,128)(2,1)} fusion(bf16[512,7168]{1,0:T(8,128)(2,1)} %all-gather.2.cloned.1.call-done, bf16[256,7168]{1,0:T(8,128)(2,1)} %param.5), kind=kOutput, calls=%fused_computation.1 | convolution fusion | flops 1879179264 | bytes 11272192 | tf_op jit(solution)/shard_map/dot_general | solution.py:14
  197.8 80.1 %reduce-scatter.4.cloned.1.call-done = bf16[896,256]{1,0:T(8,128)(2,1)} async-done(((bf16[7168,256]{1,0:T(8,128)(2,1)}), bf16[896,256]{1,0:T(8,128)(2,1)}) %reduce-scatter.4.cloned.1.call-update) | async-done | bytes 458768
  277.9 2.0 copy.6
Async XLA Ops:
  7.2 170.6 %copy-start = (bf16[512,256]{1,0:T(8,128)(2,1)S(1)}, bf16[512,256]{1,0:T(8,128)(2,1)}, u32[]{:S(2)}) copy-start(bf16[512,256]{1,0:T(8,128)(2,1)} %param.3) | copy-start | bytes 786436
  7.2 170.6 %all-gather.2.cloned.1.call-start = ((), (), s32[]{:S(2)}) async-start(), calls=%async_computation.1 | async-start | bytes 7454720 | tf_op jit(solution)/shard_map/all_gather | solution.py:20
  7.9 270.0 %reduce-scatter.4.cloned.1.call-start = ((), (), s32[]{:S(2)}) async-start(), calls=%async_computation.2 | async-start | bytes 4128768
Sparse Core Ops, SparseCore 0:
  12.4 165.3 all-gather.1
  190.9 86.8 reduce-scatter.3
where the time goes:
time: 287 us
  waiting for transfers between devices  251 us (87%)
  matrix products  14 us (5%)
  between operations  14 us (5%)
  local copies, waits for them, and re-layouts  7.92 us (3%)
    all_gather x1, waiting for transfers between devices, body(): group_grad = lax.all_gather(grad_out, 'tensor', axis=0, tiled=True)  170 us
    unnamed x3, waiting for transfers between devices  80.8 us
    unnamed x4, local copies, waits for them, and re-layouts  7.92 us
    dot_general x1, matrix products, contract_tokens(): lax.dot_general(left, right, (((0,), (0,)), ((), ())), preferred_element_...  7.09 us
    dot_general x1, matrix products, contract_width(): lax.dot_general(left, right, (((1,), (1,)), ((), ())), preferred_element_...  6.93 us
  transfers between devices with their start and end apart: 2, of which 2 were waited for; matrix products, arithmetic and copies ran while one was open for 2% of the time, Pallas kernels for 0%

commit v1 on v0

v1 whole, which is shorter than its diff:
```python
import jax
import jax.numpy as jnp
from jax import lax
from jax.sharding import Mesh, PartitionSpec as P

NX, NY, NZ, NC = 4, 4, 2, 2
AXES = ("dp", "x", "y", "zh", "core")


def contract_tokens(left, right):
    return lax.dot_general(
        left, right, (((0,), (0,)), ((), ())), preferred_element_type=jnp.float32
    )


def contract_width(left, right):
    return lax.dot_general(
        left, right, (((1,), (1,)), ((), ())), preferred_element_type=jnp.float32
    )


def shift(values, step, first):
    pairs = []
    for x in range(NX):
        for y in range(NY):
            for c in range(NC):
                if (c == 0) == first:
                    to = ((x + step) % NX, y)
                else:
                    to = (x, (y + step) % NY)
                pairs.append(((x * NY + y) * NC + c, (to[0] * NY + to[1]) * NC + c))
    return lax.ppermute(values, ("x", "y", "core"), pairs)


def swap(values, axis):
    return lax.ppermute(values, axis, [(0, 1), (1, 0)])


def stage(values, first):
    plus = shift(values, 1, first)
    minus = shift(values, -1, first)
    far = shift(values, 2, first)
    return [values, plus, far, minus]


def relative(values, axis, at):
    n = values.shape[axis]
    turned = lax.rev(values, (axis,))
    doubled = jnp.concatenate([turned, turned], axis)
    return lax.dynamic_slice_in_dim(doubled, n - 1 - at, n, axis)


def body(attn, grad_out, weight):
    x, y, z, c = (lax.axis_index(a) for a in ("x", "y", "zh", "core"))
    n_dp = lax.axis_size("dp")
    rows = attn.shape[1]
    held = grad_out.shape[0]
    width = grad_out.shape[1]
    columns = width // n_dp

    both = jnp.concatenate([grad_out, swap(grad_out, "zh")], 0)
    sliced = lax.all_to_all(both, "dp", 1, 0, tiled=True)

    by_core = attn.reshape(NX * NY * NZ, NC, held, rows)
    mine = lax.dynamic_index_in_dim(by_core, c, 1, keepdims=False)
    other = lax.dynamic_index_in_dim(by_core, 1 - c, 1, keepdims=False)
    wide = jnp.concatenate([mine, swap(other, "core")], -1)
    wide = wide.reshape(NX, NY, NZ, held, NC * rows)
    wide = jnp.where(z == 0, wide, wide[:, :, ::-1])
    wide = jnp.where(c == 0, wide.swapaxes(0, 1), wide)
    wide = relative(relative(wide, 0, jnp.where(c == 0, y, x)), 1, jnp.where(c == 0, x, y))
    tokens = NX * NY * NZ * held
    gathered = lax.all_gather(wide.reshape(tokens, NC * rows), "dp", axis=0, tiled=True)
    gathered = gathered.reshape(n_dp, NX * NY, NZ * held, NC * rows)
    gathered = gathered.swapaxes(0, 1).reshape(NX, NY * n_dp * NZ * held, NC * rows)

    weight_other = swap(weight, "core")

    line = jnp.concatenate(stage(both, True), 0)
    group = jnp.concatenate(stage(line, False), 0)
    near = contract_width(group, weight).astype(jnp.bfloat16)
    far = contract_width(group, weight_other).astype(jnp.bfloat16)
    far = swap(far, "core")

    def placed(part, core):
        part = part.reshape(NX, NY, NZ, held, rows)
        part = relative(relative(part, 0, jnp.where(core == 0, y, x)), 1, jnp.where(core == 0, x, y))
        part = jnp.where(core == 0, part.swapaxes(0, 1), part)
        return jnp.where(z == 0, part, part[:, :, ::-1])

    near, far = placed(near, c), placed(far, 1 - c)
    low, high = jnp.where(c == 0, near, far), jnp.where(c == 0, far, near)
    grad_in = jnp.stack([low, high], 3).reshape(NX * NY * NZ * NC * held, rows)

    strip = jnp.concatenate(stage(sliced, True), 0)
    total = jnp.zeros((NC * rows, columns), jnp.float32)
    for part, piece in zip(gathered, stage(strip, False)):
        total = total + contract_tokens(part, piece)
    grad_weight = (total[:rows] + swap(total[rows:], "core")).astype(jnp.bfloat16)
    return grad_in, grad_weight


def solution(mesh):
    n_dp = mesh.shape["dp"]
    fine = Mesh(mesh.devices.reshape(n_dp, NX, NY, NZ, NC), AXES)
    tensor = ("x", "y", "zh", "core")
    in_specs = (P("dp", tensor), P(("dp",) + tensor, None), P(tensor, None))
    out_specs = (P("dp", tensor), P(tensor, "dp"))
    return jax.shard_map(body, mesh=fine, in_specs=in_specs, out_specs=out_specs, check_vma=False)
```

time: 287 us -> 156 us (0.54)
  waiting for transfers between devices: 251 us -> 23.1 us
  starting transfers between devices: 0.08 us -> 89.5 us
  local copies, waits for them, and re-layouts: 7.92 us -> 13.2 us
  other arithmetic: 0 us -> 3.36 us
    all_gather x1, waiting for transfers between devices: 170 us -> 11.6 us  [body(): lax.all_gather(wide.reshape(tokens, NC * rows), 'dp', axis=0, tiled=True)]
    unnamed x3 -> x1, waiting for transfers between devices: 80.8 us -> 0.02 us
    ppermute x0 -> x17, starting transfers between devices: none -> 77.1 us  [the longest x12 39.9 us: shift(): return lax.ppermute(values, ('x', 'y', 'core'), pairs)]
    all_to_all x0 -> x1, starting transfers between devices: none -> 12.3 us  [body(): sliced = lax.all_to_all(both, 'dp', 1, 0, tiled=True)]
    ppermute x0 -> x17, waiting for transfers between devices: none -> 7.05 us  [the longest x12 5.75 us: shift(): return lax.ppermute(values, ('x', 'y', 'core'), pairs)]
    all_to_all x0 -> x1, waiting for transfers between devices: none -> 4.46 us  [body(): sliced = lax.all_to_all(both, 'dp', 1, 0, tiled=True)]
    unnamed x4 -> x10, local copies, waits for them, and re-layouts: 7.92 us -> 5.96 us
    dot_general x1 -> x4, matrix products: 7.09 us -> 5.38 us  [contract_tokens(): lax.dot_general(left, right, (((0,), (0,)), ((), ())), preferred_element_...]
  transfers between devices with their start and end apart: 2 -> 19, of which waited for: 2 -> 5; matrix products, arithmetic and copies ran while one was open for 2% -> 18% of each run, Pallas kernels for 0% -> 0%
where the time goes in v1:
time: 156 us; the launch traced here: 155 us
  starting transfers between devices  89.5 us (57%)
  waiting for transfers between devices  23.1 us (15%)
  between operations  14.5 us (9%)
  local copies, waits for them, and re-layouts  13.2 us (8%)
  matrix products  11.8 us (8%)
  other arithmetic  3.36 us (2%)
    ppermute x12, starting transfers between devices, shift(): return lax.ppermute(values, ('x', 'y', 'core'), pairs)  39.9 us
    ppermute x5, starting transfers between devices, swap(): return lax.ppermute(values, axis, [(0, 1), (1, 0)])  37.3 us
    all_to_all x1, starting transfers between devices, body(): sliced = lax.all_to_all(both, 'dp', 1, 0, tiled=True)  12.3 us
    all_gather x1, waiting for transfers between devices, body(): lax.all_gather(wide.reshape(tokens, NC * rows), 'dp', axis=0, tiled=True)  11.6 us
    dot_general x2, matrix products, contract_width(): lax.dot_general(left, right, (((1,), (1,)), ((), ())), preferred_element_...  6.39 us
    unnamed x10, local copies, waits for them, and re-layouts  5.96 us
    ppermute x12, waiting for transfers between devices, shift(): return lax.ppermute(values, ('x', 'y', 'core'), pairs)  5.75 us
    dot_general x4, matrix products, contract_tokens(): lax.dot_general(left, right, (((0,), (0,)), ((), ())), preferred_element_...  5.38 us
  transfers between devices with their start and end apart: 19, of which 5 were waited for; matrix products, arithmetic and copies ran while one was open for 18% of the time, Pallas kernels for 0%

profile of v1, /device:TPU:1, one launch (start us, length us, event | category | flops | bytes accessed | tf_op | source)
XLA Modules:
  0.0 155.4 jit_solution(4331155630969162629)
XLA Ops:
  7.2 16.3 %collective-permute-start = (bf16[8,7168]{1,0:T(8,128)(2,1)}, bf16[8,7168]{1,0:T(8,128)(2,1)S(1)}, u32[]{:S(2)}, u32[]{:S(2)}) collective-permute-start(bf16[8,7168]{1,0:T(8,128)(2,1)} %param.4), channel_id=1, source_target_pairs={{0,2},{2,0},{1,3},{3,1},{4,6},{6,4},{5,7},{7,5},{8,10},{10,8},{9,1... | collective-permute-start | bytes 344072 | tf_op jit(solution)/shard_map/ppermute | solution.py:36
  24.4 2.9 %collective-permute-start.9 = (bf16[32,8,256]{2,1,0:T(8,128)(2,1)S(1)}, bf16[32,8,256]{2,1,0:T(8,128)(2,1)S(1)}, u32[]{:S(2)}, u32[]{:S(2)}) collective-permute-start(bf16[32,8,256]{2,1,0:T(8,128)(2,1)S(1)} %get-tuple-element.7), channel_id=1, source_target_pairs={{0,1},{1,0},{2,3},{3,2},{4,5},{5,4},{6,7},{7,6},{8,9},{9,8},{10,11... | collective-permute-start | bytes 393224 | tf_op jit(solution)/shard_map/ppermute | solution.py:36
  27.3 1.6 %constant_dynamic-update-slice_fusion.6 = (bf16[64,7168]{1,0:T(8,128)(2,1)}, bf16[16,7168]{1,0:T(8,128)(2,1)S(1)}, bf16[256,7168]{1,0:T(8,128)(2,1)}) fusion(bf16[8,7168]{1,0:T(8,128)(2,1)} %param.4), kind=kLoop, calls=%fused_computation.42 | loop fusion | bytes 458752
  29.6 3.2 %collective-permute-start.1 = (bf16[16,7168]{1,0:T(8,128)(2,1)S(1)}, bf16[16,7168]{1,0:T(8,128)(2,1)S(1)}, u32[]{:S(2)}, u32[]{:S(2)}) collective-permute-start(bf16[16,7168]{1,0:T(8,128)(2,1)S(1)} %get-tuple-element.18), channel_id=1, source_target_pairs={{0,16},{1,5},{4,20},{5,9},{8,24},{9,13},{12,28},{13,1},{16,32},{17... | collective-permute-start | bytes 688136 | tf_op jit(solution)/shard_map/ppermute | solution.py:32
  32.8 4.5 %collective-permute-start.2 = (bf16[16,7168]{1,0:T(8,128)(2,1)S(1)}, bf16[16,7168]{1,0:T(8,128)(2,1)S(1)}, u32[]{:S(2)}, u32[]{:S(2)}) collective-permute-start(bf16[16,7168]{1,0:T(8,128)(2,1)S(1)} %get-tuple-element.18), channel_id=1, source_target_pairs={{0,32},{1,9},{4,36},{5,13},{8,40},{9,1},{12,44},{13,5},{16,48},{17... | collective-permute-start | bytes 688136 | tf_op jit(solution)/shard_map/ppermute | solution.py:32
  37.4 3.0 %collective-permute-start.3 = (bf16[16,7168]{1,0:T(8,128)(2,1)S(1)}, bf16[16,7168]{1,0:T(8,128)(2,1)S(1)}, u32[]{:S(2)}, u32[]{:S(2)}) collective-permute-start(bf16[16,7168]{1,0:T(8,128)(2,1)S(1)} %get-tuple-element.18), channel_id=1, source_target_pairs={{0,48},{1,13},{4,52},{5,1},{8,56},{9,5},{12,60},{13,9},{16,0},{17,... | collective-permute-start | bytes 688136 | tf_op jit(solution)/shard_map/ppermute | solution.py:32
  41.1 12.3 %all-to-all-start = ((bf16[16,8,896]{2,0,1:T(8,128)(2,1)}), bf16[16,8,896]{2,0,1:T(8,128)(2,1)S(1)}, u32[]{:S(2)}, u32[]{:S(2)}) async-start(bf16[16,8,896]{2,0,1:T(8,128)(2,1)} %bitcast.44), calls=%async_computation | async-start | bytes 458752 | tf_op jit(solution)/shard_map/all_to_all | solution.py:62
  56.0 3.1 %collective-permute-start.4 = (bf16[64,7168]{1,0:T(8,128)(2,1)}, bf16[64,7168]{1,0:T(8,128)(2,1)S(1)}, u32[]{:S(2)}, u32[]{:S(2)}) collective-permute-start(bf16[64,7168]{1,0:T(8,128)(2,1)} %get-tuple-element.10), channel_id=1, source_target_pairs={{0,4},{1,17},{4,8},{5,21},{8,12},{9,25},{12,0},{13,29},{16,20},{17... | collective-permute-start | bytes 2752520 | tf_op jit(solution)/shard_map/ppermute | solution.py:32
  60.1 4.5 %all-to-all-done = bf16[16,8,896]{2,0,1:T(8,128)(2,1)S(1)} async-done(((bf16[16,8,896]{2,0,1:T(8,128)(2,1)}), bf16[16,8,896]{2,0,1:T(8,128)(2,1)S(1)}, u32[]{:S(2)}, u32[]{:S(2)}) %all-to-all-start) | async-done | bytes 229408 | tf_op jit(solution)/shard_map/all_to_all | solution.py:62
  64.6 1.9 %collective-permute-start.12 = (bf16[128,896]{1,0:T(8,128)(2,1)S(1)}, bf16[128,896]{1,0:T(8,128)(2,1)S(1)}, u32[]{:S(2)}, u32[]{:S(2)}) collective-permute-start(bf16[128,896]{1,0:T(8,128)(2,1)S(1)} %bitcast.50), channel_id=1, source_target_pairs={{0,48},{1,13},{4,52},{5,1},{8,56},{9,5},{12,60},{13,9},{16,0},{17,... | collective-permute-start | bytes 688136 | tf_op jit(solution)/shard_map/ppermute | solution.py:32
  66.5 4.1 %collective-permute-start.11 = (bf16[128,896]{1,0:T(8,128)(2,1)S(1)}, bf16[128,896]{1,0:T(8,128)(2,1)S(1)}, u32[]{:S(2)}, u32[]{:S(2)}) collective-permute-start(bf16[128,896]{1,0:T(8,128)(2,1)S(1)} %bitcast.51), channel_id=1, source_target_pairs={{0,32},{1,9},{4,36},{5,13},{8,40},{9,1},{12,44},{13,5},{16,48},{17... | collective-permute-start | bytes 688136 | tf_op jit(solution)/shard_map/ppermute | solution.py:32
  70.6 1.9 %collective-permute-start.10 = (bf16[128,896]{1,0:T(8,128)(2,1)S(1)}, bf16[128,896]{1,0:T(8,128)(2,1)S(1)}, u32[]{:S(2)}, u32[]{:S(2)}) collective-permute-start(bf16[128,896]{1,0:T(8,128)(2,1)S(1)} %bitcast.52), channel_id=1, source_target_pairs={{0,16},{1,5},{4,20},{5,9},{8,24},{9,13},{12,28},{13,1},{16,32},{17... | collective-permute-start | bytes 688136 | tf_op jit(solution)/shard_map/ppermute | solution.py:32
  72.6 8.4 %collective-permute-start.7 = (bf16[256,7168]{1,0:T(8,128)(2,1)}, bf16[256,7168]{1,0:T(8,128)(2,1)}, u32[]{:S(2)}, u32[]{:S(2)}) collective-permute-start(bf16[256,7168]{1,0:T(8,128)(2,1)} %param.5), channel_id=1, source_target_pairs={{0,1},{1,0},{2,3},{3,2},{4,5},{5,4},{6,7},{7,6},{8,9},{9,8},{10,11... | collective-permute-start | bytes 11010056 | tf_op jit(solution)/shard_map/ppermute | solution.py:36
  81.0 4.0 %collective-permute-start.5 = (bf16[64,7168]{1,0:T(8,128)(2,1)}, bf16[64,7168]{1,0:T(8,128)(2,1)S(1)}, u32[]{:S(2)}, u32[]{:S(2)}) collective-permute-start(bf16[64,7168]{1,0:T(8,128)(2,1)} %get-tuple-element.10), channel_id=1, source_target_pairs={{0,8},{1,33},{4,12},{5,37},{8,0},{9,41},{12,4},{13,45},{16,24},{17... | collective-permute-start | bytes 2752520 | tf_op jit(solution)/shard_map/ppermute | solution.py:32
  85.0 3.1 %collective-permute-start.6 = (bf16[64,7168]{1,0:T(8,128)(2,1)}, bf16[64,7168]{1,0:T(8,128)(2,1)S(1)}, u32[]{:S(2)}, u32[]{:S(2)}) collective-permute-start(bf16[64,7168]{1,0:T(8,128)(2,1)} %get-tuple-element.10), channel_id=1, source_target_pairs={{0,12},{1,49},{4,0},{5,53},{8,4},{9,57},{12,8},{13,61},{16,28},{17... | collective-permute-start | bytes 2752520 | tf_op jit(solution)/shard_map/ppermute | solution.py:32
  88.1 1.0 pad_maximum_fusion
  89.1 4.2 %collective-permute-start.14 = (bf16[512,896]{1,0:T(8,128)(2,1)}, bf16[512,896]{1,0:T(8,128)(2,1)}, u32[]{:S(2)}, u32[]{:S(2)}) collective-permute-start(bf16[512,896]{1,0:T(8,128)(2,1)} %pad_maximum_fusion), channel_id=1, source_target_pairs={{0,8},{1,33},{4,12},{5,37},{8,0},{9,41},{12,4},{13,45},{16,24},{17... | collective-permute-start | bytes 2752520 | tf_op jit(solution)/shard_map/ppermute | solution.py:32
  93.4 1.9 %collective-permute-start.13 = (bf16[512,896]{1,0:T(8,128)(2,1)}, bf16[512,896]{1,0:T(8,128)(2,1)}, u32[]{:S(2)}, u32[]{:S(2)}) collective-permute-start(bf16[512,896]{1,0:T(8,128)(2,1)} %pad_maximum_fusion), channel_id=1, source_target_pairs={{0,4},{1,17},{4,8},{5,21},{8,12},{9,25},{12,0},{13,29},{16,20},{17... | collective-permute-start | bytes 2752520 | tf_op jit(solution)/shard_map/ppermute | solution.py:32
  96.4 1.2 collective-permute-done.5
  97.6 4.9 %collective-permute-start.15 = (bf16[512,896]{1,0:T(8,128)(2,1)}, bf16[512,896]{1,0:T(8,128)(2,1)S(1)}, u32[]{:S(2)}, u32[]{:S(2)}) collective-permute-start(bf16[512,896]{1,0:T(8,128)(2,1)} %pad_maximum_fusion), channel_id=1, source_target_pairs={{0,12},{1,49},{4,0},{5,53},{8,4},{9,57},{12,8},{13,61},{16,28},{17... | collective-permute-start | bytes 2752520 | tf_op jit(solution)/shard_map/ppermute | solution.py:32
  102.5 1.0 constant_dynamic-update-slice_fusion.8
  103.5 4.5 %collective-permute-done.6 = bf16[64,7168]{1,0:T(8,128)(2,1)S(1)} collective-permute-done((bf16[64,7168]{1,0:T(8,128)(2,1)}, bf16[64,7168]{1,0:T(8,128)(2,1)S(1)}, u32[]{:S(2)}, u32[]{:S(2)}) %collective-permute-start.6) | collective-permute-done | bytes 917536 | tf_op jit(solution)/shard_map/ppermute | solution.py:32
  109.0 3.2 %convolution_convert_fusion.1 = bf16[256,256]{1,0:T(8,128)(2,1)S(1)} fusion(bf16[256,7168]{1,0:T(8,128)(2,1)} %constant_dynamic-update-slice_fusion.7, bf16[256,7168]{1,0:T(8,128)(2,1)S(1)} %copy-done.1), kind=kOutput, calls=%fused_computation.2 | convolution fusion | flops 939589632 | bytes 7471104 | tf_op jit(solution)/shard_map/dot_general | solution.py:17
  112.4 11.6 %all-gather.2.cloned.1.call-done = bf16[2048,512]{1,0:T(8,128)(2,1)} async-done(((bf16[256,512]{1,0:T(8,128)(2,1)}), bf16[2048,512]{1,0:T(8,128)(2,1)}) %all-gather.2.cloned.1.call-update) | async-done | bytes 2097168 | tf_op jit(solution)/shard_map/all_gather | solution.py:73
  124.0 1.7 %fusion.9 = (bf16[4,8,16,512]{3,2,0,1:T(8,128)(2,1)S(1)}, bf16[4,8,16,512]{3,2,0,1:T(8,128)(2,1)S(1)}, bf16[4,8,16,512]{3,2,0,1:T(8,128)(2,1)S(1)}, bf16[4,8,16,512]{3,2,0,1:T(8,128)(2,1)S(1)}) fusion(bf16[16,8,16,512]{3,2,0,1:T(8,128)(2,1)} %bitcast.48), kind=kLoop, calls=%fused_computation.54 | loop fusion | bytes 4194304 | tf_op jit(solution)/shard_map/unstack | solution.py:97
  126.6 1.9 %fusion.11 = f32[512,896]{1,0:T(8,128)S(1)} fusion(bf16[512,512]{1,0:T(8,128)(2,1)S(1)} %bitcast.47, bf16[512,896]{1,0:T(8,128)(2,1)} %collective-permute-done.14), kind=kOutput, calls=%fused_computation.56 | convolution fusion | flops 469762048 | bytes 3276800 | tf_op jit(solution)/shard_map/dot_general | solution.py:11
  128.5 1.9 %fusion.10 = f32[512,896]{1,0:T(8,128)S(1)} fusion(bf16[512,512]{1,0:T(8,128)(2,1)S(1)} %bitcast.46, bf16[512,896]{1,0:T(8,128)(2,1)} %collective-permute-done.13), kind=kOutput, calls=%fused_computation.55 | convolution fusion | flops 469762048 | bytes 3276800 | tf_op jit(solution)/shard_map/dot_general | solution.py:11
  131.3 1.1 slice.13
  132.4 7.8 %collective-permute-start.16 = (f32[256,896]{1,0:T(8,128)}, f32[256,896]{1,0:T(8,128)S(1)}, u32[]{:S(2)}, u32[]{:S(2)}) collective-permute-start(f32[256,896]{1,0:T(8,128)} %slice.13), channel_id=1, source_target_pairs={{0,1},{1,0},{2,3},{3,2},{4,5},{5,4},{6,7},{7,6},{8,9},{9,8},{10,11... | collective-permute-start | bytes 2752520 | tf_op jit(solution)/shard_map/ppermute | solution.py:36
  140.2 3.2 %convolution_convert_fusion = bf16[256,256]{1,0:T(8,128)(2,1)S(1)} fusion(bf16[256,7168]{1,0:T(8,128)(2,1)S(1)} %copy-done, bf16[256,7168]{1,0:T(8,128)(2,1)} %collective-permute-done.7), kind=kOutput, calls=%fused_computation.1 | convolution fusion | flops 939589632 | bytes 7471104 | tf_op jit(solution)/shard_map/dot_general | solution.py:17
  143.4 1.9 %collective-permute-start.8 = (bf16[256,256]{1,0:T(8,128)(2,1)S(1)}, bf16[256,256]{1,0:T(8,128)(2,1)S(1)}, u32[]{:S(2)}, u32[]{:S(2)}) collective-permute-start(bf16[256,256]{1,0:T(8,128)(2,1)S(1)} %convolution_convert_fusion), channel_id=1, source_target_pairs={{0,1},{1,0},{2,3},{3,2},{4,5},{5,4},{6,7},{7,6},{8,9},{9,8},{10,11... | collective-permute-start | bytes 393224 | tf_op jit(solution)/shard_map/ppermute | solution.py:36
  145.3 1.3 collective-permute-done.8
  (54 shorter events, 11.8 us)
Async XLA Ops:
  7.2 21.8 %collective-permute-start = (bf16[8,7168]{1,0:T(8,128)(2,1)}, bf16[8,7168]{1,0:T(8,128)(2,1)S(1)}, u32[]{:S(2)}, u32[]{:S(2)}) collective-permute-start(bf16[8,7168]{1,0:T(8,128)(2,1)} %param.4), channel_id=1, source_target_pairs={{0,2},{2,0},{1,3},{3,1},{4,6},{6,4},{5,7},{7,5},{8,10},{10,8},{9,1... | collective-permute-start | bytes 344072 | tf_op jit(solution)/shard_map/ppermute | solution.py:36
  24.4 29.0 %collective-permute-start.9 = (bf16[32,8,256]{2,1,0:T(8,128)(2,1)S(1)}, bf16[32,8,256]{2,1,0:T(8,128)(2,1)S(1)}, u32[]{:S(2)}, u32[]{:S(2)}) collective-permute-start(bf16[32,8,256]{2,1,0:T(8,128)(2,1)S(1)} %get-tuple-element.7), channel_id=1, source_target_pairs={{0,1},{1,0},{2,3},{3,2},{4,5},{5,4},{6,7},{7,6},{8,9},{9,8},{10,11... | collective-permute-start | bytes 393224 | tf_op jit(solution)/shard_map/ppermute | solution.py:36
  29.6 23.9 %collective-permute-start.1 = (bf16[16,7168]{1,0:T(8,128)(2,1)S(1)}, bf16[16,7168]{1,0:T(8,128)(2,1)S(1)}, u32[]{:S(2)}, u32[]{:S(2)}) collective-permute-start(bf16[16,7168]{1,0:T(8,128)(2,1)S(1)} %get-tuple-element.18), channel_id=1, source_target_pairs={{0,16},{1,5},{4,20},{5,9},{8,24},{9,13},{12,28},{13,1},{16,32},{17... | collective-permute-start | bytes 688136 | tf_op jit(solution)/shard_map/ppermute | solution.py:32
  32.8 21.5 %collective-permute-start.2 = (bf16[16,7168]{1,0:T(8,128)(2,1)S(1)}, bf16[16,7168]{1,0:T(8,128)(2,1)S(1)}, u32[]{:S(2)}, u32[]{:S(2)}) collective-permute-start(bf16[16,7168]{1,0:T(8,128)(2,1)S(1)} %get-tuple-element.18), channel_id=1, source_target_pairs={{0,32},{1,9},{4,36},{5,13},{8,40},{9,1},{12,44},{13,5},{16,48},{17... | collective-permute-start | bytes 688136 | tf_op jit(solution)/shard_map/ppermute | solution.py:32
  37.4 17.8 %collective-permute-start.3 = (bf16[16,7168]{1,0:T(8,128)(2,1)S(1)}, bf16[16,7168]{1,0:T(8,128)(2,1)S(1)}, u32[]{:S(2)}, u32[]{:S(2)}) collective-permute-start(bf16[16,7168]{1,0:T(8,128)(2,1)S(1)} %get-tuple-element.18), channel_id=1, source_target_pairs={{0,48},{1,13},{4,52},{5,1},{8,56},{9,5},{12,60},{13,9},{16,0},{17,... | collective-permute-start | bytes 688136 | tf_op jit(solution)/shard_map/ppermute | solution.py:32
  41.1 23.5 %all-to-all-start = ((bf16[16,8,896]{2,0,1:T(8,128)(2,1)}), bf16[16,8,896]{2,0,1:T(8,128)(2,1)S(1)}, u32[]{:S(2)}, u32[]{:S(2)}) async-start(bf16[16,8,896]{2,0,1:T(8,128)(2,1)} %bitcast.44), calls=%async_computation | async-start | bytes 458752 | tf_op jit(solution)/shard_map/all_to_all | solution.py:62
  53.4 70.6 %all-gather.2.cloned.1.call-start = ((), (), s32[]{:S(2)}) async-start(), calls=%async_computation.1 | async-start | bytes 2359296 | tf_op jit(solution)/shard_map/all_gather | solution.py:73
  56.0 37.4 %collective-permute-start.4 = (bf16[64,7168]{1,0:T(8,128)(2,1)}, bf16[64,7168]{1,0:T(8,128)(2,1)S(1)}, u32[]{:S(2)}, u32[]{:S(2)}) collective-permute-start(bf16[64,7168]{1,0:T(8,128)(2,1)} %get-tuple-element.10), channel_id=1, source_target_pairs={{0,4},{1,17},{4,8},{5,21},{8,12},{9,25},{12,0},{13,29},{16,20},{17... | collective-permute-start | bytes 2752520 | tf_op jit(solution)/shard_map/ppermute | solution.py:32
  64.6 16.5 %collective-permute-start.12 = (bf16[128,896]{1,0:T(8,128)(2,1)S(1)}, bf16[128,896]{1,0:T(8,128)(2,1)S(1)}, u32[]{:S(2)}, u32[]{:S(2)}) collective-permute-start(bf16[128,896]{1,0:T(8,128)(2,1)S(1)} %bitcast.50), channel_id=1, source_target_pairs={{0,48},{1,13},{4,52},{5,1},{8,56},{9,5},{12,60},{13,9},{16,0},{17,... | collective-permute-start | bytes 688136 | tf_op jit(solution)/shard_map/ppermute | solution.py:32
  66.5 18.5 %collective-permute-start.11 = (bf16[128,896]{1,0:T(8,128)(2,1)S(1)}, bf16[128,896]{1,0:T(8,128)(2,1)S(1)}, u32[]{:S(2)}, u32[]{:S(2)}) collective-permute-start(bf16[128,896]{1,0:T(8,128)(2,1)S(1)} %bitcast.51), channel_id=1, source_target_pairs={{0,32},{1,9},{4,36},{5,13},{8,40},{9,1},{12,44},{13,5},{16,48},{17... | collective-permute-start | bytes 688136 | tf_op jit(solution)/shard_map/ppermute | solution.py:32
  70.6 17.5 %collective-permute-start.10 = (bf16[128,896]{1,0:T(8,128)(2,1)S(1)}, bf16[128,896]{1,0:T(8,128)(2,1)S(1)}, u32[]{:S(2)}, u32[]{:S(2)}) collective-permute-start(bf16[128,896]{1,0:T(8,128)(2,1)S(1)} %bitcast.52), channel_id=1, source_target_pairs={{0,16},{1,5},{4,20},{5,9},{8,24},{9,13},{12,28},{13,1},{16,32},{17... | collective-permute-start | bytes 688136 | tf_op jit(solution)/shard_map/ppermute | solution.py:32
  72.6 67.6 %collective-permute-start.7 = (bf16[256,7168]{1,0:T(8,128)(2,1)}, bf16[256,7168]{1,0:T(8,128)(2,1)}, u32[]{:S(2)}, u32[]{:S(2)}) collective-permute-start(bf16[256,7168]{1,0:T(8,128)(2,1)} %param.5), channel_id=1, source_target_pairs={{0,1},{1,0},{2,3},{3,2},{4,5},{5,4},{6,7},{7,6},{8,9},{9,8},{10,11... | collective-permute-start | bytes 11010056 | tf_op jit(solution)/shard_map/ppermute | solution.py:36
  81.0 28.0 %copy-start.1 = (bf16[256,7168]{1,0:T(8,128)(2,1)S(1)}, bf16[256,7168]{1,0:T(8,128)(2,1)}, u32[]{:S(2)}) copy-start(bf16[256,7168]{1,0:T(8,128)(2,1)} %param.5) | copy-start | bytes 11010052
  81.0 16.5 %collective-permute-start.5 = (bf16[64,7168]{1,0:T(8,128)(2,1)}, bf16[64,7168]{1,0:T(8,128)(2,1)S(1)}, u32[]{:S(2)}, u32[]{:S(2)}) collective-permute-start(bf16[64,7168]{1,0:T(8,128)(2,1)} %get-tuple-element.10), channel_id=1, source_target_pairs={{0,8},{1,33},{4,12},{5,37},{8,0},{9,41},{12,4},{13,45},{16,24},{17... | collective-permute-start | bytes 2752520 | tf_op jit(solution)/shard_map/ppermute | solution.py:32
  85.0 23.0 %collective-permute-start.6 = (bf16[64,7168]{1,0:T(8,128)(2,1)}, bf16[64,7168]{1,0:T(8,128)(2,1)S(1)}, u32[]{:S(2)}, u32[]{:S(2)}) collective-permute-start(bf16[64,7168]{1,0:T(8,128)(2,1)} %get-tuple-element.10), channel_id=1, source_target_pairs={{0,12},{1,49},{4,0},{5,53},{8,4},{9,57},{12,8},{13,61},{16,28},{17... | collective-permute-start | bytes 2752520 | tf_op jit(solution)/shard_map/ppermute | solution.py:32
  89.1 37.5 %collective-permute-start.14 = (bf16[512,896]{1,0:T(8,128)(2,1)}, bf16[512,896]{1,0:T(8,128)(2,1)}, u32[]{:S(2)}, u32[]{:S(2)}) collective-permute-start(bf16[512,896]{1,0:T(8,128)(2,1)} %pad_maximum_fusion), channel_id=1, source_target_pairs={{0,8},{1,33},{4,12},{5,37},{8,0},{9,41},{12,4},{13,45},{16,24},{17... | collective-permute-start | bytes 2752520 | tf_op jit(solution)/shard_map/ppermute | solution.py:32
  93.4 35.1 %collective-permute-start.13 = (bf16[512,896]{1,0:T(8,128)(2,1)}, bf16[512,896]{1,0:T(8,128)(2,1)}, u32[]{:S(2)}, u32[]{:S(2)}) collective-permute-start(bf16[512,896]{1,0:T(8,128)(2,1)} %pad_maximum_fusion), channel_id=1, source_target_pairs={{0,4},{1,17},{4,8},{5,21},{8,12},{9,25},{12,0},{13,29},{16,20},{17... | collective-permute-start | bytes 2752520 | tf_op jit(solution)/shard_map/ppermute | solution.py:32
  97.6 32.9 %collective-permute-start.15 = (bf16[512,896]{1,0:T(8,128)(2,1)}, bf16[512,896]{1,0:T(8,128)(2,1)S(1)}, u32[]{:S(2)}, u32[]{:S(2)}) collective-permute-start(bf16[512,896]{1,0:T(8,128)(2,1)} %pad_maximum_fusion), channel_id=1, source_target_pairs={{0,12},{1,49},{4,0},{5,53},{8,4},{9,57},{12,8},{13,61},{16,28},{17... | collective-permute-start | bytes 2752520 | tf_op jit(solution)/shard_map/ppermute | solution.py:32
  130.5 9.7 %copy-start = (bf16[256,7168]{1,0:T(8,128)(2,1)S(1)}, bf16[256,7168]{1,0:T(8,128)(2,1)}, u32[]{:S(2)}) copy-start(bf16[256,7168]{1,0:T(8,128)(2,1)} %constant_dynamic-update-slice_fusion.7) | copy-start | bytes 11010052
  132.4 15.3 %collective-permute-start.16 = (f32[256,896]{1,0:T(8,128)}, f32[256,896]{1,0:T(8,128)S(1)}, u32[]{:S(2)}, u32[]{:S(2)}) collective-permute-start(f32[256,896]{1,0:T(8,128)} %slice.13), channel_id=1, source_target_pairs={{0,1},{1,0},{2,3},{3,2},{4,5},{5,4},{6,7},{7,6},{8,9},{9,8},{10,11... | collective-permute-start | bytes 2752520 | tf_op jit(solution)/shard_map/ppermute | solution.py:36
  143.4 3.2 %collective-permute-start.8 = (bf16[256,256]{1,0:T(8,128)(2,1)S(1)}, bf16[256,256]{1,0:T(8,128)(2,1)S(1)}, u32[]{:S(2)}, u32[]{:S(2)}) collective-permute-start(bf16[256,256]{1,0:T(8,128)(2,1)S(1)} %convolution_convert_fusion), channel_id=1, source_target_pairs={{0,1},{1,0},{2,3},{3,2},{4,5},{5,4},{6,7},{7,6},{8,9},{9,8},{10,11... | collective-permute-start | bytes 393224 | tf_op jit(solution)/shard_map/ppermute | solution.py:36
Sparse Core Ops, SparseCore 0:
  60.2 63.6 all-gather.1

commit v2 on v0

v2 whole, which is shorter than its diff:
```python
import functools

import jax
import jax.numpy as jnp
from jax import lax
from jax.experimental import pallas as pl
from jax.experimental.pallas import tpu as pltpu
from jax.sharding import Mesh, PartitionSpec as P

NX, NY, NZ, NC = 4, 4, 2, 2
AXES = ("dp", "x", "y", "zh", "core")
RING = (0, 2, 4, 6, 7, 5, 3, 1)
BEFORE = tuple(RING[(RING.index(g) - k) % len(RING)] for g in range(len(RING)) for k in range(len(RING)))
TENSOR = ("x", "y", "zh", "core")


def lines(first):
    def at(x, y, z, c):
        return ((x * NY + y) * NZ + z) * NC + c

    groups = []
    for z in range(NZ):
        for c in range(NC):
            for k in range(NX):
                if (c == 0) == first:
                    groups.append([at(i, k, z, c) for i in range(NX)])
                else:
                    groups.append([at(k, i, z, c) for i in range(NY)])
    return groups


def spread(values, first):
    n = values.shape[0]
    copies = jnp.broadcast_to(values[None], (NX,) + values.shape).reshape((NX * n,) + values.shape[1:])
    return lax.all_to_all(copies, TENSOR, 0, 0, axis_index_groups=lines(first), tiled=True)


def turn(values, step):
    pairs = [(RING[i], RING[(i + step) % len(RING)]) for i in range(len(RING))]
    return lax.ppermute(values, "dp", pairs)


def swap(values, axis):
    return lax.ppermute(values, axis, [(0, 1), (1, 0)])


def place_kernel(place, near, far, out):
    zh, c = place[2], place[3]
    for part, core in ((near, c), (far, 1 - c)):
        for at in range(near.shape[0]):
            at2, at1, turned = at // (NX * NZ), (at // NZ) % NX, at % NZ
            px, py = jnp.where(core == 0, at1, at2), jnp.where(core == 0, at2, at1)
            z = zh if turned == 0 else 1 - zh
            out[((px * NY + py) * NZ + z) * NC + core] = part[at]


def small(kernel, shape, place, *values):
    return pl.pallas_call(
        kernel,
        out_shape=jax.ShapeDtypeStruct(shape, values[0].dtype),
        in_specs=[pl.BlockSpec(memory_space=pltpu.SMEM)]
        + [pl.BlockSpec(memory_space=pltpu.VMEM)] * len(values),
        out_specs=pl.BlockSpec(memory_space=pltpu.VMEM),
    )(place, *values)


def width_kernel(moved, mine, theirs, near, far, total):
    at = pl.program_id(0)
    chips, _, parts, _, columns = moved.shape
    left = jnp.concatenate(
        [jnp.concatenate([moved[i, 0, j] for i in range(chips)], 0) for j in range(parts)], 1
    )
    for step in range(2):
        @pl.when(at == step)
        def _(step=step):
            for half, (right, out) in enumerate(((theirs, far), (mine, near))):
                term = lax.dot_general(
                    left, right[:, step * parts * columns:(step + 1) * parts * columns],
                    (((1,), (1,)), ((), ())), preferred_element_type=jnp.float32,
                )
                if step == 0:
                    total[half] = term
                else:
                    out[...] = (total[half] + term).astype(out.dtype)


def contract_width(moved, weight, weight_other):
    chips, _, parts, deep, columns = moved.shape
    rows = weight.shape[0]
    tokens = chips * deep
    shape = jax.ShapeDtypeStruct((tokens, rows), weight.dtype)
    whole = pl.BlockSpec((tokens, rows), lambda i: (0, 0))
    return pl.pallas_call(
        width_kernel,
        grid=(2,),
        out_shape=(shape, shape),
        in_specs=[
            pl.BlockSpec((chips, 1, parts // 2, deep, columns), lambda i: (0, 0, i, 0, 0)),
            pl.BlockSpec(memory_space=pltpu.VMEM), pl.BlockSpec(memory_space=pltpu.VMEM),
        ],
        out_specs=(whole, whole),
        scratch_shapes=[pltpu.VMEM((2, tokens, rows), jnp.float32)],
        compiler_params=pltpu.CompilerParams(vmem_limit_bytes=24 * 1024 * 1024),
        cost_estimate=pl.CostEstimate(
            flops=4 * tokens * rows * parts * columns, bytes_accessed=11 * 1024 * 1024, transcendentals=0
        ),
    )(moved, weight, weight_other)


def tokens_kernel(ring, *refs):
    blocks, parts, near, far, total = refs[:4], refs[4:-3], refs[-3], refs[-2], refs[-1]
    at = pl.program_id(0)
    right = jnp.concatenate([block[i, 0, 0] for block in blocks for i in range(block.shape[0])], 0)
    for step in range(len(parts) // 4):
        @pl.when(at == step)
        def _(step=step):
            left = jnp.concatenate([part[...] for part in parts[4 * step:4 * step + 4]], 1)
            term = jnp.dot(left, right, preferred_element_type=jnp.float32)
            if step == 0:
                total[...] = term
            else:
                rows = near.shape[0]
                near[...] = total[:rows] + term[:rows]
                far[...] = (total[rows:] + term[rows:]).astype(far.dtype)


def contract_tokens(ring, moved, parts):
    chips, _, n_dp, deep, columns = moved.shape
    rows, tokens = parts[0].shape
    half = rows // NC
    whole = pl.BlockSpec((half, columns), lambda k, ring: (0, 0))
    shape = (chips, 1, 1, deep, columns)
    return pl.pallas_call(
        tokens_kernel,
        out_shape=(
            jax.ShapeDtypeStruct((half, columns), jnp.float32), jax.ShapeDtypeStruct((half, columns), jnp.bfloat16)
        ),
        grid_spec=pltpu.PrefetchScalarGridSpec(
            num_scalar_prefetch=1,
            grid=(n_dp // 4,),
            in_specs=[
                pl.BlockSpec(shape, lambda k, ring, j=j: (0, 1, ring[4 * k + j], 0, 0)) for j in range(4)
            ] + [pl.BlockSpec(memory_space=pltpu.VMEM)] * n_dp,
            out_specs=(whole, whole),
            scratch_shapes=[pltpu.VMEM((rows, columns), jnp.float32)],
        ),
        compiler_params=pltpu.CompilerParams(vmem_limit_bytes=24 * 1024 * 1024),
        cost_estimate=pl.CostEstimate(
            flops=2 * rows * tokens * n_dp * columns, bytes_accessed=8 * 1024 * 1024, transcendentals=0
        ),
    )(ring, *[moved] * 4, *parts)


def body(attn, grad_out, weight):
    place = jnp.stack([lax.axis_index(a) for a in TENSOR + ("dp",)]).astype(jnp.int32)
    c = place[3]
    n_dp = lax.axis_size("dp")
    rows = attn.shape[1]
    held, width = grad_out.shape
    columns = width // n_dp
    blocks = NX * NY * NZ
    tokens = blocks * held
    deep = NZ * held

    parts = attn.reshape(NX, NY, NZ, NC, held, rows)
    low, high = parts[:, :, :, 0].swapaxes(0, 1), parts[:, :, :, 1]
    mine = jnp.where(c == 0, low, high).reshape(tokens, rows).T
    other = jnp.where(c == 0, high, low).reshape(tokens, rows).T
    wide = jnp.concatenate([mine, swap(other, "core")], 0)

    strips = jnp.broadcast_to(
        grad_out.reshape(held, n_dp, 1, columns).transpose(1, 2, 0, 3), (n_dp, NZ, held, columns)
    ).reshape(n_dp * deep, columns)
    sliced = lax.all_to_all(strips, ("dp", "zh"), 0, 0, tiled=True)
    both = jnp.concatenate([grad_out, swap(grad_out, "zh")], 0)
    both = both.reshape(deep, n_dp, columns).swapaxes(0, 1).reshape(n_dp * deep, columns)

    both, wide = lax.optimization_barrier((both, wide))
    moved = spread(jnp.concatenate([both, sliced], 0), True)
    weight_other = swap(weight, "core")

    wide, _ = lax.optimization_barrier((wide, sliced))
    ahead, back = [wide, turn(wide, 1)], [wide, turn(wide, -1)]
    moved, ahead[1], back[1] = lax.optimization_barrier((moved, ahead[1], back[1]))
    moved = spread(moved, False).reshape(NX * NY, 2, n_dp, deep, columns)
    for _ in range(n_dp // 2 - 1):
        ahead.append(turn(ahead[-1], 1))
    for _ in range(n_dp // 2 - 2):
        back.append(turn(back[-1], -1))
    ring = lax.dynamic_slice_in_dim(jnp.asarray(BEFORE, jnp.int32), place[4] * n_dp, n_dp)

    total, part = contract_tokens(ring, moved, ahead + back[:0:-1])
    part = swap(part, "core")
    near, far = contract_width(moved, weight, weight_other)
    far = swap(far, "core")
    grad_weight = (total + part.astype(jnp.float32)).astype(jnp.bfloat16)
    grad_in = small(
        place_kernel, (NC * blocks, held, rows), place, near.reshape(blocks, held, rows), far.reshape(blocks, held, rows)
    ).reshape(NC * tokens, rows)
    return grad_in, grad_weight


def solution(mesh):
    n_dp = mesh.shape["dp"]
    fine = Mesh(mesh.devices.reshape(n_dp, NX, NY, NZ, NC), AXES)
    in_specs = (P("dp", TENSOR), P(("dp",) + TENSOR, None), P(TENSOR, None))
    out_specs = (P("dp", TENSOR), P(TENSOR, "dp"))
    return jax.shard_map(body, mesh=fine, in_specs=in_specs, out_specs=out_specs, check_vma=False)
```

time: 287 us -> 141 us (0.49)
  waiting for transfers between devices: 251 us -> 49.9 us
  starting transfers between devices: 0.08 us -> 64.9 us
  matrix products: 14 us -> 0 us
  between operations: 14 us -> 0.88 us
  Pallas kernels: 0 us -> 12.1 us
    all_gather x1 -> x0, waiting for transfers between devices: 170 us -> none  [body(): group_grad = lax.all_gather(grad_out, 'tensor', axis=0, tiled=True)]
    unnamed x3 -> x0, waiting for transfers between devices: 80.8 us -> none
    ppermute x0 -> x12, starting transfers between devices: none -> 50.3 us  [the longest x5 27.7 us: swap(): return lax.ppermute(values, axis, [(0, 1), (1, 0)])]
    ppermute x0 -> x12, waiting for transfers between devices: none -> 33.2 us  [the longest x7 32.5 us: turn(): return lax.ppermute(values, 'dp', pairs)]
    all_to_all x0 -> x3, waiting for transfers between devices: none -> 16.7 us  [the longest x1 13 us: body(): sliced = lax.all_to_all(strips, ('dp', 'zh'), 0, 0, tiled=True)]
    all_to_all x0 -> x3, starting transfers between devices: none -> 14.6 us  [the longest x2 9.77 us: spread(): lax.all_to_all(copies, TENSOR, 0, 0, axis_index_groups=lines(first), tile...]
    dot_general x2 -> x0, matrix products: 14 us -> none  [the longest x1 7.09 us: contract_tokens(): lax.dot_general(left, right, (((0,), (0,)), ((), ())), preferred_element_...]
    pallas_call x0 -> x3, Pallas kernels: none -> 12.1 us  [the longest x1 5.18 us: contract_width(): pl.pallas_call(width_kernel, grid=(2,), out_shape=(shape, shape), in_spec...]
  transfers between devices with their start and end apart: 2 -> 15, of which waited for: 2 -> 10; matrix products, arithmetic and copies ran while one was open for 2% -> 3% of each run, Pallas kernels for 0% -> 9%
where the time goes in v2:
time: 141 us; the launch traced here: 139 us
  starting transfers between devices  64.9 us (46%)
  waiting for transfers between devices  49.9 us (35%)
  Pallas kernels  12.1 us (9%)
  local copies, waits for them, and re-layouts  8.82 us (6%)
  other arithmetic  2.84 us (2%)
    ppermute x7, waiting for transfers between devices, turn(): return lax.ppermute(values, 'dp', pairs)  32.5 us
    ppermute x5, starting transfers between devices, swap(): return lax.ppermute(values, axis, [(0, 1), (1, 0)])  27.7 us
    ppermute x7, starting transfers between devices, turn(): return lax.ppermute(values, 'dp', pairs)  22.6 us
    all_to_all x1, waiting for transfers between devices, body(): sliced = lax.all_to_all(strips, ('dp', 'zh'), 0, 0, tiled=True)  13 us
    all_to_all x2, starting transfers between devices, spread(): lax.all_to_all(copies, TENSOR, 0, 0, axis_index_groups=lines(first), tile...  9.77 us
    pallas_call x1, Pallas kernels, contract_width(): pl.pallas_call(width_kernel, grid=(2,), out_shape=(shape, shape), in_spec...  5.18 us
    pallas_call x1, Pallas kernels, contract_tokens(): pl.pallas_call(tokens_kernel, out_shape=(jax.ShapeDtypeStruct((half, colu...  5.1 us
    broadcast_in_dim x2, local copies, waits for them, and re-layouts, spread(): jnp.broadcast_to(values[None], (NX,) + values.shape)  4.98 us
  transfers between devices with their start and end apart: 15, of which 10 were waited for; matrix products, arithmetic and copies ran while one was open for 3% of the time, Pallas kernels for 9%

profile of v2, /device:TPU:1, one launch (start us, length us, event | category | flops | bytes accessed | tf_op | source)
XLA Modules:
  0.0 139.5 jit_solution(4630200748951397647)
XLA Ops:
  0.6 16.3 %collective-permute-start = (bf16[8,7168]{1,0:T(8,128)(2,1)}, bf16[8,7168]{1,0:T(8,128)(2,1)S(1)}, u32[]{:S(2)}, u32[]{:S(2)}) collective-permute-start(bf16[8,7168]{1,0:T(8,128)(2,1)} %param.5), channel_id=1, source_target_pairs={{0,2},{2,0},{1,3},{3,1},{4,6},{6,4},{5,7},{7,5},{8,10},{10,8},{9,1... | collective-permute-start | bytes 344072 | tf_op jit(solution)/shard_map/ppermute | solution.py:44
  16.9 1.6 %broadcast_in_dim.9 = bf16[8,2,8,896]{3,2,1,0:T(8,128)(2,1)} broadcast(bf16[8,8,896]{2,1,0:T(8,128)(2,1)} %bitcast.50), dimensions={0,2,3} | broadcast | bytes 344064 | tf_op jit(solution)/shard_map/broadcast_in_dim | solution.py:171
  18.5 4.8 %all-to-all-start = ((bf16[16,8,896]{2,1,0:T(8,128)(2,1)}), bf16[16,8,896]{2,1,0:T(8,128)(2,1)S(1)}, u32[]{:S(2)}, u32[]{:S(2)}) async-start(bf16[16,8,896]{2,1,0:T(8,128)(2,1)} %bitcast.19), calls=%async_computation | async-start | bytes 458752 | tf_op jit(solution)/shard_map/all_to_all | solution.py:174
  23.4 1.0 broadcast_select_fusion.1
  24.5 3.1 %collective-permute-start.1 = (bf16[256,256]{1,0:T(8,128)(2,1)S(1)}, bf16[256,256]{1,0:T(8,128)(2,1)S(1)}, u32[]{:S(2)}, u32[]{:S(2)}) collective-permute-start(bf16[256,256]{1,0:T(8,128)(2,1)S(1)} %bitcast.54), channel_id=1, source_target_pairs={{0,1},{1,0},{2,3},{3,2},{4,5},{5,4},{6,7},{7,6},{8,9},{9,8},{10,11... | collective-permute-start | bytes 393224 | tf_op jit(solution)/shard_map/ppermute | solution.py:44
  27.8 0.9 pad_maximum_fusion.2
  28.8 13.0 %all-to-all-done = bf16[16,8,896]{2,1,0:T(8,128)(2,1)S(1)} async-done(((bf16[16,8,896]{2,1,0:T(8,128)(2,1)}), bf16[16,8,896]{2,1,0:T(8,128)(2,1)S(1)}, u32[]{:S(2)}, u32[]{:S(2)}) %all-to-all-start) | async-done | bytes 229408 | tf_op jit(solution)/shard_map/all_to_all | solution.py:174
  41.8 1.4 %broadcast_in_dim.10 = bf16[4,256,896]{2,1,0:T(8,128)(2,1)} broadcast(bf16[256,896]{1,0:T(8,128)(2,1)S(1)} %pad_maximum_fusion), dimensions={1,2} | broadcast | bytes 2293760 | tf_op jit(solution)/shard_map/broadcast_in_dim | solution.py:34
  43.2 4.2 %all-to-all-start.1 = ((bf16[4,256,896]{2,1,0:T(8,128)(2,1)}), bf16[4,256,896]{2,1,0:T(8,128)(2,1)S(1)}, u32[]{:S(2)}, u32[]{:S(2)}) async-start(bf16[4,256,896]{2,1,0:T(8,128)(2,1)} %broadcast_in_dim.10), calls=%async_computation.1 | async-start | bytes 3670016 | tf_op jit(solution)/shard_map/all_to_all | solution.py:35
  47.4 5.1 %collective-permute-start.2 = (bf16[512,256]{1,0:T(8,128)(2,1)S(1)}, bf16[512,256]{1,0:T(8,128)(2,1)S(1)}, u32[]{:S(2)}, u32[]{:S(2)}) collective-permute-start(bf16[512,256]{1,0:T(8,128)(2,1)S(1)} %pad_maximum_fusion.1.refs_4_), channel_id=1, source_target_pairs={{0,128},{128,256},{256,384},{384,448},{448,320},{320,192},{192,64}... | collective-permute-start | bytes 786440 | tf_op jit(solution)/shard_map/ppermute | solution.py:40
  52.5 1.9 %collective-permute-start.3 = (bf16[512,256]{1,0:T(8,128)(2,1)S(1)}, bf16[512,256]{1,0:T(8,128)(2,1)S(1)}, u32[]{:S(2)}, u32[]{:S(2)}) collective-permute-start(bf16[512,256]{1,0:T(8,128)(2,1)S(1)} %pad_maximum_fusion.1.refs_4_), channel_id=1, source_target_pairs={{0,64},{128,0},{256,128},{384,256},{448,384},{320,448},{192,320},{... | collective-permute-start | bytes 786440 | tf_op jit(solution)/shard_map/ppermute | solution.py:40
  54.5 2.7 %collective-permute-done.2.refs_5_ = bf16[512,256]{1,0:T(8,128)(2,1)S(1)} collective-permute-done((bf16[512,256]{1,0:T(8,128)(2,1)S(1)}, bf16[512,256]{1,0:T(8,128)(2,1)S(1)}, u32[]{:S(2)}, u32[]{:S(2)}) %collective-permute-start.2) | collective-permute-done | bytes 262176 | tf_op jit(solution)/shard_map/ppermute | solution.py:40
  57.1 8.2 %collective-permute-done.3.refs_11_ = bf16[512,256]{1,0:T(8,128)(2,1)S(1)} collective-permute-done((bf16[512,256]{1,0:T(8,128)(2,1)S(1)}, bf16[512,256]{1,0:T(8,128)(2,1)S(1)}, u32[]{:S(2)}, u32[]{:S(2)}) %collective-permute-start.3) | collective-permute-done | bytes 262176 | tf_op jit(solution)/shard_map/ppermute | solution.py:40
  65.4 3.6 %broadcast_in_dim.22 = bf16[4,1024,896]{2,1,0:T(8,128)(2,1)} broadcast(bf16[1024,896]{1,0:T(8,128)(2,1)S(1)} %bitcast.42), dimensions={1,2} | broadcast | bytes 9175040 | tf_op jit(solution)/shard_map/broadcast_in_dim | solution.py:34
  68.9 5.6 %all-to-all-start.2 = ((bf16[4,1024,896]{2,1,0:T(8,128)(2,1)}), bf16[4,1024,896]{2,1,0:T(8,128)(2,1)}, u32[]{:S(2)}, u32[]{:S(2)}) async-start(bf16[4,1024,896]{2,1,0:T(8,128)(2,1)} %broadcast_in_dim.22), calls=%async_computation.2 | async-start | bytes 14680064 | tf_op jit(solution)/shard_map/all_to_all | solution.py:35
  74.5 2.8 %collective-permute-start.4 = (bf16[256,7168]{1,0:T(8,128)(2,1)}, bf16[256,7168]{1,0:T(8,128)(2,1)}, u32[]{:S(2)}, u32[]{:S(2)}) collective-permute-start(bf16[256,7168]{1,0:T(8,128)(2,1)} %mine.1), channel_id=1, source_target_pairs={{0,1},{1,0},{2,3},{3,2},{4,5},{5,4},{6,7},{7,6},{8,9},{9,8},{10,11... | collective-permute-start | bytes 11010056 | tf_op jit(solution)/shard_map/ppermute | solution.py:44
  77.3 3.9 %collective-permute-start.6 = (bf16[512,256]{1,0:T(8,128)(2,1)S(1)}, bf16[512,256]{1,0:T(8,128)(2,1)S(1)}, u32[]{:S(2)}, u32[]{:S(2)}) collective-permute-start(bf16[512,256]{1,0:T(8,128)(2,1)S(1)} %collective-permute-done.2.refs_5_), channel_id=1, source_target_pairs={{0,128},{128,256},{256,384},{384,448},{448,320},{320,192},{192,64}... | collective-permute-start | bytes 786440 | tf_op jit(solution)/shard_map/ppermute | solution.py:40
  81.3 1.9 %collective-permute-start.9 = (bf16[512,256]{1,0:T(8,128)(2,1)S(1)}, bf16[512,256]{1,0:T(8,128)(2,1)S(1)}, u32[]{:S(2)}, u32[]{:S(2)}) collective-permute-start(bf16[512,256]{1,0:T(8,128)(2,1)S(1)} %collective-permute-done.3.refs_11_), channel_id=1, source_target_pairs={{0,64},{128,0},{256,128},{384,256},{448,384},{320,448},{192,320},{... | collective-permute-start | bytes 786440 | tf_op jit(solution)/shard_map/ppermute | solution.py:40
  83.2 4.1 %collective-permute-done.6.refs_6_ = bf16[512,256]{1,0:T(8,128)(2,1)S(1)} collective-permute-done((bf16[512,256]{1,0:T(8,128)(2,1)S(1)}, bf16[512,256]{1,0:T(8,128)(2,1)S(1)}, u32[]{:S(2)}, u32[]{:S(2)}) %collective-permute-start.6) | collective-permute-done | bytes 262176 | tf_op jit(solution)/shard_map/ppermute | solution.py:40
  87.3 4.8 %collective-permute-start.7 = (bf16[512,256]{1,0:T(8,128)(2,1)S(1)}, bf16[512,256]{1,0:T(8,128)(2,1)S(1)}, u32[]{:S(2)}, u32[]{:S(2)}) collective-permute-start(bf16[512,256]{1,0:T(8,128)(2,1)S(1)} %collective-permute-done.6.refs_6_), channel_id=1, source_target_pairs={{0,128},{128,256},{256,384},{384,448},{448,320},{320,192},{192,64}... | collective-permute-start | bytes 786440 | tf_op jit(solution)/shard_map/ppermute | solution.py:40
  92.1 2.4 %collective-permute-done.9.refs_10_ = bf16[512,256]{1,0:T(8,128)(2,1)S(1)} collective-permute-done((bf16[512,256]{1,0:T(8,128)(2,1)S(1)}, bf16[512,256]{1,0:T(8,128)(2,1)S(1)}, u32[]{:S(2)}, u32[]{:S(2)}) %collective-permute-start.9) | collective-permute-done | bytes 262176 | tf_op jit(solution)/shard_map/ppermute | solution.py:40
  94.5 2.3 %collective-permute-start.10 = (bf16[512,256]{1,0:T(8,128)(2,1)S(1)}, bf16[512,256]{1,0:T(8,128)(2,1)S(1)}, u32[]{:S(2)}, u32[]{:S(2)}) collective-permute-start(bf16[512,256]{1,0:T(8,128)(2,1)S(1)} %collective-permute-done.9.refs_10_), channel_id=1, source_target_pairs={{0,64},{128,0},{256,128},{384,256},{448,384},{320,448},{192,320},{... | collective-permute-start | bytes 786440 | tf_op jit(solution)/shard_map/ppermute | solution.py:40
  96.9 3.2 %collective-permute-done.7.refs_7_ = bf16[512,256]{1,0:T(8,128)(2,1)S(1)} collective-permute-done((bf16[512,256]{1,0:T(8,128)(2,1)S(1)}, bf16[512,256]{1,0:T(8,128)(2,1)S(1)}, u32[]{:S(2)}, u32[]{:S(2)}) %collective-permute-start.7) | collective-permute-done | bytes 262176 | tf_op jit(solution)/shard_map/ppermute | solution.py:40
  100.1 2.5 %collective-permute-start.8 = (bf16[512,256]{1,0:T(8,128)(2,1)S(1)}, bf16[512,256]{1,0:T(8,128)(2,1)S(1)}, u32[]{:S(2)}, u32[]{:S(2)}) collective-permute-start(bf16[512,256]{1,0:T(8,128)(2,1)S(1)} %collective-permute-done.7.refs_7_), channel_id=1, source_target_pairs={{0,128},{128,256},{256,384},{384,448},{448,320},{320,192},{192,64}... | collective-permute-start | bytes 786440 | tf_op jit(solution)/shard_map/ppermute | solution.py:40
  102.7 9.1 %collective-permute-done.10.refs_9_ = bf16[512,256]{1,0:T(8,128)(2,1)S(1)} collective-permute-done((bf16[512,256]{1,0:T(8,128)(2,1)S(1)}, bf16[512,256]{1,0:T(8,128)(2,1)S(1)}, u32[]{:S(2)}, u32[]{:S(2)}) %collective-permute-start.10) | collective-permute-done | bytes 262176 | tf_op jit(solution)/shard_map/ppermute | solution.py:40
  111.8 2.8 %collective-permute-done.8.refs_8_ = bf16[512,256]{1,0:T(8,128)(2,1)S(1)} collective-permute-done((bf16[512,256]{1,0:T(8,128)(2,1)S(1)}, bf16[512,256]{1,0:T(8,128)(2,1)S(1)}, u32[]{:S(2)}, u32[]{:S(2)}) %collective-permute-start.8) | collective-permute-done | bytes 262176 | tf_op jit(solution)/shard_map/ppermute | solution.py:40
  114.6 3.7 %all-to-all-done.2 = bf16[4,1024,896]{2,1,0:T(8,128)(2,1)} async-done(((bf16[4,1024,896]{2,1,0:T(8,128)(2,1)}), bf16[4,1024,896]{2,1,0:T(8,128)(2,1)}, u32[]{:S(2)}, u32[]{:S(2)}) %all-to-all-start.2) | async-done | bytes 7340064 | tf_op jit(solution)/shard_map/all_to_all | solution.py:35
  118.3 5.1 %shard_map.61 = (f32[256,896]{1,0:T(8,128)S(1)}, bf16[256,896]{1,0:T(8,128)(2,1)S(1)}) custom-call(s32[8]{0:T(128)S(1)} %dynamic_slice.3.ring, bf16[16,2,8,16,896]{4,3,2,1,0:T(8,128)(2,1)} %bitcast.22.moved.refs_0_.refs_1_.refs_2_.refs_3_, bf16[16,2,8,16,896]{4,3,2,1,0:T(8,128)(2,1)} %bitcast.22.moved.refs_0_.refs_1_.refs_2_.refs_3_, ...), custom_call_target="tpu_custom_call" | custom-call | flops 1879048192 | bytes 8388608 | tf_op jit(solution)/shard_map/pallas_call | solution.py:133
  123.4 3.6 %collective-permute-start.11 = (bf16[256,896]{1,0:T(8,128)(2,1)S(1)}, bf16[256,896]{1,0:T(8,128)(2,1)S(1)}, u32[]{:S(2)}, u32[]{:S(2)}) collective-permute-start(bf16[256,896]{1,0:T(8,128)(2,1)S(1)} %get-tuple-element.21), channel_id=1, source_target_pairs={{0,1},{1,0},{2,3},{3,2},{4,5},{5,4},{6,7},{7,6},{8,9},{9,8},{10,11... | collective-permute-start | bytes 1376264 | tf_op jit(solution)/shard_map/ppermute | solution.py:44
  127.1 5.2 %shard_map.59 = (bf16[256,256]{1,0:T(8,128)(2,1)S(1)}, bf16[256,256]{1,0:T(8,128)(2,1)S(1)}) custom-call(bf16[16,2,8,16,896]{4,3,2,1,0:T(8,128)(2,1)} %bitcast.22.moved.refs_0_.refs_1_.refs_2_.refs_3_, bf16[256,7168]{1,0:T(8,128)(2,1)S(1)} %copy-done, bf16[256,7168]{1,0:T(8,128)(2,1)} %collective-permute-done.4.theirs), custom_call_target="tpu_custom_call" | custom-call | flops 1879048192 | bytes 11534336 | tf_op jit(solution)/shard_map/pallas_call | solution.py:93
  133.0 1.9 %collective-permute-start.5 = (bf16[256,256]{1,0:T(8,128)(2,1)S(1)}, bf16[256,256]{1,0:T(8,128)(2,1)S(1)}, u32[]{:S(2)}, u32[]{:S(2)}) collective-permute-start(bf16[256,256]{1,0:T(8,128)(2,1)S(1)} %get-tuple-element.17), channel_id=1, source_target_pairs={{0,1},{1,0},{2,3},{3,2},{4,5},{5,4},{6,7},{7,6},{8,9},{9,8},{10,11... | collective-permute-start | bytes 393224 | tf_op jit(solution)/shard_map/ppermute | solution.py:44
  136.8 1.8 %shard_map.60 = bf16[64,8,256]{2,1,0:T(8,128)(2,1)} custom-call(s32[5]{0:T(128)} %stack.23.place, bf16[32,8,256]{2,1,0:T(8,128)(2,1)} %bitcast.41, bf16[32,8,256]{2,1,0:T(8,128)(2,1)} %bitcast.53), custom_call_target="tpu_custom_call" | custom-call | tf_op jit(solution)/shard_map/pallas_call | solution.py:58
  (23 shorter events, 3.8 us)
Async XLA Ops:
  0.6 27.1 %collective-permute-start = (bf16[8,7168]{1,0:T(8,128)(2,1)}, bf16[8,7168]{1,0:T(8,128)(2,1)S(1)}, u32[]{:S(2)}, u32[]{:S(2)}) collective-permute-start(bf16[8,7168]{1,0:T(8,128)(2,1)} %param.5), channel_id=1, source_target_pairs={{0,2},{2,0},{1,3},{3,1},{4,6},{6,4},{5,7},{7,5},{8,10},{10,8},{9,1... | collective-permute-start | bytes 344072 | tf_op jit(solution)/shard_map/ppermute | solution.py:44
  18.5 23.2 %all-to-all-start = ((bf16[16,8,896]{2,1,0:T(8,128)(2,1)}), bf16[16,8,896]{2,1,0:T(8,128)(2,1)S(1)}, u32[]{:S(2)}, u32[]{:S(2)}) async-start(bf16[16,8,896]{2,1,0:T(8,128)(2,1)} %bitcast.19), calls=%async_computation | async-start | bytes 458752 | tf_op jit(solution)/shard_map/all_to_all | solution.py:174
  24.5 4.3 %collective-permute-start.1 = (bf16[256,256]{1,0:T(8,128)(2,1)S(1)}, bf16[256,256]{1,0:T(8,128)(2,1)S(1)}, u32[]{:S(2)}, u32[]{:S(2)}) collective-permute-start(bf16[256,256]{1,0:T(8,128)(2,1)S(1)} %bitcast.54), channel_id=1, source_target_pairs={{0,1},{1,0},{2,3},{3,2},{4,5},{5,4},{6,7},{7,6},{8,9},{9,8},{10,11... | collective-permute-start | bytes 393224 | tf_op jit(solution)/shard_map/ppermute | solution.py:44
  43.2 22.2 %all-to-all-start.1 = ((bf16[4,256,896]{2,1,0:T(8,128)(2,1)}), bf16[4,256,896]{2,1,0:T(8,128)(2,1)S(1)}, u32[]{:S(2)}, u32[]{:S(2)}) async-start(bf16[4,256,896]{2,1,0:T(8,128)(2,1)} %broadcast_in_dim.10), calls=%async_computation.1 | async-start | bytes 3670016 | tf_op jit(solution)/shard_map/all_to_all | solution.py:35
  47.4 9.7 %collective-permute-start.2 = (bf16[512,256]{1,0:T(8,128)(2,1)S(1)}, bf16[512,256]{1,0:T(8,128)(2,1)S(1)}, u32[]{:S(2)}, u32[]{:S(2)}) collective-permute-start(bf16[512,256]{1,0:T(8,128)(2,1)S(1)} %pad_maximum_fusion.1.refs_4_), channel_id=1, source_target_pairs={{0,128},{128,256},{256,384},{384,448},{448,320},{320,192},{192,64}... | collective-permute-start | bytes 786440 | tf_op jit(solution)/shard_map/ppermute | solution.py:40
  52.5 12.8 %collective-permute-start.3 = (bf16[512,256]{1,0:T(8,128)(2,1)S(1)}, bf16[512,256]{1,0:T(8,128)(2,1)S(1)}, u32[]{:S(2)}, u32[]{:S(2)}) collective-permute-start(bf16[512,256]{1,0:T(8,128)(2,1)S(1)} %pad_maximum_fusion.1.refs_4_), channel_id=1, source_target_pairs={{0,64},{128,0},{256,128},{384,256},{448,384},{320,448},{192,320},{... | collective-permute-start | bytes 786440 | tf_op jit(solution)/shard_map/ppermute | solution.py:40
  68.9 33.6 %copy-start.3 = (s32[64]{0:T(128)S(1)}, s32[64]{0:T(128)}, u32[]{:S(2)}) copy-start(s32[64]{0:T(128)} %constant.29.clone) | copy-start | bytes 772
  68.9 49.4 %all-to-all-start.2 = ((bf16[4,1024,896]{2,1,0:T(8,128)(2,1)}), bf16[4,1024,896]{2,1,0:T(8,128)(2,1)}, u32[]{:S(2)}, u32[]{:S(2)}) async-start(bf16[4,1024,896]{2,1,0:T(8,128)(2,1)} %broadcast_in_dim.22), calls=%async_computation.2 | async-start | bytes 14680064 | tf_op jit(solution)/shard_map/all_to_all | solution.py:35
  74.5 52.6 %collective-permute-start.4 = (bf16[256,7168]{1,0:T(8,128)(2,1)}, bf16[256,7168]{1,0:T(8,128)(2,1)}, u32[]{:S(2)}, u32[]{:S(2)}) collective-permute-start(bf16[256,7168]{1,0:T(8,128)(2,1)} %mine.1), channel_id=1, source_target_pairs={{0,1},{1,0},{2,3},{3,2},{4,5},{5,4},{6,7},{7,6},{8,9},{9,8},{10,11... | collective-permute-start | bytes 11010056 | tf_op jit(solution)/shard_map/ppermute | solution.py:44
  77.3 10.0 %collective-permute-start.6 = (bf16[512,256]{1,0:T(8,128)(2,1)S(1)}, bf16[512,256]{1,0:T(8,128)(2,1)S(1)}, u32[]{:S(2)}, u32[]{:S(2)}) collective-permute-start(bf16[512,256]{1,0:T(8,128)(2,1)S(1)} %collective-permute-done.2.refs_5_), channel_id=1, source_target_pairs={{0,128},{128,256},{256,384},{384,448},{448,320},{320,192},{192,64}... | collective-permute-start | bytes 786440 | tf_op jit(solution)/shard_map/ppermute | solution.py:40
  81.3 13.2 %collective-permute-start.9 = (bf16[512,256]{1,0:T(8,128)(2,1)S(1)}, bf16[512,256]{1,0:T(8,128)(2,1)S(1)}, u32[]{:S(2)}, u32[]{:S(2)}) collective-permute-start(bf16[512,256]{1,0:T(8,128)(2,1)S(1)} %collective-permute-done.3.refs_11_), channel_id=1, source_target_pairs={{0,64},{128,0},{256,128},{384,256},{448,384},{320,448},{192,320},{... | collective-permute-start | bytes 786440 | tf_op jit(solution)/shard_map/ppermute | solution.py:40
  87.3 12.8 %collective-permute-start.7 = (bf16[512,256]{1,0:T(8,128)(2,1)S(1)}, bf16[512,256]{1,0:T(8,128)(2,1)S(1)}, u32[]{:S(2)}, u32[]{:S(2)}) collective-permute-start(bf16[512,256]{1,0:T(8,128)(2,1)S(1)} %collective-permute-done.6.refs_6_), channel_id=1, source_target_pairs={{0,128},{128,256},{256,384},{384,448},{448,320},{320,192},{192,64}... | collective-permute-start | bytes 786440 | tf_op jit(solution)/shard_map/ppermute | solution.py:40
  94.5 17.3 %collective-permute-start.10 = (bf16[512,256]{1,0:T(8,128)(2,1)S(1)}, bf16[512,256]{1,0:T(8,128)(2,1)S(1)}, u32[]{:S(2)}, u32[]{:S(2)}) collective-permute-start(bf16[512,256]{1,0:T(8,128)(2,1)S(1)} %collective-permute-done.9.refs_10_), channel_id=1, source_target_pairs={{0,64},{128,0},{256,128},{384,256},{448,384},{320,448},{192,320},{... | collective-permute-start | bytes 786440 | tf_op jit(solution)/shard_map/ppermute | solution.py:40
  100.1 14.5 %collective-permute-start.8 = (bf16[512,256]{1,0:T(8,128)(2,1)S(1)}, bf16[512,256]{1,0:T(8,128)(2,1)S(1)}, u32[]{:S(2)}, u32[]{:S(2)}) collective-permute-start(bf16[512,256]{1,0:T(8,128)(2,1)S(1)} %collective-permute-done.7.refs_7_), channel_id=1, source_target_pairs={{0,128},{128,256},{256,384},{384,448},{448,320},{320,192},{192,64}... | collective-permute-start | bytes 786440 | tf_op jit(solution)/shard_map/ppermute | solution.py:40
  118.3 8.8 %copy-start = (bf16[256,7168]{1,0:T(8,128)(2,1)S(1)}, bf16[256,7168]{1,0:T(8,128)(2,1)}, u32[]{:S(2)}) copy-start(bf16[256,7168]{1,0:T(8,128)(2,1)} %mine.1) | copy-start | bytes 11010052
  123.4 15.2 %collective-permute-start.11 = (bf16[256,896]{1,0:T(8,128)(2,1)S(1)}, bf16[256,896]{1,0:T(8,128)(2,1)S(1)}, u32[]{:S(2)}, u32[]{:S(2)}) collective-permute-start(bf16[256,896]{1,0:T(8,128)(2,1)S(1)} %get-tuple-element.21), channel_id=1, source_target_pairs={{0,1},{1,0},{2,3},{3,2},{4,5},{5,4},{6,7},{7,6},{8,9},{9,8},{10,11... | collective-permute-start | bytes 1376264 | tf_op jit(solution)/shard_map/ppermute | solution.py:44
  132.3 0.7 copy-start.1
  133.0 3.2 %collective-permute-start.5 = (bf16[256,256]{1,0:T(8,128)(2,1)S(1)}, bf16[256,256]{1,0:T(8,128)(2,1)S(1)}, u32[]{:S(2)}, u32[]{:S(2)}) collective-permute-start(bf16[256,256]{1,0:T(8,128)(2,1)S(1)} %get-tuple-element.17), channel_id=1, source_target_pairs={{0,1},{1,0},{2,3},{3,2},{4,5},{5,4},{6,7},{7,6},{8,9},{9,8},{10,11... | collective-permute-start | bytes 393224 | tf_op jit(solution)/shard_map/ppermute | solution.py:44
  136.2 0.6 copy-start.2

commit v3 on v0

v3 whole, which is shorter than its diff:
```python
import functools

import jax
import jax.numpy as jnp
from jax import lax
from jax.experimental import pallas as pl
from jax.experimental.pallas import tpu as pltpu
from jax.sharding import Mesh, PartitionSpec as P

NX, NY, NZ, NC = 4, 4, 2, 2
AXES = ("dp", "x", "y", "zh", "core")
RING = (0, 2, 4, 6, 7, 5, 3, 1)
BEFORE = tuple(RING[(RING.index(g) - k) % len(RING)] for g in range(len(RING)) for k in range(len(RING)))
TENSOR = ("x", "y", "zh", "core")


def lines(first):
    def at(x, y, z, c):
        return ((x * NY + y) * NZ + z) * NC + c

    groups = []
    for z in range(NZ):
        for c in range(NC):
            for k in range(NX):
                if (c == 0) == first:
                    groups.append([at(i, k, z, c) for i in range(NX)])
                else:
                    groups.append([at(k, i, z, c) for i in range(NY)])
    return groups


def spread(values, first):
    n = values.shape[0]
    copies = jnp.broadcast_to(values[None], (NX,) + values.shape).reshape((NX * n,) + values.shape[1:])
    return lax.all_to_all(copies, TENSOR, 0, 0, axis_index_groups=lines(first), tiled=True)


def turn(values, step):
    pairs = [(RING[i], RING[(i + step) % len(RING)]) for i in range(len(RING))]
    return lax.ppermute(values, "dp", pairs)


def swap(values, axis):
    return lax.ppermute(values, axis, [(0, 1), (1, 0)])


def products_kernel(ring, moved, mine, theirs, *refs):
    parts, refs = refs[:-8], refs[-8:]
    near_in, near_weight, far, wide, strips, weights, total, sems = refs
    chips, _, n_dp, _, columns = moved.shape
    rows = near_weight.shape[0]
    half = n_dp // 2
    blocks = far.shape[0]

    arrive = [
        pltpu.make_async_copy(moved.at[:, 1, ring[k]], strips.at[k], sems.at[k]) for k in range(n_dp)
    ]
    for copy in arrive:
        copy.start()
    fetch = []
    for h in range(2):
        cut = pl.ds(h * half * columns, half * columns)
        at = n_dp + 3 * h
        fetch.append([
            pltpu.make_async_copy(moved.at[:, 0, pl.ds(h * half, half)], wide.at[h], sems.at[at]),
            pltpu.make_async_copy(mine.at[:, cut], weights.at[0, h], sems.at[at + 1]),
            pltpu.make_async_copy(theirs.at[:, cut], weights.at[1, h], sems.at[at + 2]),
        ])
        for copy in fetch[h]:
            copy.start()

    for h in range(2):
        for copy in arrive[h * half:(h + 1) * half]:
            copy.wait()
        right = jnp.concatenate(
            [strips[k, i] for k in range(h * half, (h + 1) * half) for i in range(chips)], 0
        )
        left = jnp.concatenate([part[...] for part in parts[h * half:(h + 1) * half]], 1)
        term = jnp.dot(left, right, preferred_element_type=jnp.float32)
        if h == 0:
            total[...] = term
        else:
            near_weight[...] = total[:rows] + term[:rows]
            part = total[rows:] + term[rows:]
            far[:, :, rows:] = part.reshape(blocks, -1, columns).astype(far.dtype)

    sums = [None, None]
    for h in range(2):
        for copy in fetch[h]:
            copy.wait()
        left = jnp.concatenate(
            [jnp.concatenate([wide[h, i, j] for i in range(chips)], 0) for j in range(half)], 1
        )
        for at in range(NC):
            term = lax.dot_general(
                left, weights[at, h], (((1,), (1,)), ((), ())), preferred_element_type=jnp.float32
            )
            sums[at] = term if h == 0 else sums[at] + term
    near_in[...] = sums[0].reshape(blocks, -1, rows).astype(near_in.dtype)
    far[:, :, :rows] = sums[1].reshape(blocks, -1, rows).astype(far.dtype)


def products(ring, moved, weight, weight_other, parts, held):
    chips, _, n_dp, deep, columns = moved.shape
    rows = weight.shape[0]
    blocks = chips * deep // held
    vmem, whole = pl.BlockSpec(memory_space=pltpu.VMEM), pl.BlockSpec(memory_space=pl.ANY)
    return pl.pallas_call(
        products_kernel,
        out_shape=(
            jax.ShapeDtypeStruct((blocks, held, rows), jnp.bfloat16),
            jax.ShapeDtypeStruct((rows, columns), jnp.float32),
            jax.ShapeDtypeStruct((blocks, held, rows + columns), jnp.bfloat16),
        ),
        in_specs=[pl.BlockSpec(memory_space=pltpu.SMEM), whole, pl.BlockSpec(memory_space=pltpu.HBM), whole]
        + [vmem] * len(parts),
        out_specs=(vmem, vmem, vmem),
        scratch_shapes=[
            pltpu.VMEM((2, chips, n_dp // 2, deep, columns), jnp.bfloat16),
            pltpu.VMEM((n_dp, chips, deep, columns), jnp.bfloat16),
            pltpu.VMEM((NC, 2, rows, n_dp // 2 * columns), jnp.bfloat16),
            pltpu.VMEM((NC * rows, columns), jnp.float32),
            pltpu.SemaphoreType.DMA((n_dp + 6,)),
        ],
        compiler_params=pltpu.CompilerParams(vmem_limit_bytes=50 * 1024 * 1024),
        cost_estimate=pl.CostEstimate(
            flops=8 * blocks * held * rows * n_dp * columns, bytes_accessed=17 * 1024 * 1024, transcendentals=0
        ),
    )(ring, moved, weight, weight_other, *parts)


def finish_kernel(place, near_in, near_weight, far, grad_in, grad_weight):
    zh, c = place[2], place[3]
    rows = near_in.shape[-1]
    for part, core in ((near_in, c), (far, 1 - c)):
        for at in range(near_in.shape[0]):
            at2, at1, turned = at // (NX * NZ), (at // NZ) % NX, at % NZ
            px, py = jnp.where(core == 0, at1, at2), jnp.where(core == 0, at2, at1)
            z = zh if turned == 0 else 1 - zh
            grad_in[((px * NY + py) * NZ + z) * NC + core] = part[at, :, :rows]
    part = far[:, :, rows:].astype(jnp.float32).reshape(near_weight.shape)
    grad_weight[...] = (near_weight[...] + part).astype(grad_weight.dtype)


def finish(place, near_in, near_weight, far):
    blocks, held, rows = near_in.shape
    vmem = pl.BlockSpec(memory_space=pltpu.VMEM)
    return pl.pallas_call(
        finish_kernel,
        out_shape=(
            jax.ShapeDtypeStruct((NC * blocks, held, rows), jnp.bfloat16),
            jax.ShapeDtypeStruct(near_weight.shape, jnp.bfloat16),
        ),
        in_specs=[pl.BlockSpec(memory_space=pltpu.SMEM), vmem, vmem, vmem],
        out_specs=(vmem, vmem),
        compiler_params=pltpu.CompilerParams(vmem_limit_bytes=8 * 1024 * 1024),
    )(place, near_in, near_weight, far)


def body(attn, grad_out, weight):
    place = jnp.stack([lax.axis_index(a) for a in TENSOR + ("dp",)]).astype(jnp.int32)
    c = place[3]
    n_dp = lax.axis_size("dp")
    rows = attn.shape[1]
    held, width = grad_out.shape
    columns = width // n_dp
    blocks = NX * NY * NZ
    tokens = blocks * held
    deep = NZ * held

    parts = attn.reshape(NX, NY, NZ, NC, held, rows)
    low, high = parts[:, :, :, 0].swapaxes(0, 1), parts[:, :, :, 1]
    mine = jnp.where(c == 0, low, high).reshape(tokens, rows).T
    other = jnp.where(c == 0, high, low).reshape(tokens, rows).T
    wide = jnp.concatenate([mine, swap(other, "core")], 0)

    strips = jnp.broadcast_to(
        grad_out.reshape(held, n_dp, 1, columns).transpose(1, 2, 0, 3), (n_dp, NZ, held, columns)
    ).reshape(n_dp * deep, columns)
    sliced = lax.all_to_all(strips, ("dp", "zh"), 0, 0, tiled=True)
    both = jnp.concatenate([grad_out, swap(grad_out, "zh")], 0)
    both = both.reshape(deep, n_dp, columns).swapaxes(0, 1).reshape(n_dp * deep, columns)

    both, wide = lax.optimization_barrier((both, wide))
    moved = spread(jnp.concatenate([both, sliced], 0), True)
    weight_other = swap(weight, "core")

    wide, _ = lax.optimization_barrier((wide, sliced))
    ahead, back = [wide, turn(wide, 1)], [wide, turn(wide, -1)]
    moved, ahead[1], back[1] = lax.optimization_barrier((moved, ahead[1], back[1]))
    moved = spread(moved, False).reshape(NX * NY, 2, n_dp, deep, columns)
    for _ in range(n_dp // 2 - 1):
        ahead.append(turn(ahead[-1], 1))
    for _ in range(n_dp // 2 - 2):
        back.append(turn(back[-1], -1))
    ring = lax.dynamic_slice_in_dim(jnp.asarray(BEFORE, jnp.int32), place[4] * n_dp, n_dp)

    near_in, near_weight, far = products(ring, moved, weight, weight_other, ahead + back[:0:-1], held)
    far = swap(far, "core")
    grad_in, grad_weight = finish(place, near_in, near_weight, far)
    return grad_in.reshape(NC * tokens, rows), grad_weight


def solution(mesh):
    n_dp = mesh.shape["dp"]
    fine = Mesh(mesh.devices.reshape(n_dp, NX, NY, NZ, NC), AXES)
    in_specs = (P("dp", TENSOR), P(("dp",) + TENSOR, None), P(TENSOR, None))
    out_specs = (P("dp", TENSOR), P(TENSOR, "dp"))
    return jax.shard_map(body, mesh=fine, in_specs=in_specs, out_specs=out_specs, check_vma=False)
```

time: 287 us -> 135 us (0.47)
  waiting for transfers between devices: 251 us -> 50.9 us
  starting transfers between devices: 0.08 us -> 63 us
  matrix products: 14 us -> 0 us
  between operations: 14 us -> 0.84 us
  Pallas kernels: 0 us -> 10.4 us
    all_gather x1 -> x0, waiting for transfers between devices: 170 us -> none  [body(): group_grad = lax.all_gather(grad_out, 'tensor', axis=0, tiled=True)]
    unnamed x3 -> x0, waiting for transfers between devices: 80.8 us -> none
    ppermute x0 -> x11, starting transfers between devices: none -> 48.4 us  [the longest x4 25.8 us: swap(): return lax.ppermute(values, axis, [(0, 1), (1, 0)])]
    ppermute x0 -> x11, waiting for transfers between devices: none -> 34.2 us  [the longest x7 32.5 us: turn(): return lax.ppermute(values, 'dp', pairs)]
    all_to_all x0 -> x3, waiting for transfers between devices: none -> 16.7 us  [the longest x1 13 us: body(): sliced = lax.all_to_all(strips, ('dp', 'zh'), 0, 0, tiled=True)]
    all_to_all x0 -> x3, starting transfers between devices: none -> 14.6 us  [the longest x2 9.76 us: spread(): lax.all_to_all(copies, TENSOR, 0, 0, axis_index_groups=lines(first), tile...]
    dot_general x2 -> x0, matrix products: 14 us -> none  [the longest x1 7.09 us: contract_tokens(): lax.dot_general(left, right, (((0,), (0,)), ((), ())), preferred_element_...]
    pallas_call x0 -> x2, Pallas kernels: none -> 10.4 us  [the longest x1 8.83 us: products(): pl.pallas_call(products_kernel, out_shape=(jax.ShapeDtypeStruct((blocks,...]
  transfers between devices with their start and end apart: 2 -> 14, of which waited for: 2 -> 10; matrix products, arithmetic and copies ran while one was open for 2% -> 3% of each run, Pallas kernels for 0% -> 0%
where the time goes in v3:
time: 135 us; the launch traced here: 134 us
  starting transfers between devices  63 us (47%)
  waiting for transfers between devices  50.9 us (38%)
  Pallas kernels  10.4 us (8%)
  local copies, waits for them, and re-layouts  7 us (5%)
  other arithmetic  1.99 us (1%)
    ppermute x7, waiting for transfers between devices, turn(): return lax.ppermute(values, 'dp', pairs)  32.5 us
    ppermute x4, starting transfers between devices, swap(): return lax.ppermute(values, axis, [(0, 1), (1, 0)])  25.8 us
    ppermute x7, starting transfers between devices, turn(): return lax.ppermute(values, 'dp', pairs)  22.6 us
    all_to_all x1, waiting for transfers between devices, body(): sliced = lax.all_to_all(strips, ('dp', 'zh'), 0, 0, tiled=True)  13 us
    all_to_all x2, starting transfers between devices, spread(): lax.all_to_all(copies, TENSOR, 0, 0, axis_index_groups=lines(first), tile...  9.76 us
    pallas_call x1, Pallas kernels, products(): pl.pallas_call(products_kernel, out_shape=(jax.ShapeDtypeStruct((blocks,...  8.83 us
    broadcast_in_dim x2, local copies, waits for them, and re-layouts, spread(): jnp.broadcast_to(values[None], (NX,) + values.shape)  4.97 us
    all_to_all x1, starting transfers between devices, body(): sliced = lax.all_to_all(strips, ('dp', 'zh'), 0, 0, tiled=True)  4.85 us
  transfers between devices with their start and end apart: 14, of which 10 were waited for; matrix products, arithmetic and copies ran while one was open for 3% of the time, Pallas kernels for 0%

profile of v3, /device:TPU:1, one launch (start us, length us, event | category | flops | bytes accessed | tf_op | source)
XLA Modules:
  0.0 134.1 jit_solution(8201489393701540147)
XLA Ops:
  0.6 16.3 %collective-permute-start = (bf16[8,7168]{1,0:T(8,128)(2,1)}, bf16[8,7168]{1,0:T(8,128)(2,1)S(1)}, u32[]{:S(2)}, u32[]{:S(2)}) collective-permute-start(bf16[8,7168]{1,0:T(8,128)(2,1)} %param.5), channel_id=1, source_target_pairs={{0,2},{2,0},{1,3},{3,1},{4,6},{6,4},{5,7},{7,5},{8,10},{10,8},{9,1... | collective-permute-start | bytes 344072 | tf_op jit(solution)/shard_map/ppermute | solution.py:44
  16.9 1.6 %broadcast_in_dim.9 = bf16[8,2,8,896]{3,2,1,0:T(8,128)(2,1)} broadcast(bf16[8,8,896]{2,1,0:T(8,128)(2,1)} %bitcast.47), dimensions={0,2,3} | broadcast | bytes 344064 | tf_op jit(solution)/shard_map/broadcast_in_dim | solution.py:177
  18.5 4.8 %all-to-all-start = ((bf16[16,8,896]{2,1,0:T(8,128)(2,1)}), bf16[16,8,896]{2,1,0:T(8,128)(2,1)S(1)}, u32[]{:S(2)}, u32[]{:S(2)}) async-start(bf16[16,8,896]{2,1,0:T(8,128)(2,1)} %bitcast.19), calls=%async_computation | async-start | bytes 458752 | tf_op jit(solution)/shard_map/all_to_all | solution.py:180
  23.4 1.0 broadcast_select_fusion.1
  24.4 0.1 copy.14
  24.5 3.1 %collective-permute-start.1 = (bf16[256,256]{1,0:T(8,128)(2,1)S(1)}, bf16[256,256]{1,0:T(8,128)(2,1)S(1)}, u32[]{:S(2)}, u32[]{:S(2)}) collective-permute-start(bf16[256,256]{1,0:T(8,128)(2,1)S(1)} %bitcast.49), channel_id=1, source_target_pairs={{0,1},{1,0},{2,3},{3,2},{4,5},{5,4},{6,7},{7,6},{8,9},{9,8},{10,11... | collective-permute-start | bytes 393224 | tf_op jit(solution)/shard_map/ppermute | solution.py:44
  27.8 0.9 pad_maximum_fusion.2
  28.8 13.0 %all-to-all-done = bf16[16,8,896]{2,1,0:T(8,128)(2,1)S(1)} async-done(((bf16[16,8,896]{2,1,0:T(8,128)(2,1)}), bf16[16,8,896]{2,1,0:T(8,128)(2,1)S(1)}, u32[]{:S(2)}, u32[]{:S(2)}) %all-to-all-start) | async-done | bytes 229408 | tf_op jit(solution)/shard_map/all_to_all | solution.py:180
  41.8 1.4 %broadcast_in_dim.10 = bf16[4,256,896]{2,1,0:T(8,128)(2,1)} broadcast(bf16[256,896]{1,0:T(8,128)(2,1)S(1)} %pad_maximum_fusion), dimensions={1,2} | broadcast | bytes 2293760 | tf_op jit(solution)/shard_map/broadcast_in_dim | solution.py:34
  43.2 4.2 %all-to-all-start.1 = ((bf16[4,256,896]{2,1,0:T(8,128)(2,1)}), bf16[4,256,896]{2,1,0:T(8,128)(2,1)S(1)}, u32[]{:S(2)}, u32[]{:S(2)}) async-start(bf16[4,256,896]{2,1,0:T(8,128)(2,1)} %broadcast_in_dim.10), calls=%async_computation.1 | async-start | bytes 3670016 | tf_op jit(solution)/shard_map/all_to_all | solution.py:35
  47.4 5.1 %collective-permute-start.2 = (bf16[512,256]{1,0:T(8,128)(2,1)S(1)}, bf16[512,256]{1,0:T(8,128)(2,1)S(1)}, u32[]{:S(2)}, u32[]{:S(2)}) collective-permute-start(bf16[512,256]{1,0:T(8,128)(2,1)S(1)} %pad_maximum_fusion.1.refs_0_), channel_id=1, source_target_pairs={{0,128},{128,256},{256,384},{384,448},{448,320},{320,192},{192,64}... | collective-permute-start | bytes 786440 | tf_op jit(solution)/shard_map/ppermute | solution.py:40
  52.5 1.9 %collective-permute-start.3 = (bf16[512,256]{1,0:T(8,128)(2,1)S(1)}, bf16[512,256]{1,0:T(8,128)(2,1)S(1)}, u32[]{:S(2)}, u32[]{:S(2)}) collective-permute-start(bf16[512,256]{1,0:T(8,128)(2,1)S(1)} %pad_maximum_fusion.1.refs_0_), channel_id=1, source_target_pairs={{0,64},{128,0},{256,128},{384,256},{448,384},{320,448},{192,320},{... | collective-permute-start | bytes 786440 | tf_op jit(solution)/shard_map/ppermute | solution.py:40
  54.4 2.7 %collective-permute-done.2.refs_1_ = bf16[512,256]{1,0:T(8,128)(2,1)S(1)} collective-permute-done((bf16[512,256]{1,0:T(8,128)(2,1)S(1)}, bf16[512,256]{1,0:T(8,128)(2,1)S(1)}, u32[]{:S(2)}, u32[]{:S(2)}) %collective-permute-start.2) | collective-permute-done | bytes 262176 | tf_op jit(solution)/shard_map/ppermute | solution.py:40
  57.1 8.2 %collective-permute-done.3.refs_7_ = bf16[512,256]{1,0:T(8,128)(2,1)S(1)} collective-permute-done((bf16[512,256]{1,0:T(8,128)(2,1)S(1)}, bf16[512,256]{1,0:T(8,128)(2,1)S(1)}, u32[]{:S(2)}, u32[]{:S(2)}) %collective-permute-start.3) | collective-permute-done | bytes 262176 | tf_op jit(solution)/shard_map/ppermute | solution.py:40
  65.3 3.6 %broadcast_in_dim.22 = bf16[4,1024,896]{2,1,0:T(8,128)(2,1)} broadcast(bf16[1024,896]{1,0:T(8,128)(2,1)S(1)} %bitcast.39), dimensions={1,2} | broadcast | bytes 9175040 | tf_op jit(solution)/shard_map/broadcast_in_dim | solution.py:34
  68.9 5.6 %all-to-all-start.2 = ((bf16[4,1024,896]{2,1,0:T(8,128)(2,1)}), bf16[4,1024,896]{2,1,0:T(8,128)(2,1)}, u32[]{:S(2)}, u32[]{:S(2)}) async-start(bf16[4,1024,896]{2,1,0:T(8,128)(2,1)} %broadcast_in_dim.22), calls=%async_computation.2 | async-start | bytes 14680064 | tf_op jit(solution)/shard_map/all_to_all | solution.py:35
  74.5 2.8 %collective-permute-start.4 = (bf16[256,7168]{1,0:T(8,128)(2,1)}, bf16[256,7168]{1,0:T(8,128)(2,1)}, u32[]{:S(2)}, u32[]{:S(2)}) collective-permute-start(bf16[256,7168]{1,0:T(8,128)(2,1)} %mine.1), channel_id=1, source_target_pairs={{0,1},{1,0},{2,3},{3,2},{4,5},{5,4},{6,7},{7,6},{8,9},{9,8},{10,11... | collective-permute-start | bytes 11010056 | tf_op jit(solution)/shard_map/ppermute | solution.py:44
  77.3 3.9 %collective-permute-start.5 = (bf16[512,256]{1,0:T(8,128)(2,1)S(1)}, bf16[512,256]{1,0:T(8,128)(2,1)S(1)}, u32[]{:S(2)}, u32[]{:S(2)}) collective-permute-start(bf16[512,256]{1,0:T(8,128)(2,1)S(1)} %collective-permute-done.2.refs_1_), channel_id=1, source_target_pairs={{0,128},{128,256},{256,384},{384,448},{448,320},{320,192},{192,64}... | collective-permute-start | bytes 786440 | tf_op jit(solution)/shard_map/ppermute | solution.py:40
  81.2 1.9 %collective-permute-start.8 = (bf16[512,256]{1,0:T(8,128)(2,1)S(1)}, bf16[512,256]{1,0:T(8,128)(2,1)S(1)}, u32[]{:S(2)}, u32[]{:S(2)}) collective-permute-start(bf16[512,256]{1,0:T(8,128)(2,1)S(1)} %collective-permute-done.3.refs_7_), channel_id=1, source_target_pairs={{0,64},{128,0},{256,128},{384,256},{448,384},{320,448},{192,320},{... | collective-permute-start | bytes 786440 | tf_op jit(solution)/shard_map/ppermute | solution.py:40
  83.2 4.1 %collective-permute-done.5.refs_2_ = bf16[512,256]{1,0:T(8,128)(2,1)S(1)} collective-permute-done((bf16[512,256]{1,0:T(8,128)(2,1)S(1)}, bf16[512,256]{1,0:T(8,128)(2,1)S(1)}, u32[]{:S(2)}, u32[]{:S(2)}) %collective-permute-start.5) | collective-permute-done | bytes 262176 | tf_op jit(solution)/shard_map/ppermute | solution.py:40
  87.3 4.8 %collective-permute-start.6 = (bf16[512,256]{1,0:T(8,128)(2,1)S(1)}, bf16[512,256]{1,0:T(8,128)(2,1)S(1)}, u32[]{:S(2)}, u32[]{:S(2)}) collective-permute-start(bf16[512,256]{1,0:T(8,128)(2,1)S(1)} %collective-permute-done.5.refs_2_), channel_id=1, source_target_pairs={{0,128},{128,256},{256,384},{384,448},{448,320},{320,192},{192,64}... | collective-permute-start | bytes 786440 | tf_op jit(solution)/shard_map/ppermute | solution.py:40
  92.1 2.4 %collective-permute-done.8.refs_6_ = bf16[512,256]{1,0:T(8,128)(2,1)S(1)} collective-permute-done((bf16[512,256]{1,0:T(8,128)(2,1)S(1)}, bf16[512,256]{1,0:T(8,128)(2,1)S(1)}, u32[]{:S(2)}, u32[]{:S(2)}) %collective-permute-start.8) | collective-permute-done | bytes 262176 | tf_op jit(solution)/shard_map/ppermute | solution.py:40
  94.5 2.3 %collective-permute-start.9 = (bf16[512,256]{1,0:T(8,128)(2,1)S(1)}, bf16[512,256]{1,0:T(8,128)(2,1)S(1)}, u32[]{:S(2)}, u32[]{:S(2)}) collective-permute-start(bf16[512,256]{1,0:T(8,128)(2,1)S(1)} %collective-permute-done.8.refs_6_), channel_id=1, source_target_pairs={{0,64},{128,0},{256,128},{384,256},{448,384},{320,448},{192,320},{... | collective-permute-start | bytes 786440 | tf_op jit(solution)/shard_map/ppermute | solution.py:40
  96.8 3.2 %collective-permute-done.6.refs_3_ = bf16[512,256]{1,0:T(8,128)(2,1)S(1)} collective-permute-done((bf16[512,256]{1,0:T(8,128)(2,1)S(1)}, bf16[512,256]{1,0:T(8,128)(2,1)S(1)}, u32[]{:S(2)}, u32[]{:S(2)}) %collective-permute-start.6) | collective-permute-done | bytes 262176 | tf_op jit(solution)/shard_map/ppermute | solution.py:40
  100.0 2.5 %collective-permute-start.7 = (bf16[512,256]{1,0:T(8,128)(2,1)S(1)}, bf16[512,256]{1,0:T(8,128)(2,1)S(1)}, u32[]{:S(2)}, u32[]{:S(2)}) collective-permute-start(bf16[512,256]{1,0:T(8,128)(2,1)S(1)} %collective-permute-done.6.refs_3_), channel_id=1, source_target_pairs={{0,128},{128,256},{256,384},{384,448},{448,320},{320,192},{192,64}... | collective-permute-start | bytes 786440 | tf_op jit(solution)/shard_map/ppermute | solution.py:40
  102.6 9.1 %collective-permute-done.9.refs_5_ = bf16[512,256]{1,0:T(8,128)(2,1)S(1)} collective-permute-done((bf16[512,256]{1,0:T(8,128)(2,1)S(1)}, bf16[512,256]{1,0:T(8,128)(2,1)S(1)}, u32[]{:S(2)}, u32[]{:S(2)}) %collective-permute-start.9) | collective-permute-done | bytes 262176 | tf_op jit(solution)/shard_map/ppermute | solution.py:40
  111.8 2.8 %collective-permute-done.7.refs_4_ = bf16[512,256]{1,0:T(8,128)(2,1)S(1)} collective-permute-done((bf16[512,256]{1,0:T(8,128)(2,1)S(1)}, bf16[512,256]{1,0:T(8,128)(2,1)S(1)}, u32[]{:S(2)}, u32[]{:S(2)}) %collective-permute-start.7) | collective-permute-done | bytes 262176 | tf_op jit(solution)/shard_map/ppermute | solution.py:40
  114.6 3.7 %all-to-all-done.2 = bf16[4,1024,896]{2,1,0:T(8,128)(2,1)} async-done(((bf16[4,1024,896]{2,1,0:T(8,128)(2,1)}), bf16[4,1024,896]{2,1,0:T(8,128)(2,1)}, u32[]{:S(2)}, u32[]{:S(2)}) %all-to-all-start.2) | async-done | bytes 7340064 | tf_op jit(solution)/shard_map/all_to_all | solution.py:35
  118.3 8.8 %shard_map.59 = (bf16[32,8,256]{2,1,0:T(8,128)(2,1)S(1)}, f32[256,896]{1,0:T(8,128)S(1)}, bf16[32,8,1152]{2,1,0:T(8,128)(2,1)}) custom-call(s32[8]{0:T(128)S(1)} %dynamic_slice.3.ring, bf16[16,2,8,16,896]{4,3,2,1,0:T(8,128)(2,1)} %bitcast.22.moved, bf16[256,7168]{1,0:T(8,128)(2,1)} %mine.1, bf16[256,7168]{1,0:T(8,128)(2,1)} %collective-permute-done.4.theirs, ...), custom_call_target="tpu_custom_call" | custom-call | flops 3758096384 | bytes 17825792 | tf_op jit(solution)/shard_map/pallas_call | solution.py:108
  127.2 3.6 %collective-permute-start.10 = (bf16[32,8,1152]{2,1,0:T(8,128)(2,1)}, bf16[32,8,1152]{2,1,0:T(8,128)(2,1)S(1)}, u32[]{:S(2)}, u32[]{:S(2)}) collective-permute-start(bf16[32,8,1152]{2,1,0:T(8,128)(2,1)} %get-tuple-element.21), channel_id=1, source_target_pairs={{0,1},{1,0},{2,3},{3,2},{4,5},{5,4},{6,7},{7,6},{8,9},{9,8},{10,11... | collective-permute-start | bytes 1769480 | tf_op jit(solution)/shard_map/ppermute | solution.py:44
  130.9 1.7 %collective-permute-done.10.far = bf16[32,8,1152]{2,1,0:T(8,128)(2,1)S(1)} collective-permute-done((bf16[32,8,1152]{2,1,0:T(8,128)(2,1)}, bf16[32,8,1152]{2,1,0:T(8,128)(2,1)S(1)}, u32[]{:S(2)}, u32[]{:S(2)}) %collective-permute-start.10) | collective-permute-done | bytes 589856 | tf_op jit(solution)/shard_map/ppermute | solution.py:44
  132.6 1.5 %shard_map.60 = (bf16[64,8,256]{2,1,0:T(8,128)(2,1)}, bf16[256,896]{1,0:T(8,128)(2,1)}) custom-call(s32[5]{0:T(128)S(1)} %stack.23.place, bf16[32,8,256]{2,1,0:T(8,128)(2,1)S(1)} %get-tuple-element.19.near_in, f32[256,896]{1,0:T(8,128)S(1)} %get-tuple-element.20.near_weight, bf16[32,8,1152]{2,1,0:T(8,128)(2,1)S(1)} %collective-permute-done.10.far), custom_call_target="tpu_custom_call" | custom-call | tf_op jit(solution)/shard_map/pallas_call | solution.py:148
  (13 shorter events, 0.4 us)
Async XLA Ops:
  0.6 27.1 %collective-permute-start = (bf16[8,7168]{1,0:T(8,128)(2,1)}, bf16[8,7168]{1,0:T(8,128)(2,1)S(1)}, u32[]{:S(2)}, u32[]{:S(2)}) collective-permute-start(bf16[8,7168]{1,0:T(8,128)(2,1)} %param.5), channel_id=1, source_target_pairs={{0,2},{2,0},{1,3},{3,1},{4,6},{6,4},{5,7},{7,5},{8,10},{10,8},{9,1... | collective-permute-start | bytes 344072 | tf_op jit(solution)/shard_map/ppermute | solution.py:44
  18.5 23.2 %all-to-all-start = ((bf16[16,8,896]{2,1,0:T(8,128)(2,1)}), bf16[16,8,896]{2,1,0:T(8,128)(2,1)S(1)}, u32[]{:S(2)}, u32[]{:S(2)}) async-start(bf16[16,8,896]{2,1,0:T(8,128)(2,1)} %bitcast.19), calls=%async_computation | async-start | bytes 458752 | tf_op jit(solution)/shard_map/all_to_all | solution.py:180
  24.5 4.3 %collective-permute-start.1 = (bf16[256,256]{1,0:T(8,128)(2,1)S(1)}, bf16[256,256]{1,0:T(8,128)(2,1)S(1)}, u32[]{:S(2)}, u32[]{:S(2)}) collective-permute-start(bf16[256,256]{1,0:T(8,128)(2,1)S(1)} %bitcast.49), channel_id=1, source_target_pairs={{0,1},{1,0},{2,3},{3,2},{4,5},{5,4},{6,7},{7,6},{8,9},{9,8},{10,11... | collective-permute-start | bytes 393224 | tf_op jit(solution)/shard_map/ppermute | solution.py:44
  43.2 22.2 %all-to-all-start.1 = ((bf16[4,256,896]{2,1,0:T(8,128)(2,1)}), bf16[4,256,896]{2,1,0:T(8,128)(2,1)S(1)}, u32[]{:S(2)}, u32[]{:S(2)}) async-start(bf16[4,256,896]{2,1,0:T(8,128)(2,1)} %broadcast_in_dim.10), calls=%async_computation.1 | async-start | bytes 3670016 | tf_op jit(solution)/shard_map/all_to_all | solution.py:35
  47.4 9.7 %collective-permute-start.2 = (bf16[512,256]{1,0:T(8,128)(2,1)S(1)}, bf16[512,256]{1,0:T(8,128)(2,1)S(1)}, u32[]{:S(2)}, u32[]{:S(2)}) collective-permute-start(bf16[512,256]{1,0:T(8,128)(2,1)S(1)} %pad_maximum_fusion.1.refs_0_), channel_id=1, source_target_pairs={{0,128},{128,256},{256,384},{384,448},{448,320},{320,192},{192,64}... | collective-permute-start | bytes 786440 | tf_op jit(solution)/shard_map/ppermute | solution.py:40
  52.5 12.8 %collective-permute-start.3 = (bf16[512,256]{1,0:T(8,128)(2,1)S(1)}, bf16[512,256]{1,0:T(8,128)(2,1)S(1)}, u32[]{:S(2)}, u32[]{:S(2)}) collective-permute-start(bf16[512,256]{1,0:T(8,128)(2,1)S(1)} %pad_maximum_fusion.1.refs_0_), channel_id=1, source_target_pairs={{0,64},{128,0},{256,128},{384,256},{448,384},{320,448},{192,320},{... | collective-permute-start | bytes 786440 | tf_op jit(solution)/shard_map/ppermute | solution.py:40
  68.9 33.6 %copy-start = (s32[64]{0:T(128)S(1)}, s32[64]{0:T(128)}, u32[]{:S(2)}) copy-start(s32[64]{0:T(128)} %constant.29.clone) | copy-start | bytes 772
  68.9 49.4 %all-to-all-start.2 = ((bf16[4,1024,896]{2,1,0:T(8,128)(2,1)}), bf16[4,1024,896]{2,1,0:T(8,128)(2,1)}, u32[]{:S(2)}, u32[]{:S(2)}) async-start(bf16[4,1024,896]{2,1,0:T(8,128)(2,1)} %broadcast_in_dim.22), calls=%async_computation.2 | async-start | bytes 14680064 | tf_op jit(solution)/shard_map/all_to_all | solution.py:35
  74.5 40.1 %collective-permute-start.4 = (bf16[256,7168]{1,0:T(8,128)(2,1)}, bf16[256,7168]{1,0:T(8,128)(2,1)}, u32[]{:S(2)}, u32[]{:S(2)}) collective-permute-start(bf16[256,7168]{1,0:T(8,128)(2,1)} %mine.1), channel_id=1, source_target_pairs={{0,1},{1,0},{2,3},{3,2},{4,5},{5,4},{6,7},{7,6},{8,9},{9,8},{10,11... | collective-permute-start | bytes 11010056 | tf_op jit(solution)/shard_map/ppermute | solution.py:44
  77.3 10.0 %collective-permute-start.5 = (bf16[512,256]{1,0:T(8,128)(2,1)S(1)}, bf16[512,256]{1,0:T(8,128)(2,1)S(1)}, u32[]{:S(2)}, u32[]{:S(2)}) collective-permute-start(bf16[512,256]{1,0:T(8,128)(2,1)S(1)} %collective-permute-done.2.refs_1_), channel_id=1, source_target_pairs={{0,128},{128,256},{256,384},{384,448},{448,320},{320,192},{192,64}... | collective-permute-start | bytes 786440 | tf_op jit(solution)/shard_map/ppermute | solution.py:40
  81.2 13.2 %collective-permute-start.8 = (bf16[512,256]{1,0:T(8,128)(2,1)S(1)}, bf16[512,256]{1,0:T(8,128)(2,1)S(1)}, u32[]{:S(2)}, u32[]{:S(2)}) collective-permute-start(bf16[512,256]{1,0:T(8,128)(2,1)S(1)} %collective-permute-done.3.refs_7_), channel_id=1, source_target_pairs={{0,64},{128,0},{256,128},{384,256},{448,384},{320,448},{192,320},{... | collective-permute-start | bytes 786440 | tf_op jit(solution)/shard_map/ppermute | solution.py:40
  87.3 12.8 %collective-permute-start.6 = (bf16[512,256]{1,0:T(8,128)(2,1)S(1)}, bf16[512,256]{1,0:T(8,128)(2,1)S(1)}, u32[]{:S(2)}, u32[]{:S(2)}) collective-permute-start(bf16[512,256]{1,0:T(8,128)(2,1)S(1)} %collective-permute-done.5.refs_2_), channel_id=1, source_target_pairs={{0,128},{128,256},{256,384},{384,448},{448,320},{320,192},{192,64}... | collective-permute-start | bytes 786440 | tf_op jit(solution)/shard_map/ppermute | solution.py:40
  94.5 17.3 %collective-permute-start.9 = (bf16[512,256]{1,0:T(8,128)(2,1)S(1)}, bf16[512,256]{1,0:T(8,128)(2,1)S(1)}, u32[]{:S(2)}, u32[]{:S(2)}) collective-permute-start(bf16[512,256]{1,0:T(8,128)(2,1)S(1)} %collective-permute-done.8.refs_6_), channel_id=1, source_target_pairs={{0,64},{128,0},{256,128},{384,256},{448,384},{320,448},{192,320},{... | collective-permute-start | bytes 786440 | tf_op jit(solution)/shard_map/ppermute | solution.py:40
  100.0 14.5 %collective-permute-start.7 = (bf16[512,256]{1,0:T(8,128)(2,1)S(1)}, bf16[512,256]{1,0:T(8,128)(2,1)S(1)}, u32[]{:S(2)}, u32[]{:S(2)}) collective-permute-start(bf16[512,256]{1,0:T(8,128)(2,1)S(1)} %collective-permute-done.6.refs_3_), channel_id=1, source_target_pairs={{0,128},{128,256},{256,384},{384,448},{448,320},{320,192},{192,64}... | collective-permute-start | bytes 786440 | tf_op jit(solution)/shard_map/ppermute | solution.py:40
  127.2 5.5 %collective-permute-start.10 = (bf16[32,8,1152]{2,1,0:T(8,128)(2,1)}, bf16[32,8,1152]{2,1,0:T(8,128)(2,1)S(1)}, u32[]{:S(2)}, u32[]{:S(2)}) collective-permute-start(bf16[32,8,1152]{2,1,0:T(8,128)(2,1)} %get-tuple-element.21), channel_id=1, source_target_pairs={{0,1},{1,0},{2,3},{3,2},{4,5},{5,4},{6,7},{7,6},{8,9},{9,8},{10,11... | collective-permute-start | bytes 1769480 | tf_op jit(solution)/shard_map/ppermute | solution.py:44

commit v4 on v3

--- a/solution.py
+++ b/solution.py
@@ -10,7 +10,16 @@
 NX, NY, NZ, NC = 4, 4, 2, 2
 AXES = ("dp", "x", "y", "zh", "core")
 RING = (0, 2, 4, 6, 7, 5, 3, 1)
-BEFORE = tuple(RING[(RING.index(g) - k) % len(RING)] for g in range(len(RING)) for k in range(len(RING)))
+LAST = len(RING) - 1
+
+
+def place_of(g, other):
+    return g if other == g else len(RING) + (g if other == LAST else other)
+
+
+BEFORE = tuple(
+    place_of(g, RING[(RING.index(g) - k) % len(RING)]) for g in range(len(RING)) for k in range(len(RING))
+)
 TENSOR = ("x", "y", "zh", "core")
 
 
@@ -47,13 +56,13 @@
 def products_kernel(ring, moved, mine, theirs, *refs):
     parts, refs = refs[:-8], refs[-8:]
     near_in, near_weight, far, wide, strips, weights, total, sems = refs
-    chips, _, n_dp, _, columns = moved.shape
-    rows = near_weight.shape[0]
+    chips, _, _, columns = moved.shape
+    n_dp, rows = len(parts), near_weight.shape[0]
     half = n_dp // 2
     blocks = far.shape[0]
 
     arrive = [
-        pltpu.make_async_copy(moved.at[:, 1, ring[k]], strips.at[k], sems.at[k]) for k in range(n_dp)
+        pltpu.make_async_copy(moved.at[:, ring[k]], strips.at[k], sems.at[k]) for k in range(n_dp)
     ]
     for copy in arrive:
         copy.start()
@@ -62,7 +71,7 @@
         cut = pl.ds(h * half * columns, half * columns)
         at = n_dp + 3 * h
         fetch.append([
-            pltpu.make_async_copy(moved.at[:, 0, pl.ds(h * half, half)], wide.at[h], sems.at[at]),
+            pltpu.make_async_copy(moved.at[:, pl.ds(h * half, half)], wide.at[h], sems.at[at]),
             pltpu.make_async_copy(mine.at[:, cut], weights.at[0, h], sems.at[at + 1]),
             pltpu.make_async_copy(theirs.at[:, cut], weights.at[1, h], sems.at[at + 2]),
         ])
@@ -101,8 +110,8 @@
 
 
 def products(ring, moved, weight, weight_other, parts, held):
-    chips, _, n_dp, deep, columns = moved.shape
-    rows = weight.shape[0]
+    chips, _, deep, columns = moved.shape
+    n_dp, rows = len(parts), weight.shape[0]
     blocks = chips * deep // held
     vmem, whole = pl.BlockSpec(memory_space=pltpu.VMEM), pl.BlockSpec(memory_space=pl.ANY)
     return pl.pallas_call(
@@ -159,7 +168,7 @@
 
 def body(attn, grad_out, weight):
     place = jnp.stack([lax.axis_index(a) for a in TENSOR + ("dp",)]).astype(jnp.int32)
-    c = place[3]
+    zh, c, dp = place[2], place[3], place[4]
     n_dp = lax.axis_size("dp")
     rows = attn.shape[1]
     held, width = grad_out.shape
@@ -177,25 +186,29 @@
     strips = jnp.broadcast_to(
         grad_out.reshape(held, n_dp, 1, columns).transpose(1, 2, 0, 3), (n_dp, NZ, held, columns)
     ).reshape(n_dp * deep, columns)
-    sliced = lax.all_to_all(strips, ("dp", "zh"), 0, 0, tiled=True)
+    sliced = lax.all_to_all(strips, ("dp", "zh"), 0, 0, tiled=True).reshape(n_dp, deep, columns)
+    own = lax.broadcasted_iota(jnp.int32, (LAST, 1, 1), 0) == dp
+    others = jnp.where(own, sliced[LAST:], sliced[:LAST]).reshape(LAST * deep, columns)
     both = jnp.concatenate([grad_out, swap(grad_out, "zh")], 0)
     both = both.reshape(deep, n_dp, columns).swapaxes(0, 1).reshape(n_dp * deep, columns)
 
-    both, wide = lax.optimization_barrier((both, wide))
-    moved = spread(jnp.concatenate([both, sliced], 0), True)
     weight_other = swap(weight, "core")
-
-    wide, _ = lax.optimization_barrier((wide, sliced))
-    ahead, back = [wide, turn(wide, 1)], [wide, turn(wide, -1)]
-    moved, ahead[1], back[1] = lax.optimization_barrier((moved, ahead[1], back[1]))
-    moved = spread(moved, False).reshape(NX * NY, 2, n_dp, deep, columns)
-    for _ in range(n_dp // 2 - 1):
+    wide, both = lax.optimization_barrier((wide, both))
+    ahead, back = [wide, turn(wide, 1)], [wide]
+    both, ahead[1] = lax.optimization_barrier((both, ahead[1]))
+    moved = spread(jnp.concatenate([both, others], 0), True)
+    ahead.append(turn(ahead[-1], 1))
+    back.append(turn(wide, -1))
+    moved, ahead[2], back[1] = lax.optimization_barrier((moved, ahead[2], back[1]))
+    moved = spread(moved, False).reshape(NX * NY, n_dp + LAST, deep, columns)
+    for _ in range(n_dp // 2 - 2):
         ahead.append(turn(ahead[-1], 1))
-    for _ in range(n_dp // 2 - 2):
         back.append(turn(back[-1], -1))
-    ring = lax.dynamic_slice_in_dim(jnp.asarray(BEFORE, jnp.int32), place[4] * n_dp, n_dp)
-
-    near_in, near_weight, far = products(ring, moved, weight, weight_other, ahead + back[:0:-1], held)
+    ring = lax.dynamic_slice_in_dim(jnp.asarray(BEFORE, jnp.int32), dp * n_dp, n_dp)
+
+    first = wide.reshape(NC * rows, NX * NY, NZ, held)
+    first = jnp.where(zh == 0, first, first[:, :, ::-1]).reshape(NC * rows, tokens)
+    near_in, near_weight, far = products(ring, moved, weight, weight_other, [first] + ahead[1:] + back[:0:-1], held)
     far = swap(far, "core")
     grad_in, grad_weight = finish(place, near_in, near_weight, far)
     return grad_in.reshape(NC * tokens, rows), grad_weight

time: 135 us -> 133 us (0.985)
  waiting for transfers between devices: 50.9 us -> 45.2 us
  starting transfers between devices: 63 us -> 66 us
    all_to_all x1, waiting for transfers between devices: 13 us -> 0.01 us  [body(): lax.all_to_all(strips, ('dp', 'zh'), 0, 0, tiled=True)]
    all_to_all x2, waiting for transfers between devices: 3.73 us -> 7.98 us  [spread(): lax.all_to_all(copies, TENSOR, 0, 0, axis_index_groups=lines(first), tile...]
    ppermute x7, starting transfers between devices: 22.6 us -> 26.4 us  [turn(): return lax.ppermute(values, 'dp', pairs)]
    ppermute x7, waiting for transfers between devices: 32.5 us -> 35.5 us  [turn(): return lax.ppermute(values, 'dp', pairs)]
  transfers between devices with their start and end apart: 14 -> 14, of which waited for: 10 -> 9; matrix products, arithmetic and copies ran while one was open for 3% -> 3% of each run, Pallas kernels for 0% -> 0%
where the time goes in v4:
time: 133 us; the launch traced here: 132 us
  starting transfers between devices  66 us (50%)
  waiting for transfers between devices  45.2 us (34%)
  Pallas kernels  10.4 us (8%)
  local copies, waits for them, and re-layouts  7.24 us (5%)
  other arithmetic  2.15 us (2%)
    ppermute x7, waiting for transfers between devices, turn(): return lax.ppermute(values, 'dp', pairs)  35.5 us
    ppermute x7, starting transfers between devices, turn(): return lax.ppermute(values, 'dp', pairs)  26.4 us
    ppermute x4, starting transfers between devices, swap(): return lax.ppermute(values, axis, [(0, 1), (1, 0)])  25.1 us
    all_to_all x2, starting transfers between devices, spread(): lax.all_to_all(copies, TENSOR, 0, 0, axis_index_groups=lines(first), tile...  9.69 us
    pallas_call x1, Pallas kernels, products(): pl.pallas_call(products_kernel, out_shape=(jax.ShapeDtypeStruct((blocks,...  8.84 us
    all_to_all x2, waiting for transfers between devices, spread(): lax.all_to_all(copies, TENSOR, 0, 0, axis_index_groups=lines(first), tile...  7.98 us
    all_to_all x1, starting transfers between devices, body(): lax.all_to_all(strips, ('dp', 'zh'), 0, 0, tiled=True)  4.85 us
    broadcast_in_dim x2, local copies, waits for them, and re-layouts, spread(): jnp.broadcast_to(values[None], (NX,) + values.shape)  4.77 us
  transfers between devices with their start and end apart: 14, of which 9 were waited for; matrix products, arithmetic and copies ran while one was open for 3% of the time, Pallas kernels for 0%

profile of v4, /device:TPU:1, one launch (start us, length us, event | category | flops | bytes accessed | tf_op | source)
XLA Modules:
  0.0 131.9 jit_solution(15601094718707063425)
XLA Ops:
  0.6 16.3 %collective-permute-start.1 = (bf16[8,7168]{1,0:T(8,128)(2,1)}, bf16[8,7168]{1,0:T(8,128)(2,1)S(1)}, u32[]{:S(2)}, u32[]{:S(2)}) collective-permute-start(bf16[8,7168]{1,0:T(8,128)(2,1)} %param.5), channel_id=1, source_target_pairs={{0,2},{2,0},{1,3},{3,1},{4,6},{6,4},{5,7},{7,5},{8,10},{10,8},{9,1... | collective-permute-start | bytes 344072 | tf_op jit(solution)/shard_map/ppermute | solution.py:53
  16.9 1.6 %broadcast_in_dim.47 = bf16[8,2,8,896]{3,2,1,0:T(8,128)(2,1)} broadcast(bf16[8,8,896]{2,1,0:T(8,128)(2,1)} %bitcast.57), dimensions={0,2,3} | broadcast | bytes 344064 | tf_op jit(solution)/shard_map/broadcast_in_dim | solution.py:186
  18.5 4.8 %all-to-all-start = ((bf16[16,8,896]{2,1,0:T(8,128)(2,1)}), bf16[16,8,896]{2,1,0:T(8,128)(2,1)S(1)}, u32[]{:S(2)}, u32[]{:S(2)}) async-start(bf16[16,8,896]{2,1,0:T(8,128)(2,1)} %bitcast.19), calls=%async_computation | async-start | bytes 458752 | tf_op jit(solution)/shard_map/all_to_all | solution.py:189
  23.4 1.0 broadcast_select_fusion.1
  24.5 3.1 %collective-permute-start = (bf16[256,256]{1,0:T(8,128)(2,1)S(1)}, bf16[256,256]{1,0:T(8,128)(2,1)S(1)}, u32[]{:S(2)}, u32[]{:S(2)}) collective-permute-start(bf16[256,256]{1,0:T(8,128)(2,1)S(1)} %bitcast.59), channel_id=1, source_target_pairs={{0,1},{1,0},{2,3},{3,2},{4,5},{5,4},{6,7},{7,6},{8,9},{9,8},{10,11... | collective-permute-start | bytes 393224 | tf_op jit(solution)/shard_map/ppermute | solution.py:53
  27.8 0.9 pad_maximum_fusion.2
  28.8 4.4 %collective-permute-start.2 = (bf16[512,256]{1,0:T(8,128)(2,1)S(1)}, bf16[512,256]{1,0:T(8,128)(2,1)S(1)}, u32[]{:S(2)}, u32[]{:S(2)}) collective-permute-start(bf16[512,256]{1,0:T(8,128)(2,1)S(1)} %pad_maximum_fusion.1), channel_id=1, source_target_pairs={{0,128},{128,256},{256,384},{384,448},{448,320},{320,192},{192,64}... | collective-permute-start | bytes 786440 | tf_op jit(solution)/shard_map/ppermute | solution.py:49
  33.4 10.4 %collective-permute-done.2.refs_1_ = bf16[512,256]{1,0:T(8,128)(2,1)S(1)} collective-permute-done((bf16[512,256]{1,0:T(8,128)(2,1)S(1)}, bf16[512,256]{1,0:T(8,128)(2,1)S(1)}, u32[]{:S(2)}, u32[]{:S(2)}) %collective-permute-start.2) | collective-permute-done | bytes 262176 | tf_op jit(solution)/shard_map/ppermute | solution.py:49
  43.9 0.1 fusion
  44.0 1.4 %broadcast_in_dim.51 = bf16[4,240,896]{2,1,0:T(8,128)(2,1)} broadcast(bf16[240,896]{1,0:T(8,128)(2,1)S(1)} %pad_maximum_fusion), dimensions={1,2} | broadcast | bytes 2150400 | tf_op jit(solution)/shard_map/broadcast_in_dim | solution.py:43
  45.4 4.2 %all-to-all-start.1 = ((bf16[4,240,896]{2,1,0:T(8,128)(2,1)}), bf16[4,240,896]{2,1,0:T(8,128)(2,1)S(1)}, u32[]{:S(2)}, u32[]{:S(2)}) async-start(bf16[4,240,896]{2,1,0:T(8,128)(2,1)} %broadcast_in_dim.51), calls=%async_computation.1 | async-start | bytes 3440640 | tf_op jit(solution)/shard_map/all_to_all | solution.py:44
  49.6 2.4 %collective-permute-start.4 = (bf16[512,256]{1,0:T(8,128)(2,1)S(1)}, bf16[512,256]{1,0:T(8,128)(2,1)S(1)}, u32[]{:S(2)}, u32[]{:S(2)}) collective-permute-start(bf16[512,256]{1,0:T(8,128)(2,1)S(1)} %pad_maximum_fusion.1), channel_id=1, source_target_pairs={{0,64},{128,0},{256,128},{384,256},{448,384},{320,448},{192,320},{... | collective-permute-start | bytes 786440 | tf_op jit(solution)/shard_map/ppermute | solution.py:49
  51.9 3.8 %collective-permute-start.3 = (bf16[512,256]{1,0:T(8,128)(2,1)S(1)}, bf16[512,256]{1,0:T(8,128)(2,1)S(1)}, u32[]{:S(2)}, u32[]{:S(2)}) collective-permute-start(bf16[512,256]{1,0:T(8,128)(2,1)S(1)} %collective-permute-done.2.refs_1_), channel_id=1, source_target_pairs={{0,128},{128,256},{256,384},{384,448},{448,320},{320,192},{192,64}... | collective-permute-start | bytes 786440 | tf_op jit(solution)/shard_map/ppermute | solution.py:49
  55.8 3.4 %collective-permute-done.4.refs_7_ = bf16[512,256]{1,0:T(8,128)(2,1)S(1)} collective-permute-done((bf16[512,256]{1,0:T(8,128)(2,1)S(1)}, bf16[512,256]{1,0:T(8,128)(2,1)S(1)}, u32[]{:S(2)}, u32[]{:S(2)}) %collective-permute-start.4) | collective-permute-done | bytes 262176 | tf_op jit(solution)/shard_map/ppermute | solution.py:49
  59.2 7.0 %collective-permute-done.3.refs_2_ = bf16[512,256]{1,0:T(8,128)(2,1)S(1)} collective-permute-done((bf16[512,256]{1,0:T(8,128)(2,1)S(1)}, bf16[512,256]{1,0:T(8,128)(2,1)S(1)}, u32[]{:S(2)}, u32[]{:S(2)}) %collective-permute-start.3) | collective-permute-done | bytes 262176 | tf_op jit(solution)/shard_map/ppermute | solution.py:49
  66.2 3.4 %broadcast_in_dim.52 = bf16[4,960,896]{2,1,0:T(8,128)(2,1)} broadcast(bf16[960,896]{1,0:T(8,128)(2,1)S(1)} %bitcast.48), dimensions={1,2} | broadcast | bytes 8601600 | tf_op jit(solution)/shard_map/broadcast_in_dim | solution.py:43
  69.6 5.5 %all-to-all-start.2 = ((bf16[4,960,896]{2,1,0:T(8,128)(2,1)}), bf16[4,960,896]{2,1,0:T(8,128)(2,1)}, u32[]{:S(2)}, u32[]{:S(2)}) async-start(bf16[4,960,896]{2,1,0:T(8,128)(2,1)} %broadcast_in_dim.52), calls=%async_computation.2 | async-start | bytes 13762560 | tf_op jit(solution)/shard_map/all_to_all | solution.py:44
  75.1 2.4 %collective-permute-start.5 = (bf16[256,7168]{1,0:T(8,128)(2,1)}, bf16[256,7168]{1,0:T(8,128)(2,1)}, u32[]{:S(2)}, u32[]{:S(2)}) collective-permute-start(bf16[256,7168]{1,0:T(8,128)(2,1)} %mine.1), channel_id=1, source_target_pairs={{0,1},{1,0},{2,3},{3,2},{4,5},{5,4},{6,7},{7,6},{8,9},{9,8},{10,11... | collective-permute-start | bytes 11010056 | tf_op jit(solution)/shard_map/ppermute | solution.py:53
  77.5 2.5 %collective-permute-start.6 = (bf16[512,256]{1,0:T(8,128)(2,1)S(1)}, bf16[512,256]{1,0:T(8,128)(2,1)S(1)}, u32[]{:S(2)}, u32[]{:S(2)}) collective-permute-start(bf16[512,256]{1,0:T(8,128)(2,1)S(1)} %collective-permute-done.3.refs_2_), channel_id=1, source_target_pairs={{0,128},{128,256},{256,384},{384,448},{448,320},{320,192},{192,64}... | collective-permute-start | bytes 786440 | tf_op jit(solution)/shard_map/ppermute | solution.py:49
  80.0 3.7 %collective-permute-start.8 = (bf16[512,256]{1,0:T(8,128)(2,1)S(1)}, bf16[512,256]{1,0:T(8,128)(2,1)S(1)}, u32[]{:S(2)}, u32[]{:S(2)}) collective-permute-start(bf16[512,256]{1,0:T(8,128)(2,1)S(1)} %collective-permute-done.4.refs_7_), channel_id=1, source_target_pairs={{0,64},{128,0},{256,128},{384,256},{448,384},{320,448},{192,320},{... | collective-permute-start | bytes 786440 | tf_op jit(solution)/shard_map/ppermute | solution.py:49
  83.7 4.9 %collective-permute-done.6.refs_3_ = bf16[512,256]{1,0:T(8,128)(2,1)S(1)} collective-permute-done((bf16[512,256]{1,0:T(8,128)(2,1)S(1)}, bf16[512,256]{1,0:T(8,128)(2,1)S(1)}, u32[]{:S(2)}, u32[]{:S(2)}) %collective-permute-start.6) | collective-permute-done | bytes 262176 | tf_op jit(solution)/shard_map/ppermute | solution.py:49
  88.6 7.7 %collective-permute-start.7 = (bf16[512,256]{1,0:T(8,128)(2,1)S(1)}, bf16[512,256]{1,0:T(8,128)(2,1)S(1)}, u32[]{:S(2)}, u32[]{:S(2)}) collective-permute-start(bf16[512,256]{1,0:T(8,128)(2,1)S(1)} %collective-permute-done.6.refs_3_), channel_id=1, source_target_pairs={{0,128},{128,256},{256,384},{384,448},{448,320},{320,192},{192,64}... | collective-permute-start | bytes 786440 | tf_op jit(solution)/shard_map/ppermute | solution.py:49
  96.5 1.9 %collective-permute-start.9 = (bf16[512,256]{1,0:T(8,128)(2,1)S(1)}, bf16[512,256]{1,0:T(8,128)(2,1)S(1)}, u32[]{:S(2)}, u32[]{:S(2)}) collective-permute-start(bf16[512,256]{1,0:T(8,128)(2,1)S(1)} %collective-permute-done.8.refs_6_), channel_id=1, source_target_pairs={{0,64},{128,0},{256,128},{384,256},{448,384},{320,448},{192,320},{... | collective-permute-start | bytes 786440 | tf_op jit(solution)/shard_map/ppermute | solution.py:49
  98.5 0.1 copy.17
  98.7 0.1 copy.18.refs_0_
  98.8 3.1 %collective-permute-done.7.refs_4_ = bf16[512,256]{1,0:T(8,128)(2,1)S(1)} collective-permute-done((bf16[512,256]{1,0:T(8,128)(2,1)S(1)}, bf16[512,256]{1,0:T(8,128)(2,1)S(1)}, u32[]{:S(2)}, u32[]{:S(2)}) %collective-permute-start.7) | collective-permute-done | bytes 262176 | tf_op jit(solution)/shard_map/ppermute | solution.py:49
  102.0 6.5 %collective-permute-done.9.refs_5_ = bf16[512,256]{1,0:T(8,128)(2,1)S(1)} collective-permute-done((bf16[512,256]{1,0:T(8,128)(2,1)S(1)}, bf16[512,256]{1,0:T(8,128)(2,1)S(1)}, u32[]{:S(2)}, u32[]{:S(2)}) %collective-permute-start.9) | collective-permute-done | bytes 262176 | tf_op jit(solution)/shard_map/ppermute | solution.py:49
  108.5 8.0 %all-to-all-done.2 = bf16[4,960,896]{2,1,0:T(8,128)(2,1)} async-done(((bf16[4,960,896]{2,1,0:T(8,128)(2,1)}), bf16[4,960,896]{2,1,0:T(8,128)(2,1)}, u32[]{:S(2)}, u32[]{:S(2)}) %all-to-all-start.2) | async-done | bytes 6881312 | tf_op jit(solution)/shard_map/all_to_all | solution.py:44
  116.5 8.8 %shard_map.59 = (bf16[32,8,256]{2,1,0:T(8,128)(2,1)S(1)}, f32[256,896]{1,0:T(8,128)S(1)}, bf16[32,8,1152]{2,1,0:T(8,128)(2,1)}) custom-call(s32[8]{0:T(128)S(1)} %dynamic_slice.3.ring, bf16[16,15,16,896]{3,2,1,0:T(8,128)(2,1)} %bitcast.24.moved, bf16[256,7168]{1,0:T(8,128)(2,1)} %mine.1, bf16[256,7168]{1,0:T(8,128)(2,1)} %collective-permute-done.5.theirs, ...), custom_call_target="tpu_custom_call" | custom-call | flops 3758096384 | bytes 17825792 | tf_op jit(solution)/shard_map/pallas_call | solution.py:117
  125.3 3.3 %collective-permute-start.10 = (bf16[32,8,1152]{2,1,0:T(8,128)(2,1)}, bf16[32,8,1152]{2,1,0:T(8,128)(2,1)S(1)}, u32[]{:S(2)}, u32[]{:S(2)}) collective-permute-start(bf16[32,8,1152]{2,1,0:T(8,128)(2,1)} %get-tuple-element.23), channel_id=1, source_target_pairs={{0,1},{1,0},{2,3},{3,2},{4,5},{5,4},{6,7},{7,6},{8,9},{9,8},{10,11... | collective-permute-start | bytes 1769480 | tf_op jit(solution)/shard_map/ppermute | solution.py:53
  128.7 1.7 %collective-permute-done.10.far = bf16[32,8,1152]{2,1,0:T(8,128)(2,1)S(1)} collective-permute-done((bf16[32,8,1152]{2,1,0:T(8,128)(2,1)}, bf16[32,8,1152]{2,1,0:T(8,128)(2,1)S(1)}, u32[]{:S(2)}, u32[]{:S(2)}) %collective-permute-start.10) | collective-permute-done | bytes 589856 | tf_op jit(solution)/shard_map/ppermute | solution.py:53
  130.4 1.5 %shard_map.60 = (bf16[64,8,256]{2,1,0:T(8,128)(2,1)}, bf16[256,896]{1,0:T(8,128)(2,1)}) custom-call(s32[5]{0:T(128)S(1)} %stack.23.place, bf16[32,8,256]{2,1,0:T(8,128)(2,1)S(1)} %get-tuple-element.21.near_in, f32[256,896]{1,0:T(8,128)S(1)} %get-tuple-element.22.near_weight, bf16[32,8,1152]{2,1,0:T(8,128)(2,1)S(1)} %collective-permute-done.10.far), custom_call_target="tpu_custom_call" | custom-call | tf_op jit(solution)/shard_map/pallas_call | solution.py:157
  (21 shorter events, 0.8 us)
Async XLA Ops:
  0.6 27.1 %collective-permute-start.1 = (bf16[8,7168]{1,0:T(8,128)(2,1)}, bf16[8,7168]{1,0:T(8,128)(2,1)S(1)}, u32[]{:S(2)}, u32[]{:S(2)}) collective-permute-start(bf16[8,7168]{1,0:T(8,128)(2,1)} %param.5), channel_id=1, source_target_pairs={{0,2},{2,0},{1,3},{3,1},{4,6},{6,4},{5,7},{7,5},{8,10},{10,8},{9,1... | collective-permute-start | bytes 344072 | tf_op jit(solution)/shard_map/ppermute | solution.py:53
  18.5 25.3 %all-to-all-start = ((bf16[16,8,896]{2,1,0:T(8,128)(2,1)}), bf16[16,8,896]{2,1,0:T(8,128)(2,1)S(1)}, u32[]{:S(2)}, u32[]{:S(2)}) async-start(bf16[16,8,896]{2,1,0:T(8,128)(2,1)} %bitcast.19), calls=%async_computation | async-start | bytes 458752 | tf_op jit(solution)/shard_map/all_to_all | solution.py:189
  24.5 4.3 %collective-permute-start = (bf16[256,256]{1,0:T(8,128)(2,1)S(1)}, bf16[256,256]{1,0:T(8,128)(2,1)S(1)}, u32[]{:S(2)}, u32[]{:S(2)}) collective-permute-start(bf16[256,256]{1,0:T(8,128)(2,1)S(1)} %bitcast.59), channel_id=1, source_target_pairs={{0,1},{1,0},{2,3},{3,2},{4,5},{5,4},{6,7},{7,6},{8,9},{9,8},{10,11... | collective-permute-start | bytes 393224 | tf_op jit(solution)/shard_map/ppermute | solution.py:53
  28.8 15.1 %collective-permute-start.2 = (bf16[512,256]{1,0:T(8,128)(2,1)S(1)}, bf16[512,256]{1,0:T(8,128)(2,1)S(1)}, u32[]{:S(2)}, u32[]{:S(2)}) collective-permute-start(bf16[512,256]{1,0:T(8,128)(2,1)S(1)} %pad_maximum_fusion.1), channel_id=1, source_target_pairs={{0,128},{128,256},{256,384},{384,448},{448,320},{320,192},{192,64}... | collective-permute-start | bytes 786440 | tf_op jit(solution)/shard_map/ppermute | solution.py:49
  45.4 20.8 %all-to-all-start.1 = ((bf16[4,240,896]{2,1,0:T(8,128)(2,1)}), bf16[4,240,896]{2,1,0:T(8,128)(2,1)S(1)}, u32[]{:S(2)}, u32[]{:S(2)}) async-start(bf16[4,240,896]{2,1,0:T(8,128)(2,1)} %broadcast_in_dim.51), calls=%async_computation.1 | async-start | bytes 3440640 | tf_op jit(solution)/shard_map/all_to_all | solution.py:44
  49.6 9.6 %collective-permute-start.4 = (bf16[512,256]{1,0:T(8,128)(2,1)S(1)}, bf16[512,256]{1,0:T(8,128)(2,1)S(1)}, u32[]{:S(2)}, u32[]{:S(2)}) collective-permute-start(bf16[512,256]{1,0:T(8,128)(2,1)S(1)} %pad_maximum_fusion.1), channel_id=1, source_target_pairs={{0,64},{128,0},{256,128},{384,256},{448,384},{320,448},{192,320},{... | collective-permute-start | bytes 786440 | tf_op jit(solution)/shard_map/ppermute | solution.py:49
  51.9 14.3 %collective-permute-start.3 = (bf16[512,256]{1,0:T(8,128)(2,1)S(1)}, bf16[512,256]{1,0:T(8,128)(2,1)S(1)}, u32[]{:S(2)}, u32[]{:S(2)}) collective-permute-start(bf16[512,256]{1,0:T(8,128)(2,1)S(1)} %collective-permute-done.2.refs_1_), channel_id=1, source_target_pairs={{0,128},{128,256},{256,384},{384,448},{448,320},{320,192},{192,64}... | collective-permute-start | bytes 786440 | tf_op jit(solution)/shard_map/ppermute | solution.py:49
  69.6 28.8 %copy-start = (s32[64]{0:T(128)S(1)}, s32[64]{0:T(128)}, u32[]{:S(2)}) copy-start(s32[64]{0:T(128)} %constant.29.clone) | copy-start | bytes 772
  69.6 46.9 %all-to-all-start.2 = ((bf16[4,960,896]{2,1,0:T(8,128)(2,1)}), bf16[4,960,896]{2,1,0:T(8,128)(2,1)}, u32[]{:S(2)}, u32[]{:S(2)}) async-start(bf16[4,960,896]{2,1,0:T(8,128)(2,1)} %broadcast_in_dim.52), calls=%async_computation.2 | async-start | bytes 13762560 | tf_op jit(solution)/shard_map/all_to_all | solution.py:44
  75.1 33.4 %collective-permute-start.5 = (bf16[256,7168]{1,0:T(8,128)(2,1)}, bf16[256,7168]{1,0:T(8,128)(2,1)}, u32[]{:S(2)}, u32[]{:S(2)}) collective-permute-start(bf16[256,7168]{1,0:T(8,128)(2,1)} %mine.1), channel_id=1, source_target_pairs={{0,1},{1,0},{2,3},{3,2},{4,5},{5,4},{6,7},{7,6},{8,9},{9,8},{10,11... | collective-permute-start | bytes 11010056 | tf_op jit(solution)/shard_map/ppermute | solution.py:53
  77.5 11.1 %collective-permute-start.6 = (bf16[512,256]{1,0:T(8,128)(2,1)S(1)}, bf16[512,256]{1,0:T(8,128)(2,1)S(1)}, u32[]{:S(2)}, u32[]{:S(2)}) collective-permute-start(bf16[512,256]{1,0:T(8,128)(2,1)S(1)} %collective-permute-done.3.refs_2_), channel_id=1, source_target_pairs={{0,128},{128,256},{256,384},{384,448},{448,320},{320,192},{192,64}... | collective-permute-start | bytes 786440 | tf_op jit(solution)/shard_map/ppermute | solution.py:49
  80.0 16.4 %collective-permute-start.8 = (bf16[512,256]{1,0:T(8,128)(2,1)S(1)}, bf16[512,256]{1,0:T(8,128)(2,1)S(1)}, u32[]{:S(2)}, u32[]{:S(2)}) collective-permute-start(bf16[512,256]{1,0:T(8,128)(2,1)S(1)} %collective-permute-done.4.refs_7_), channel_id=1, source_target_pairs={{0,64},{128,0},{256,128},{384,256},{448,384},{320,448},{192,320},{... | collective-permute-start | bytes 786440 | tf_op jit(solution)/shard_map/ppermute | solution.py:49
  88.6 13.3 %collective-permute-start.7 = (bf16[512,256]{1,0:T(8,128)(2,1)S(1)}, bf16[512,256]{1,0:T(8,128)(2,1)S(1)}, u32[]{:S(2)}, u32[]{:S(2)}) collective-permute-start(bf16[512,256]{1,0:T(8,128)(2,1)S(1)} %collective-permute-done.6.refs_3_), channel_id=1, source_target_pairs={{0,128},{128,256},{256,384},{384,448},{448,320},{320,192},{192,64}... | collective-permute-start | bytes 786440 | tf_op jit(solution)/shard_map/ppermute | solution.py:49
  96.5 12.0 %collective-permute-start.9 = (bf16[512,256]{1,0:T(8,128)(2,1)S(1)}, bf16[512,256]{1,0:T(8,128)(2,1)S(1)}, u32[]{:S(2)}, u32[]{:S(2)}) collective-permute-start(bf16[512,256]{1,0:T(8,128)(2,1)S(1)} %collective-permute-done.8.refs_6_), channel_id=1, source_target_pairs={{0,64},{128,0},{256,128},{384,256},{448,384},{320,448},{192,320},{... | collective-permute-start | bytes 786440 | tf_op jit(solution)/shard_map/ppermute | solution.py:49
  125.3 5.1 %collective-permute-start.10 = (bf16[32,8,1152]{2,1,0:T(8,128)(2,1)}, bf16[32,8,1152]{2,1,0:T(8,128)(2,1)S(1)}, u32[]{:S(2)}, u32[]{:S(2)}) collective-permute-start(bf16[32,8,1152]{2,1,0:T(8,128)(2,1)} %get-tuple-element.23), channel_id=1, source_target_pairs={{0,1},{1,0},{2,3},{3,2},{4,5},{5,4},{6,7},{7,6},{8,9},{9,8},{10,11... | collective-permute-start | bytes 1769480 | tf_op jit(solution)/shard_map/ppermute | solution.py:53

commit v5 on v4

--- a/solution.py
+++ b/solution.py
@@ -197,12 +197,15 @@
     ahead, back = [wide, turn(wide, 1)], [wide]
     both, ahead[1] = lax.optimization_barrier((both, ahead[1]))
     moved = spread(jnp.concatenate([both, others], 0), True)
+    back.append(turn(wide, -1))
+    moved, back[1] = lax.optimization_barrier((moved, back[1]))
+    moved = spread(moved, False).reshape(NX * NY, n_dp + LAST, deep, columns)
     ahead.append(turn(ahead[-1], 1))
-    back.append(turn(wide, -1))
-    moved, ahead[2], back[1] = lax.optimization_barrier((moved, ahead[2], back[1]))
-    moved = spread(moved, False).reshape(NX * NY, n_dp + LAST, deep, columns)
+    back.append(turn(back[-1], -1))
+    ahead[2], back[2] = lax.optimization_barrier((ahead[2], back[2]))
     for _ in range(n_dp // 2 - 2):
         ahead.append(turn(ahead[-1], 1))
+    for _ in range(n_dp // 2 - 3):
         back.append(turn(back[-1], -1))
     ring = lax.dynamic_slice_in_dim(jnp.asarray(BEFORE, jnp.int32), dp * n_dp, n_dp)
 

time: 133 us -> 131 us (0.985)
  waiting for transfers between devices: 45.2 us -> 43.1 us
    all_to_all x2, waiting for transfers between devices: 7.98 us -> 4.07 us  [spread(): lax.all_to_all(copies, TENSOR, 0, 0, axis_index_groups=lines(first), tile...]
    ppermute x4, starting transfers between devices: 25.1 us -> 27.6 us  [swap(): return lax.ppermute(values, axis, [(0, 1), (1, 0)])]
    ppermute x7, starting transfers between devices: 26.4 us -> 24.5 us  [turn(): return lax.ppermute(values, 'dp', pairs)]
    ppermute x7, waiting for transfers between devices: 35.5 us -> 37.3 us  [turn(): return lax.ppermute(values, 'dp', pairs)]
where the time goes in v5:
time: 131 us; the launch traced here: 130 us
  starting transfers between devices  66.6 us (51%)
  waiting for transfers between devices  43.1 us (33%)
  Pallas kernels  10.4 us (8%)
  local copies, waits for them, and re-layouts  7.24 us (6%)
  other arithmetic  2.15 us (2%)
    ppermute x7, waiting for transfers between devices, turn(): return lax.ppermute(values, 'dp', pairs)  37.3 us
    ppermute x4, starting transfers between devices, swap(): return lax.ppermute(values, axis, [(0, 1), (1, 0)])  27.6 us
    ppermute x7, starting transfers between devices, turn(): return lax.ppermute(values, 'dp', pairs)  24.5 us
    all_to_all x2, starting transfers between devices, spread(): lax.all_to_all(copies, TENSOR, 0, 0, axis_index_groups=lines(first), tile...  9.69 us
    pallas_call x1, Pallas kernels, products(): pl.pallas_call(products_kernel, out_shape=(jax.ShapeDtypeStruct((blocks,...  8.84 us
    all_to_all x1, starting transfers between devices, body(): lax.all_to_all(strips, ('dp', 'zh'), 0, 0, tiled=True)  4.85 us
    broadcast_in_dim x2, local copies, waits for them, and re-layouts, spread(): jnp.broadcast_to(values[None], (NX,) + values.shape)  4.77 us
    all_to_all x2, waiting for transfers between devices, spread(): lax.all_to_all(copies, TENSOR, 0, 0, axis_index_groups=lines(first), tile...  4.07 us
  transfers between devices with their start and end apart: 14, of which 9 were waited for; matrix products, arithmetic and copies ran while one was open for 3% of the time, Pallas kernels for 0%

profile of v5, /device:TPU:1, one launch (start us, length us, event | category | flops | bytes accessed | tf_op | source)
XLA Modules:
  0.0 130.3 jit_solution(1395481398904716161)
XLA Ops:
  0.6 16.3 %collective-permute-start.1 = (bf16[8,7168]{1,0:T(8,128)(2,1)}, bf16[8,7168]{1,0:T(8,128)(2,1)S(1)}, u32[]{:S(2)}, u32[]{:S(2)}) collective-permute-start(bf16[8,7168]{1,0:T(8,128)(2,1)} %param.5), channel_id=1, source_target_pairs={{0,2},{2,0},{1,3},{3,1},{4,6},{6,4},{5,7},{7,5},{8,10},{10,8},{9,1... | collective-permute-start | bytes 344072 | tf_op jit(solution)/shard_map/ppermute | solution.py:53
  16.9 1.6 %broadcast_in_dim.47 = bf16[8,2,8,896]{3,2,1,0:T(8,128)(2,1)} broadcast(bf16[8,8,896]{2,1,0:T(8,128)(2,1)} %bitcast.57), dimensions={0,2,3} | broadcast | bytes 344064 | tf_op jit(solution)/shard_map/broadcast_in_dim | solution.py:186
  18.5 4.8 %all-to-all-start = ((bf16[16,8,896]{2,1,0:T(8,128)(2,1)}), bf16[16,8,896]{2,1,0:T(8,128)(2,1)S(1)}, u32[]{:S(2)}, u32[]{:S(2)}) async-start(bf16[16,8,896]{2,1,0:T(8,128)(2,1)} %bitcast.19), calls=%async_computation | async-start | bytes 458752 | tf_op jit(solution)/shard_map/all_to_all | solution.py:189
  23.4 1.0 broadcast_select_fusion.1
  24.5 3.1 %collective-permute-start = (bf16[256,256]{1,0:T(8,128)(2,1)S(1)}, bf16[256,256]{1,0:T(8,128)(2,1)S(1)}, u32[]{:S(2)}, u32[]{:S(2)}) collective-permute-start(bf16[256,256]{1,0:T(8,128)(2,1)S(1)} %bitcast.59), channel_id=1, source_target_pairs={{0,1},{1,0},{2,3},{3,2},{4,5},{5,4},{6,7},{7,6},{8,9},{9,8},{10,11... | collective-permute-start | bytes 393224 | tf_op jit(solution)/shard_map/ppermute | solution.py:53
  27.8 0.9 pad_maximum_fusion.2
  28.8 4.4 %collective-permute-start.2 = (bf16[512,256]{1,0:T(8,128)(2,1)S(1)}, bf16[512,256]{1,0:T(8,128)(2,1)S(1)}, u32[]{:S(2)}, u32[]{:S(2)}) collective-permute-start(bf16[512,256]{1,0:T(8,128)(2,1)S(1)} %pad_maximum_fusion.1), channel_id=1, source_target_pairs={{0,128},{128,256},{256,384},{384,448},{448,320},{320,192},{192,64}... | collective-permute-start | bytes 786440 | tf_op jit(solution)/shard_map/ppermute | solution.py:49
  33.4 10.4 %collective-permute-done.2.refs_1_ = bf16[512,256]{1,0:T(8,128)(2,1)S(1)} collective-permute-done((bf16[512,256]{1,0:T(8,128)(2,1)S(1)}, bf16[512,256]{1,0:T(8,128)(2,1)S(1)}, u32[]{:S(2)}, u32[]{:S(2)}) %collective-permute-start.2) | collective-permute-done | bytes 262176 | tf_op jit(solution)/shard_map/ppermute | solution.py:49
  43.9 0.1 fusion
  44.0 1.4 %broadcast_in_dim.51 = bf16[4,240,896]{2,1,0:T(8,128)(2,1)} broadcast(bf16[240,896]{1,0:T(8,128)(2,1)S(1)} %pad_maximum_fusion), dimensions={1,2} | broadcast | bytes 2150400 | tf_op jit(solution)/shard_map/broadcast_in_dim | solution.py:43
  45.4 4.2 %all-to-all-start.1 = ((bf16[4,240,896]{2,1,0:T(8,128)(2,1)}), bf16[4,240,896]{2,1,0:T(8,128)(2,1)S(1)}, u32[]{:S(2)}, u32[]{:S(2)}) async-start(bf16[4,240,896]{2,1,0:T(8,128)(2,1)} %broadcast_in_dim.51), calls=%async_computation.1 | async-start | bytes 3440640 | tf_op jit(solution)/shard_map/all_to_all | solution.py:44
  49.6 2.4 %collective-permute-start.3 = (bf16[512,256]{1,0:T(8,128)(2,1)S(1)}, bf16[512,256]{1,0:T(8,128)(2,1)S(1)}, u32[]{:S(2)}, u32[]{:S(2)}) collective-permute-start(bf16[512,256]{1,0:T(8,128)(2,1)S(1)} %pad_maximum_fusion.1), channel_id=1, source_target_pairs={{0,64},{128,0},{256,128},{384,256},{448,384},{320,448},{192,320},{... | collective-permute-start | bytes 786440 | tf_op jit(solution)/shard_map/ppermute | solution.py:49
  51.9 7.2 %collective-permute-done.3.refs_7_ = bf16[512,256]{1,0:T(8,128)(2,1)S(1)} collective-permute-done((bf16[512,256]{1,0:T(8,128)(2,1)S(1)}, bf16[512,256]{1,0:T(8,128)(2,1)S(1)}, u32[]{:S(2)}, u32[]{:S(2)}) %collective-permute-start.3) | collective-permute-done | bytes 262176 | tf_op jit(solution)/shard_map/ppermute | solution.py:49
  59.1 4.1 %all-to-all-done.1 = bf16[4,240,896]{2,1,0:T(8,128)(2,1)S(1)} async-done(((bf16[4,240,896]{2,1,0:T(8,128)(2,1)}), bf16[4,240,896]{2,1,0:T(8,128)(2,1)S(1)}, u32[]{:S(2)}, u32[]{:S(2)}) %all-to-all-start.1) | async-done | bytes 1720352 | tf_op jit(solution)/shard_map/all_to_all | solution.py:44
  63.2 3.4 %broadcast_in_dim.52 = bf16[4,960,896]{2,1,0:T(8,128)(2,1)} broadcast(bf16[960,896]{1,0:T(8,128)(2,1)S(1)} %bitcast.48), dimensions={1,2} | broadcast | bytes 8601600 | tf_op jit(solution)/shard_map/broadcast_in_dim | solution.py:43
  66.6 5.5 %all-to-all-start.2 = ((bf16[4,960,896]{2,1,0:T(8,128)(2,1)}), bf16[4,960,896]{2,1,0:T(8,128)(2,1)}, u32[]{:S(2)}, u32[]{:S(2)}) async-start(bf16[4,960,896]{2,1,0:T(8,128)(2,1)} %broadcast_in_dim.52), calls=%async_computation.2 | async-start | bytes 13762560 | tf_op jit(solution)/shard_map/all_to_all | solution.py:44
  72.1 3.8 %collective-permute-start.4 = (bf16[256,7168]{1,0:T(8,128)(2,1)}, bf16[256,7168]{1,0:T(8,128)(2,1)}, u32[]{:S(2)}, u32[]{:S(2)}) collective-permute-start(bf16[256,7168]{1,0:T(8,128)(2,1)} %mine.1), channel_id=1, source_target_pairs={{0,1},{1,0},{2,3},{3,2},{4,5},{5,4},{6,7},{7,6},{8,9},{9,8},{10,11... | collective-permute-start | bytes 11010056 | tf_op jit(solution)/shard_map/ppermute | solution.py:53
  75.9 3.1 %collective-permute-start.5 = (bf16[512,256]{1,0:T(8,128)(2,1)S(1)}, bf16[512,256]{1,0:T(8,128)(2,1)S(1)}, u32[]{:S(2)}, u32[]{:S(2)}) collective-permute-start(bf16[512,256]{1,0:T(8,128)(2,1)S(1)} %collective-permute-done.2.refs_1_), channel_id=1, source_target_pairs={{0,128},{128,256},{256,384},{384,448},{448,320},{320,192},{192,64}... | collective-permute-start | bytes 786440 | tf_op jit(solution)/shard_map/ppermute | solution.py:49
  79.0 2.2 %collective-permute-start.6 = (bf16[512,256]{1,0:T(8,128)(2,1)S(1)}, bf16[512,256]{1,0:T(8,128)(2,1)S(1)}, u32[]{:S(2)}, u32[]{:S(2)}) collective-permute-start(bf16[512,256]{1,0:T(8,128)(2,1)S(1)} %collective-permute-done.3.refs_7_), channel_id=1, source_target_pairs={{0,64},{128,0},{256,128},{384,256},{448,384},{320,448},{192,320},{... | collective-permute-start | bytes 786440 | tf_op jit(solution)/shard_map/ppermute | solution.py:49
  81.2 4.7 %collective-permute-done.5.refs_2_ = bf16[512,256]{1,0:T(8,128)(2,1)S(1)} collective-permute-done((bf16[512,256]{1,0:T(8,128)(2,1)S(1)}, bf16[512,256]{1,0:T(8,128)(2,1)S(1)}, u32[]{:S(2)}, u32[]{:S(2)}) %collective-permute-start.5) | collective-permute-done | bytes 262176 | tf_op jit(solution)/shard_map/ppermute | solution.py:49
  85.9 6.8 %collective-permute-done.6.refs_6_ = bf16[512,256]{1,0:T(8,128)(2,1)S(1)} collective-permute-done((bf16[512,256]{1,0:T(8,128)(2,1)S(1)}, bf16[512,256]{1,0:T(8,128)(2,1)S(1)}, u32[]{:S(2)}, u32[]{:S(2)}) %collective-permute-start.6) | collective-permute-done | bytes 262176 | tf_op jit(solution)/shard_map/ppermute | solution.py:49
  92.7 5.4 %collective-permute-start.7 = (bf16[512,256]{1,0:T(8,128)(2,1)S(1)}, bf16[512,256]{1,0:T(8,128)(2,1)S(1)}, u32[]{:S(2)}, u32[]{:S(2)}) collective-permute-start(bf16[512,256]{1,0:T(8,128)(2,1)S(1)} %collective-permute-done.5.refs_2_), channel_id=1, source_target_pairs={{0,128},{128,256},{256,384},{384,448},{448,320},{320,192},{192,64}... | collective-permute-start | bytes 786440 | tf_op jit(solution)/shard_map/ppermute | solution.py:49
  98.1 1.9 %collective-permute-start.9 = (bf16[512,256]{1,0:T(8,128)(2,1)S(1)}, bf16[512,256]{1,0:T(8,128)(2,1)S(1)}, u32[]{:S(2)}, u32[]{:S(2)}) collective-permute-start(bf16[512,256]{1,0:T(8,128)(2,1)S(1)} %collective-permute-done.6.refs_6_), channel_id=1, source_target_pairs={{0,64},{128,0},{256,128},{384,256},{448,384},{320,448},{192,320},{... | collective-permute-start | bytes 786440 | tf_op jit(solution)/shard_map/ppermute | solution.py:49
  100.0 3.3 %collective-permute-done.7.refs_3_ = bf16[512,256]{1,0:T(8,128)(2,1)S(1)} collective-permute-done((bf16[512,256]{1,0:T(8,128)(2,1)S(1)}, bf16[512,256]{1,0:T(8,128)(2,1)S(1)}, u32[]{:S(2)}, u32[]{:S(2)}) %collective-permute-start.7) | collective-permute-done | bytes 262176 | tf_op jit(solution)/shard_map/ppermute | solution.py:49
  103.3 5.1 %collective-permute-start.8 = (bf16[512,256]{1,0:T(8,128)(2,1)S(1)}, bf16[512,256]{1,0:T(8,128)(2,1)S(1)}, u32[]{:S(2)}, u32[]{:S(2)}) collective-permute-start(bf16[512,256]{1,0:T(8,128)(2,1)S(1)} %collective-permute-done.7.refs_3_), channel_id=1, source_target_pairs={{0,128},{128,256},{256,384},{384,448},{448,320},{320,192},{192,64}... | collective-permute-start | bytes 786440 | tf_op jit(solution)/shard_map/ppermute | solution.py:49
  108.5 0.1 copy.17
  108.7 0.1 copy.18.refs_0_
  108.9 4.8 %collective-permute-done.8.refs_4_ = bf16[512,256]{1,0:T(8,128)(2,1)S(1)} collective-permute-done((bf16[512,256]{1,0:T(8,128)(2,1)S(1)}, bf16[512,256]{1,0:T(8,128)(2,1)S(1)}, u32[]{:S(2)}, u32[]{:S(2)}) %collective-permute-start.8) | collective-permute-done | bytes 262176 | tf_op jit(solution)/shard_map/ppermute | solution.py:49
  113.7 8.8 %shard_map.59 = (bf16[32,8,256]{2,1,0:T(8,128)(2,1)S(1)}, f32[256,896]{1,0:T(8,128)S(1)}, bf16[32,8,1152]{2,1,0:T(8,128)(2,1)}) custom-call(s32[8]{0:T(128)S(1)} %dynamic_slice.3.ring, bf16[16,15,16,896]{3,2,1,0:T(8,128)(2,1)} %bitcast.24.moved, bf16[256,7168]{1,0:T(8,128)(2,1)} %mine.1, bf16[256,7168]{1,0:T(8,128)(2,1)} %collective-permute-done.4.theirs, ...), custom_call_target="tpu_custom_call" | custom-call | flops 3758096384 | bytes 17825792 | tf_op jit(solution)/shard_map/pallas_call | solution.py:117
  122.6 4.4 %collective-permute-start.10 = (bf16[32,8,1152]{2,1,0:T(8,128)(2,1)}, bf16[32,8,1152]{2,1,0:T(8,128)(2,1)S(1)}, u32[]{:S(2)}, u32[]{:S(2)}) collective-permute-start(bf16[32,8,1152]{2,1,0:T(8,128)(2,1)} %get-tuple-element.25), channel_id=1, source_target_pairs={{0,1},{1,0},{2,3},{3,2},{4,5},{5,4},{6,7},{7,6},{8,9},{9,8},{10,11... | collective-permute-start | bytes 1769480 | tf_op jit(solution)/shard_map/ppermute | solution.py:53
  127.1 1.7 %collective-permute-done.10.far = bf16[32,8,1152]{2,1,0:T(8,128)(2,1)S(1)} collective-permute-done((bf16[32,8,1152]{2,1,0:T(8,128)(2,1)}, bf16[32,8,1152]{2,1,0:T(8,128)(2,1)S(1)}, u32[]{:S(2)}, u32[]{:S(2)}) %collective-permute-start.10) | collective-permute-done | bytes 589856 | tf_op jit(solution)/shard_map/ppermute | solution.py:53
  128.8 1.5 %shard_map.60 = (bf16[64,8,256]{2,1,0:T(8,128)(2,1)}, bf16[256,896]{1,0:T(8,128)(2,1)}) custom-call(s32[5]{0:T(128)S(1)} %stack.23.place, bf16[32,8,256]{2,1,0:T(8,128)(2,1)S(1)} %get-tuple-element.23.near_in, f32[256,896]{1,0:T(8,128)S(1)} %get-tuple-element.24.near_weight, bf16[32,8,1152]{2,1,0:T(8,128)(2,1)S(1)} %collective-permute-done.10.far), custom_call_target="tpu_custom_call" | custom-call | tf_op jit(solution)/shard_map/pallas_call | solution.py:157
  (21 shorter events, 0.8 us)
Async XLA Ops:
  0.6 27.1 %collective-permute-start.1 = (bf16[8,7168]{1,0:T(8,128)(2,1)}, bf16[8,7168]{1,0:T(8,128)(2,1)S(1)}, u32[]{:S(2)}, u32[]{:S(2)}) collective-permute-start(bf16[8,7168]{1,0:T(8,128)(2,1)} %param.5), channel_id=1, source_target_pairs={{0,2},{2,0},{1,3},{3,1},{4,6},{6,4},{5,7},{7,5},{8,10},{10,8},{9,1... | collective-permute-start | bytes 344072 | tf_op jit(solution)/shard_map/ppermute | solution.py:53
  18.5 25.3 %all-to-all-start = ((bf16[16,8,896]{2,1,0:T(8,128)(2,1)}), bf16[16,8,896]{2,1,0:T(8,128)(2,1)S(1)}, u32[]{:S(2)}, u32[]{:S(2)}) async-start(bf16[16,8,896]{2,1,0:T(8,128)(2,1)} %bitcast.19), calls=%async_computation | async-start | bytes 458752 | tf_op jit(solution)/shard_map/all_to_all | solution.py:189
  24.5 4.3 %collective-permute-start = (bf16[256,256]{1,0:T(8,128)(2,1)S(1)}, bf16[256,256]{1,0:T(8,128)(2,1)S(1)}, u32[]{:S(2)}, u32[]{:S(2)}) collective-permute-start(bf16[256,256]{1,0:T(8,128)(2,1)S(1)} %bitcast.59), channel_id=1, source_target_pairs={{0,1},{1,0},{2,3},{3,2},{4,5},{5,4},{6,7},{7,6},{8,9},{9,8},{10,11... | collective-permute-start | bytes 393224 | tf_op jit(solution)/shard_map/ppermute | solution.py:53
  28.8 15.1 %collective-permute-start.2 = (bf16[512,256]{1,0:T(8,128)(2,1)S(1)}, bf16[512,256]{1,0:T(8,128)(2,1)S(1)}, u32[]{:S(2)}, u32[]{:S(2)}) collective-permute-start(bf16[512,256]{1,0:T(8,128)(2,1)S(1)} %pad_maximum_fusion.1), channel_id=1, source_target_pairs={{0,128},{128,256},{256,384},{384,448},{448,320},{320,192},{192,64}... | collective-permute-start | bytes 786440 | tf_op jit(solution)/shard_map/ppermute | solution.py:49
  45.4 17.8 %all-to-all-start.1 = ((bf16[4,240,896]{2,1,0:T(8,128)(2,1)}), bf16[4,240,896]{2,1,0:T(8,128)(2,1)S(1)}, u32[]{:S(2)}, u32[]{:S(2)}) async-start(bf16[4,240,896]{2,1,0:T(8,128)(2,1)} %broadcast_in_dim.51), calls=%async_computation.1 | async-start | bytes 3440640 | tf_op jit(solution)/shard_map/all_to_all | solution.py:44
  49.6 9.6 %collective-permute-start.3 = (bf16[512,256]{1,0:T(8,128)(2,1)S(1)}, bf16[512,256]{1,0:T(8,128)(2,1)S(1)}, u32[]{:S(2)}, u32[]{:S(2)}) collective-permute-start(bf16[512,256]{1,0:T(8,128)(2,1)S(1)} %pad_maximum_fusion.1), channel_id=1, source_target_pairs={{0,64},{128,0},{256,128},{384,256},{448,384},{320,448},{192,320},{... | collective-permute-start | bytes 786440 | tf_op jit(solution)/shard_map/ppermute | solution.py:49
  66.6 41.8 %copy-start = (s32[64]{0:T(128)S(1)}, s32[64]{0:T(128)}, u32[]{:S(2)}) copy-start(s32[64]{0:T(128)} %constant.29.clone) | copy-start | bytes 772
  66.6 47.1 %all-to-all-start.2 = ((bf16[4,960,896]{2,1,0:T(8,128)(2,1)}), bf16[4,960,896]{2,1,0:T(8,128)(2,1)}, u32[]{:S(2)}, u32[]{:S(2)}) async-start(bf16[4,960,896]{2,1,0:T(8,128)(2,1)} %broadcast_in_dim.52), calls=%async_computation.2 | async-start | bytes 13762560 | tf_op jit(solution)/shard_map/all_to_all | solution.py:44
  72.1 41.6 %collective-permute-start.4 = (bf16[256,7168]{1,0:T(8,128)(2,1)}, bf16[256,7168]{1,0:T(8,128)(2,1)}, u32[]{:S(2)}, u32[]{:S(2)}) collective-permute-start(bf16[256,7168]{1,0:T(8,128)(2,1)} %mine.1), channel_id=1, source_target_pairs={{0,1},{1,0},{2,3},{3,2},{4,5},{5,4},{6,7},{7,6},{8,9},{9,8},{10,11... | collective-permute-start | bytes 11010056 | tf_op jit(solution)/shard_map/ppermute | solution.py:53
  75.9 10.0 %collective-permute-start.5 = (bf16[512,256]{1,0:T(8,128)(2,1)S(1)}, bf16[512,256]{1,0:T(8,128)(2,1)S(1)}, u32[]{:S(2)}, u32[]{:S(2)}) collective-permute-start(bf16[512,256]{1,0:T(8,128)(2,1)S(1)} %collective-permute-done.2.refs_1_), channel_id=1, source_target_pairs={{0,128},{128,256},{256,384},{384,448},{448,320},{320,192},{192,64}... | collective-permute-start | bytes 786440 | tf_op jit(solution)/shard_map/ppermute | solution.py:49
  79.0 13.7 %collective-permute-start.6 = (bf16[512,256]{1,0:T(8,128)(2,1)S(1)}, bf16[512,256]{1,0:T(8,128)(2,1)S(1)}, u32[]{:S(2)}, u32[]{:S(2)}) collective-permute-start(bf16[512,256]{1,0:T(8,128)(2,1)S(1)} %collective-permute-done.3.refs_7_), channel_id=1, source_target_pairs={{0,64},{128,0},{256,128},{384,256},{448,384},{320,448},{192,320},{... | collective-permute-start | bytes 786440 | tf_op jit(solution)/shard_map/ppermute | solution.py:49
  92.7 10.6 %collective-permute-start.7 = (bf16[512,256]{1,0:T(8,128)(2,1)S(1)}, bf16[512,256]{1,0:T(8,128)(2,1)S(1)}, u32[]{:S(2)}, u32[]{:S(2)}) collective-permute-start(bf16[512,256]{1,0:T(8,128)(2,1)S(1)} %collective-permute-done.5.refs_2_), channel_id=1, source_target_pairs={{0,128},{128,256},{256,384},{384,448},{448,320},{320,192},{192,64}... | collective-permute-start | bytes 786440 | tf_op jit(solution)/shard_map/ppermute | solution.py:49
  98.1 10.9 %collective-permute-start.9 = (bf16[512,256]{1,0:T(8,128)(2,1)S(1)}, bf16[512,256]{1,0:T(8,128)(2,1)S(1)}, u32[]{:S(2)}, u32[]{:S(2)}) collective-permute-start(bf16[512,256]{1,0:T(8,128)(2,1)S(1)} %collective-permute-done.6.refs_6_), channel_id=1, source_target_pairs={{0,64},{128,0},{256,128},{384,256},{448,384},{320,448},{192,320},{... | collective-permute-start | bytes 786440 | tf_op jit(solution)/shard_map/ppermute | solution.py:49
  103.3 10.4 %collective-permute-start.8 = (bf16[512,256]{1,0:T(8,128)(2,1)S(1)}, bf16[512,256]{1,0:T(8,128)(2,1)S(1)}, u32[]{:S(2)}, u32[]{:S(2)}) collective-permute-start(bf16[512,256]{1,0:T(8,128)(2,1)S(1)} %collective-permute-done.7.refs_3_), channel_id=1, source_target_pairs={{0,128},{128,256},{256,384},{384,448},{448,320},{320,192},{192,64}... | collective-permute-start | bytes 786440 | tf_op jit(solution)/shard_map/ppermute | solution.py:49
  122.6 6.2 %collective-permute-start.10 = (bf16[32,8,1152]{2,1,0:T(8,128)(2,1)}, bf16[32,8,1152]{2,1,0:T(8,128)(2,1)S(1)}, u32[]{:S(2)}, u32[]{:S(2)}) collective-permute-start(bf16[32,8,1152]{2,1,0:T(8,128)(2,1)} %get-tuple-element.25), channel_id=1, source_target_pairs={{0,1},{1,0},{2,3},{3,2},{4,5},{5,4},{6,7},{7,6},{8,9},{9,8},{10,11... | collective-permute-start | bytes 1769480 | tf_op jit(solution)/shard_map/ppermute | solution.py:53

commit v6 on v5

--- a/solution.py
+++ b/solution.py
@@ -38,9 +38,11 @@
     return groups
 
 
-def spread(values, first):
+def spread(values, first, before=None):
     n = values.shape[0]
     copies = jnp.broadcast_to(values[None], (NX,) + values.shape).reshape((NX * n,) + values.shape[1:])
+    if before is not None:
+        copies, _ = lax.optimization_barrier((copies, before))
     return lax.all_to_all(copies, TENSOR, 0, 0, axis_index_groups=lines(first), tiled=True)
 
 
@@ -195,8 +197,7 @@
     weight_other = swap(weight, "core")
     wide, both = lax.optimization_barrier((wide, both))
     ahead, back = [wide, turn(wide, 1)], [wide]
-    both, ahead[1] = lax.optimization_barrier((both, ahead[1]))
-    moved = spread(jnp.concatenate([both, others], 0), True)
+    moved = spread(jnp.concatenate([both, others], 0), True, ahead[1])
     back.append(turn(wide, -1))
     moved, back[1] = lax.optimization_barrier((moved, back[1]))
     moved = spread(moved, False).reshape(NX * NY, n_dp + LAST, deep, columns)

time: 131 us -> 131 us (level)
    ppermute x7, waiting for transfers between devices: 37.3 us -> 28.8 us  [turn(): return lax.ppermute(values, 'dp', pairs)]
    all_to_all x1, waiting for transfers between devices: 0.01 us -> 8.32 us  [body(): lax.all_to_all(strips, ('dp', 'zh'), 0, 0, tiled=True)]
  transfers between devices with their start and end apart: 14 -> 14, of which waited for: 9 -> 10; matrix products, arithmetic and copies ran while one was open for 3% -> 4% of each run, Pallas kernels for 0% -> 0%
where the time goes in v6:
time: 131 us; the launch traced here: 130 us
  starting transfers between devices  66.6 us (51%)
  waiting for transfers between devices  42.9 us (33%)
  Pallas kernels  10.4 us (8%)
  local copies, waits for them, and re-layouts  7.24 us (6%)
  other arithmetic  2.15 us (2%)
    ppermute x7, waiting for transfers between devices, turn(): return lax.ppermute(values, 'dp', pairs)  28.8 us
    ppermute x4, starting transfers between devices, swap(): return lax.ppermute(values, axis, [(0, 1), (1, 0)])  27.6 us
    ppermute x7, starting transfers between devices, turn(): return lax.ppermute(values, 'dp', pairs)  24.5 us
    all_to_all x2, starting transfers between devices, spread(): lax.all_to_all(copies, TENSOR, 0, 0, axis_index_groups=lines(first), tile...  9.69 us
    pallas_call x1, Pallas kernels, products(): pl.pallas_call(products_kernel, out_shape=(jax.ShapeDtypeStruct((blocks,...  8.84 us
    all_to_all x1, waiting for transfers between devices, body(): lax.all_to_all(strips, ('dp', 'zh'), 0, 0, tiled=True)  8.32 us
    all_to_all x1, starting transfers between devices, body(): lax.all_to_all(strips, ('dp', 'zh'), 0, 0, tiled=True)  4.85 us
    broadcast_in_dim x2, local copies, waits for them, and re-layouts, spread(): jnp.broadcast_to(values[None], (NX,) + values.shape)  4.77 us
  transfers between devices with their start and end apart: 14, of which 10 were waited for; matrix products, arithmetic and copies ran while one was open for 4% of the time, Pallas kernels for 0%

profile of v6, /device:TPU:1, one launch (start us, length us, event | category | flops | bytes accessed | tf_op | source)
XLA Modules:
  0.0 130.1 jit_solution(15094231822848313045)
XLA Ops:
  0.6 16.3 %collective-permute-start.1 = (bf16[8,7168]{1,0:T(8,128)(2,1)}, bf16[8,7168]{1,0:T(8,128)(2,1)S(1)}, u32[]{:S(2)}, u32[]{:S(2)}) collective-permute-start(bf16[8,7168]{1,0:T(8,128)(2,1)} %param.5), channel_id=1, source_target_pairs={{0,2},{2,0},{1,3},{3,1},{4,6},{6,4},{5,7},{7,5},{8,10},{10,8},{9,1... | collective-permute-start | bytes 344072 | tf_op jit(solution)/shard_map/ppermute | solution.py:55
  16.9 1.6 %broadcast_in_dim.47 = bf16[8,2,8,896]{3,2,1,0:T(8,128)(2,1)} broadcast(bf16[8,8,896]{2,1,0:T(8,128)(2,1)} %bitcast.59), dimensions={0,2,3} | broadcast | bytes 344064 | tf_op jit(solution)/shard_map/broadcast_in_dim | solution.py:188
  18.5 4.8 %all-to-all-start = ((bf16[16,8,896]{2,1,0:T(8,128)(2,1)}), bf16[16,8,896]{2,1,0:T(8,128)(2,1)S(1)}, u32[]{:S(2)}, u32[]{:S(2)}) async-start(bf16[16,8,896]{2,1,0:T(8,128)(2,1)} %bitcast.19), calls=%async_computation | async-start | bytes 458752 | tf_op jit(solution)/shard_map/all_to_all | solution.py:191
  23.4 1.0 broadcast_select_fusion.1
  24.5 3.1 %collective-permute-start = (bf16[256,256]{1,0:T(8,128)(2,1)S(1)}, bf16[256,256]{1,0:T(8,128)(2,1)S(1)}, u32[]{:S(2)}, u32[]{:S(2)}) collective-permute-start(bf16[256,256]{1,0:T(8,128)(2,1)S(1)} %bitcast.61), channel_id=1, source_target_pairs={{0,1},{1,0},{2,3},{3,2},{4,5},{5,4},{6,7},{7,6},{8,9},{9,8},{10,11... | collective-permute-start | bytes 393224 | tf_op jit(solution)/shard_map/ppermute | solution.py:55
  28.0 0.9 pad_maximum_fusion.2
  29.0 4.4 %collective-permute-start.2 = (bf16[512,256]{1,0:T(8,128)(2,1)S(1)}, bf16[512,256]{1,0:T(8,128)(2,1)S(1)}, u32[]{:S(2)}, u32[]{:S(2)}) collective-permute-start(bf16[512,256]{1,0:T(8,128)(2,1)S(1)} %pad_maximum_fusion.1), channel_id=1, source_target_pairs={{0,128},{128,256},{256,384},{384,448},{448,320},{320,192},{192,64}... | collective-permute-start | bytes 786440 | tf_op jit(solution)/shard_map/ppermute | solution.py:51
  33.4 8.3 %all-to-all-done = bf16[16,8,896]{2,1,0:T(8,128)(2,1)S(1)} async-done(((bf16[16,8,896]{2,1,0:T(8,128)(2,1)}), bf16[16,8,896]{2,1,0:T(8,128)(2,1)S(1)}, u32[]{:S(2)}, u32[]{:S(2)}) %all-to-all-start) | async-done | bytes 229408 | tf_op jit(solution)/shard_map/all_to_all | solution.py:191
  41.9 1.9 %collective-permute-done.2.refs_1_ = bf16[512,256]{1,0:T(8,128)(2,1)S(1)} collective-permute-done((bf16[512,256]{1,0:T(8,128)(2,1)S(1)}, bf16[512,256]{1,0:T(8,128)(2,1)S(1)}, u32[]{:S(2)}, u32[]{:S(2)}) %collective-permute-start.2) | collective-permute-done | bytes 262176 | tf_op jit(solution)/shard_map/ppermute | solution.py:51
  43.9 1.4 %broadcast_in_dim.51 = bf16[4,240,896]{2,1,0:T(8,128)(2,1)} broadcast(bf16[240,896]{1,0:T(8,128)(2,1)S(1)} %pad_maximum_fusion), dimensions={1,2} | broadcast | bytes 2150400 | tf_op jit(solution)/shard_map/broadcast_in_dim | solution.py:43
  45.2 4.2 %all-to-all-start.1 = ((bf16[4,240,896]{2,1,0:T(8,128)(2,1)}), bf16[4,240,896]{2,1,0:T(8,128)(2,1)S(1)}, u32[]{:S(2)}, u32[]{:S(2)}) async-start(bf16[4,240,896]{2,1,0:T(8,128)(2,1)} %broadcast_in_dim.51), calls=%async_computation.1 | async-start | bytes 3440640 | tf_op jit(solution)/shard_map/all_to_all | solution.py:46
  49.4 2.4 %collective-permute-start.3 = (bf16[512,256]{1,0:T(8,128)(2,1)S(1)}, bf16[512,256]{1,0:T(8,128)(2,1)S(1)}, u32[]{:S(2)}, u32[]{:S(2)}) collective-permute-start(bf16[512,256]{1,0:T(8,128)(2,1)S(1)} %pad_maximum_fusion.1), channel_id=1, source_target_pairs={{0,64},{128,0},{256,128},{384,256},{448,384},{320,448},{192,320},{... | collective-permute-start | bytes 786440 | tf_op jit(solution)/shard_map/ppermute | solution.py:51
  51.8 7.2 %collective-permute-done.3.refs_7_ = bf16[512,256]{1,0:T(8,128)(2,1)S(1)} collective-permute-done((bf16[512,256]{1,0:T(8,128)(2,1)S(1)}, bf16[512,256]{1,0:T(8,128)(2,1)S(1)}, u32[]{:S(2)}, u32[]{:S(2)}) %collective-permute-start.3) | collective-permute-done | bytes 262176 | tf_op jit(solution)/shard_map/ppermute | solution.py:51
  59.0 4.1 %all-to-all-done.1 = bf16[4,240,896]{2,1,0:T(8,128)(2,1)S(1)} async-done(((bf16[4,240,896]{2,1,0:T(8,128)(2,1)}), bf16[4,240,896]{2,1,0:T(8,128)(2,1)S(1)}, u32[]{:S(2)}, u32[]{:S(2)}) %all-to-all-start.1) | async-done | bytes 1720352 | tf_op jit(solution)/shard_map/all_to_all | solution.py:46
  63.0 3.4 %broadcast_in_dim.52 = bf16[4,960,896]{2,1,0:T(8,128)(2,1)} broadcast(bf16[960,896]{1,0:T(8,128)(2,1)S(1)} %bitcast.50), dimensions={1,2} | broadcast | bytes 8601600 | tf_op jit(solution)/shard_map/broadcast_in_dim | solution.py:43
  66.5 5.5 %all-to-all-start.2 = ((bf16[4,960,896]{2,1,0:T(8,128)(2,1)}), bf16[4,960,896]{2,1,0:T(8,128)(2,1)}, u32[]{:S(2)}, u32[]{:S(2)}) async-start(bf16[4,960,896]{2,1,0:T(8,128)(2,1)} %broadcast_in_dim.52), calls=%async_computation.2 | async-start | bytes 13762560 | tf_op jit(solution)/shard_map/all_to_all | solution.py:46
  72.0 3.8 %collective-permute-start.4 = (bf16[256,7168]{1,0:T(8,128)(2,1)}, bf16[256,7168]{1,0:T(8,128)(2,1)}, u32[]{:S(2)}, u32[]{:S(2)}) collective-permute-start(bf16[256,7168]{1,0:T(8,128)(2,1)} %mine.1), channel_id=1, source_target_pairs={{0,1},{1,0},{2,3},{3,2},{4,5},{5,4},{6,7},{7,6},{8,9},{9,8},{10,11... | collective-permute-start | bytes 11010056 | tf_op jit(solution)/shard_map/ppermute | solution.py:55
  75.8 3.2 %collective-permute-start.5 = (bf16[512,256]{1,0:T(8,128)(2,1)S(1)}, bf16[512,256]{1,0:T(8,128)(2,1)S(1)}, u32[]{:S(2)}, u32[]{:S(2)}) collective-permute-start(bf16[512,256]{1,0:T(8,128)(2,1)S(1)} %collective-permute-done.2.refs_1_), channel_id=1, source_target_pairs={{0,128},{128,256},{256,384},{384,448},{448,320},{320,192},{192,64}... | collective-permute-start | bytes 786440 | tf_op jit(solution)/shard_map/ppermute | solution.py:51
  79.0 2.1 %collective-permute-start.6 = (bf16[512,256]{1,0:T(8,128)(2,1)S(1)}, bf16[512,256]{1,0:T(8,128)(2,1)S(1)}, u32[]{:S(2)}, u32[]{:S(2)}) collective-permute-start(bf16[512,256]{1,0:T(8,128)(2,1)S(1)} %collective-permute-done.3.refs_7_), channel_id=1, source_target_pairs={{0,64},{128,0},{256,128},{384,256},{448,384},{320,448},{192,320},{... | collective-permute-start | bytes 786440 | tf_op jit(solution)/shard_map/ppermute | solution.py:51
  81.1 4.7 %collective-permute-done.5.refs_2_ = bf16[512,256]{1,0:T(8,128)(2,1)S(1)} collective-permute-done((bf16[512,256]{1,0:T(8,128)(2,1)S(1)}, bf16[512,256]{1,0:T(8,128)(2,1)S(1)}, u32[]{:S(2)}, u32[]{:S(2)}) %collective-permute-start.5) | collective-permute-done | bytes 262176 | tf_op jit(solution)/shard_map/ppermute | solution.py:51
  85.8 6.8 %collective-permute-done.6.refs_6_ = bf16[512,256]{1,0:T(8,128)(2,1)S(1)} collective-permute-done((bf16[512,256]{1,0:T(8,128)(2,1)S(1)}, bf16[512,256]{1,0:T(8,128)(2,1)S(1)}, u32[]{:S(2)}, u32[]{:S(2)}) %collective-permute-start.6) | collective-permute-done | bytes 262176 | tf_op jit(solution)/shard_map/ppermute | solution.py:51
  92.5 5.4 %collective-permute-start.7 = (bf16[512,256]{1,0:T(8,128)(2,1)S(1)}, bf16[512,256]{1,0:T(8,128)(2,1)S(1)}, u32[]{:S(2)}, u32[]{:S(2)}) collective-permute-start(bf16[512,256]{1,0:T(8,128)(2,1)S(1)} %collective-permute-done.5.refs_2_), channel_id=1, source_target_pairs={{0,128},{128,256},{256,384},{384,448},{448,320},{320,192},{192,64}... | collective-permute-start | bytes 786440 | tf_op jit(solution)/shard_map/ppermute | solution.py:51
  97.9 1.9 %collective-permute-start.9 = (bf16[512,256]{1,0:T(8,128)(2,1)S(1)}, bf16[512,256]{1,0:T(8,128)(2,1)S(1)}, u32[]{:S(2)}, u32[]{:S(2)}) collective-permute-start(bf16[512,256]{1,0:T(8,128)(2,1)S(1)} %collective-permute-done.6.refs_6_), channel_id=1, source_target_pairs={{0,64},{128,0},{256,128},{384,256},{448,384},{320,448},{192,320},{... | collective-permute-start | bytes 786440 | tf_op jit(solution)/shard_map/ppermute | solution.py:51
  99.8 3.3 %collective-permute-done.7.refs_3_ = bf16[512,256]{1,0:T(8,128)(2,1)S(1)} collective-permute-done((bf16[512,256]{1,0:T(8,128)(2,1)S(1)}, bf16[512,256]{1,0:T(8,128)(2,1)S(1)}, u32[]{:S(2)}, u32[]{:S(2)}) %collective-permute-start.7) | collective-permute-done | bytes 262176 | tf_op jit(solution)/shard_map/ppermute | solution.py:51
  103.1 5.1 %collective-permute-start.8 = (bf16[512,256]{1,0:T(8,128)(2,1)S(1)}, bf16[512,256]{1,0:T(8,128)(2,1)S(1)}, u32[]{:S(2)}, u32[]{:S(2)}) collective-permute-start(bf16[512,256]{1,0:T(8,128)(2,1)S(1)} %collective-permute-done.7.refs_3_), channel_id=1, source_target_pairs={{0,128},{128,256},{256,384},{384,448},{448,320},{320,192},{192,64}... | collective-permute-start | bytes 786440 | tf_op jit(solution)/shard_map/ppermute | solution.py:51
  108.3 0.1 copy.17
  108.5 0.1 copy.18.refs_0_
  108.7 4.8 %collective-permute-done.8.refs_4_ = bf16[512,256]{1,0:T(8,128)(2,1)S(1)} collective-permute-done((bf16[512,256]{1,0:T(8,128)(2,1)S(1)}, bf16[512,256]{1,0:T(8,128)(2,1)S(1)}, u32[]{:S(2)}, u32[]{:S(2)}) %collective-permute-start.8) | collective-permute-done | bytes 262176 | tf_op jit(solution)/shard_map/ppermute | solution.py:51
  113.6 8.8 %shard_map.59 = (bf16[32,8,256]{2,1,0:T(8,128)(2,1)S(1)}, f32[256,896]{1,0:T(8,128)S(1)}, bf16[32,8,1152]{2,1,0:T(8,128)(2,1)}) custom-call(s32[8]{0:T(128)S(1)} %dynamic_slice.3.ring, bf16[16,15,16,896]{3,2,1,0:T(8,128)(2,1)} %bitcast.26.moved, bf16[256,7168]{1,0:T(8,128)(2,1)} %mine.1, bf16[256,7168]{1,0:T(8,128)(2,1)} %collective-permute-done.4.theirs, ...), custom_call_target="tpu_custom_call" | custom-call | flops 3758096384 | bytes 17825792 | tf_op jit(solution)/shard_map/pallas_call | solution.py:119
  122.4 4.4 %collective-permute-start.10 = (bf16[32,8,1152]{2,1,0:T(8,128)(2,1)}, bf16[32,8,1152]{2,1,0:T(8,128)(2,1)S(1)}, u32[]{:S(2)}, u32[]{:S(2)}) collective-permute-start(bf16[32,8,1152]{2,1,0:T(8,128)(2,1)} %get-tuple-element.23), channel_id=1, source_target_pairs={{0,1},{1,0},{2,3},{3,2},{4,5},{5,4},{6,7},{7,6},{8,9},{9,8},{10,11... | collective-permute-start | bytes 1769480 | tf_op jit(solution)/shard_map/ppermute | solution.py:55
  126.9 1.7 %collective-permute-done.10.far = bf16[32,8,1152]{2,1,0:T(8,128)(2,1)S(1)} collective-permute-done((bf16[32,8,1152]{2,1,0:T(8,128)(2,1)}, bf16[32,8,1152]{2,1,0:T(8,128)(2,1)S(1)}, u32[]{:S(2)}, u32[]{:S(2)}) %collective-permute-start.10) | collective-permute-done | bytes 589856 | tf_op jit(solution)/shard_map/ppermute | solution.py:55
  128.6 1.5 %shard_map.60 = (bf16[64,8,256]{2,1,0:T(8,128)(2,1)}, bf16[256,896]{1,0:T(8,128)(2,1)}) custom-call(s32[5]{0:T(128)S(1)} %stack.23.place, bf16[32,8,256]{2,1,0:T(8,128)(2,1)S(1)} %get-tuple-element.21.near_in, f32[256,896]{1,0:T(8,128)S(1)} %get-tuple-element.22.near_weight, bf16[32,8,1152]{2,1,0:T(8,128)(2,1)S(1)} %collective-permute-done.10.far), custom_call_target="tpu_custom_call" | custom-call | tf_op jit(solution)/shard_map/pallas_call | solution.py:159
  (21 shorter events, 0.9 us)
Async XLA Ops:
  0.6 27.3 %collective-permute-start.1 = (bf16[8,7168]{1,0:T(8,128)(2,1)}, bf16[8,7168]{1,0:T(8,128)(2,1)S(1)}, u32[]{:S(2)}, u32[]{:S(2)}) collective-permute-start(bf16[8,7168]{1,0:T(8,128)(2,1)} %param.5), channel_id=1, source_target_pairs={{0,2},{2,0},{1,3},{3,1},{4,6},{6,4},{5,7},{7,5},{8,10},{10,8},{9,1... | collective-permute-start | bytes 344072 | tf_op jit(solution)/shard_map/ppermute | solution.py:55
  18.5 23.2 %all-to-all-start = ((bf16[16,8,896]{2,1,0:T(8,128)(2,1)}), bf16[16,8,896]{2,1,0:T(8,128)(2,1)S(1)}, u32[]{:S(2)}, u32[]{:S(2)}) async-start(bf16[16,8,896]{2,1,0:T(8,128)(2,1)} %bitcast.19), calls=%async_computation | async-start | bytes 458752 | tf_op jit(solution)/shard_map/all_to_all | solution.py:191
  24.5 4.4 %collective-permute-start = (bf16[256,256]{1,0:T(8,128)(2,1)S(1)}, bf16[256,256]{1,0:T(8,128)(2,1)S(1)}, u32[]{:S(2)}, u32[]{:S(2)}) collective-permute-start(bf16[256,256]{1,0:T(8,128)(2,1)S(1)} %bitcast.61), channel_id=1, source_target_pairs={{0,1},{1,0},{2,3},{3,2},{4,5},{5,4},{6,7},{7,6},{8,9},{9,8},{10,11... | collective-permute-start | bytes 393224 | tf_op jit(solution)/shard_map/ppermute | solution.py:55
  29.0 14.9 %collective-permute-start.2 = (bf16[512,256]{1,0:T(8,128)(2,1)S(1)}, bf16[512,256]{1,0:T(8,128)(2,1)S(1)}, u32[]{:S(2)}, u32[]{:S(2)}) collective-permute-start(bf16[512,256]{1,0:T(8,128)(2,1)S(1)} %pad_maximum_fusion.1), channel_id=1, source_target_pairs={{0,128},{128,256},{256,384},{384,448},{448,320},{320,192},{192,64}... | collective-permute-start | bytes 786440 | tf_op jit(solution)/shard_map/ppermute | solution.py:51
  45.2 17.8 %all-to-all-start.1 = ((bf16[4,240,896]{2,1,0:T(8,128)(2,1)}), bf16[4,240,896]{2,1,0:T(8,128)(2,1)S(1)}, u32[]{:S(2)}, u32[]{:S(2)}) async-start(bf16[4,240,896]{2,1,0:T(8,128)(2,1)} %broadcast_in_dim.51), calls=%async_computation.1 | async-start | bytes 3440640 | tf_op jit(solution)/shard_map/all_to_all | solution.py:46
  49.4 9.6 %collective-permute-start.3 = (bf16[512,256]{1,0:T(8,128)(2,1)S(1)}, bf16[512,256]{1,0:T(8,128)(2,1)S(1)}, u32[]{:S(2)}, u32[]{:S(2)}) collective-permute-start(bf16[512,256]{1,0:T(8,128)(2,1)S(1)} %pad_maximum_fusion.1), channel_id=1, source_target_pairs={{0,64},{128,0},{256,128},{384,256},{448,384},{320,448},{192,320},{... | collective-permute-start | bytes 786440 | tf_op jit(solution)/shard_map/ppermute | solution.py:51
  66.5 41.8 %copy-start = (s32[64]{0:T(128)S(1)}, s32[64]{0:T(128)}, u32[]{:S(2)}) copy-start(s32[64]{0:T(128)} %constant.29.clone) | copy-start | bytes 772
  66.5 47.1 %all-to-all-start.2 = ((bf16[4,960,896]{2,1,0:T(8,128)(2,1)}), bf16[4,960,896]{2,1,0:T(8,128)(2,1)}, u32[]{:S(2)}, u32[]{:S(2)}) async-start(bf16[4,960,896]{2,1,0:T(8,128)(2,1)} %broadcast_in_dim.52), calls=%async_computation.2 | async-start | bytes 13762560 | tf_op jit(solution)/shard_map/all_to_all | solution.py:46
  72.0 41.6 %collective-permute-start.4 = (bf16[256,7168]{1,0:T(8,128)(2,1)}, bf16[256,7168]{1,0:T(8,128)(2,1)}, u32[]{:S(2)}, u32[]{:S(2)}) collective-permute-start(bf16[256,7168]{1,0:T(8,128)(2,1)} %mine.1), channel_id=1, source_target_pairs={{0,1},{1,0},{2,3},{3,2},{4,5},{5,4},{6,7},{7,6},{8,9},{9,8},{10,11... | collective-permute-start | bytes 11010056 | tf_op jit(solution)/shard_map/ppermute | solution.py:55
  75.8 10.0 %collective-permute-start.5 = (bf16[512,256]{1,0:T(8,128)(2,1)S(1)}, bf16[512,256]{1,0:T(8,128)(2,1)S(1)}, u32[]{:S(2)}, u32[]{:S(2)}) collective-permute-start(bf16[512,256]{1,0:T(8,128)(2,1)S(1)} %collective-permute-done.2.refs_1_), channel_id=1, source_target_pairs={{0,128},{128,256},{256,384},{384,448},{448,320},{320,192},{192,64}... | collective-permute-start | bytes 786440 | tf_op jit(solution)/shard_map/ppermute | solution.py:51
  79.0 13.5 %collective-permute-start.6 = (bf16[512,256]{1,0:T(8,128)(2,1)S(1)}, bf16[512,256]{1,0:T(8,128)(2,1)S(1)}, u32[]{:S(2)}, u32[]{:S(2)}) collective-permute-start(bf16[512,256]{1,0:T(8,128)(2,1)S(1)} %collective-permute-done.3.refs_7_), channel_id=1, source_target_pairs={{0,64},{128,0},{256,128},{384,256},{448,384},{320,448},{192,320},{... | collective-permute-start | bytes 786440 | tf_op jit(solution)/shard_map/ppermute | solution.py:51
  92.5 10.6 %collective-permute-start.7 = (bf16[512,256]{1,0:T(8,128)(2,1)S(1)}, bf16[512,256]{1,0:T(8,128)(2,1)S(1)}, u32[]{:S(2)}, u32[]{:S(2)}) collective-permute-start(bf16[512,256]{1,0:T(8,128)(2,1)S(1)} %collective-permute-done.5.refs_2_), channel_id=1, source_target_pairs={{0,128},{128,256},{256,384},{384,448},{448,320},{320,192},{192,64}... | collective-permute-start | bytes 786440 | tf_op jit(solution)/shard_map/ppermute | solution.py:51
  97.9 10.8 %collective-permute-start.9 = (bf16[512,256]{1,0:T(8,128)(2,1)S(1)}, bf16[512,256]{1,0:T(8,128)(2,1)S(1)}, u32[]{:S(2)}, u32[]{:S(2)}) collective-permute-start(bf16[512,256]{1,0:T(8,128)(2,1)S(1)} %collective-permute-done.6.refs_6_), channel_id=1, source_target_pairs={{0,64},{128,0},{256,128},{384,256},{448,384},{320,448},{192,320},{... | collective-permute-start | bytes 786440 | tf_op jit(solution)/shard_map/ppermute | solution.py:51
  103.1 10.4 %collective-permute-start.8 = (bf16[512,256]{1,0:T(8,128)(2,1)S(1)}, bf16[512,256]{1,0:T(8,128)(2,1)S(1)}, u32[]{:S(2)}, u32[]{:S(2)}) collective-permute-start(bf16[512,256]{1,0:T(8,128)(2,1)S(1)} %collective-permute-done.7.refs_3_), channel_id=1, source_target_pairs={{0,128},{128,256},{256,384},{384,448},{448,320},{320,192},{192,64}... | collective-permute-start | bytes 786440 | tf_op jit(solution)/shard_map/ppermute | solution.py:51
  122.4 6.2 %collective-permute-start.10 = (bf16[32,8,1152]{2,1,0:T(8,128)(2,1)}, bf16[32,8,1152]{2,1,0:T(8,128)(2,1)S(1)}, u32[]{:S(2)}, u32[]{:S(2)}) collective-permute-start(bf16[32,8,1152]{2,1,0:T(8,128)(2,1)} %get-tuple-element.23), channel_id=1, source_target_pairs={{0,1},{1,0},{2,3},{3,2},{4,5},{5,4},{6,7},{7,6},{8,9},{9,8},{10,11... | collective-permute-start | bytes 1769480 | tf_op jit(solution)/shard_map/ppermute | solution.py:55
